TPU v7x, 32 devices: a whole 2x2x4 slice. The times are simulated.
32 devices in a mesh: blk: 8 (over z, y), rep: 4 (over x, core).
Axes of the slice: x: 2, y: 2, z: 4, core: 2. Of those that a mesh axis runs over, the one named last changes fastest.
Arguments:
- patches: bfloat16 [4, 4096, 768], P('rep', 'blk'), may hold values from -6 to 6
- queries: bfloat16 [4, 800, 768], P('rep'), may hold values from -6 to 6
- window_valid: int32 [4, 64], P('rep', 'blk'), may hold values from 0 to 1, as said below
- answer_length: int32 [4], P('rep'), may hold values from 200 to 800
- norm_gain: float32 [6, 768], replicated, may hold values from 0.5 to 1.5
- norm_bias: float32 [6, 768], replicated, may hold values from -1.5 to 1.5
- attn_in: bfloat16 [4, 768, 2304], replicated, may hold values from -0.21875 to 0.21875
- attn_out: bfloat16 [4, 768, 768], replicated, may hold values from -0.625 to 0.625
- mlp_in: bfloat16 [2, 768, 3072], replicated, may hold values from -0.21875 to 0.21875
- mlp_out: bfloat16 [2, 3072, 768], replicated, may hold values from -0.109375 to 0.109375
- cot_patches: bfloat16 [4, 4096, 768], P('rep', 'blk'), may hold values from -6 to 6
- cot_queries: bfloat16 [4, 800, 768], P('rep'), may hold values from -6 to 6
Outputs:
- out_patches: bfloat16 [4, 4096, 768], P('rep', 'blk')
- out_queries: bfloat16 [4, 800, 768], P('rep', None, 'blk')
- grad_patches: float32 [4, 4096, 768], P('rep', 'blk')
- grad_queries: float32 [4, 800, 768], P('rep', None, 'blk')
- grad_norm_gain: float32 [6, 768], P(None, 'blk')
- grad_norm_bias: float32 [6, 768], P(None, 'blk')
- grad_attn_in: float32 [4, 768, 2304], P(None, 'blk')
- grad_attn_out: float32 [4, 768, 768], P(None, 'blk')
- grad_mlp_in: float32 [2, 768, 3072], P(None, 'blk')
- grad_mlp_out: float32 [2, 3072, 768], P(None, 'blk')
Inputs may be any that keep to these rules, and one draw needn't show every extreme that they name: `window_valid`: in every aligned block of 8 windows at least one window is valid.
All inputs are finite; a program needn't handle non-finite values.
Results may differ from a plain program's by a relative error of at most 0.015.
Values may be sent and summed in bfloat16 or wider, within the bound.
A program may use at most 576 MiB of HBM per device.

v0:
```python
import math

import jax
import jax.numpy as jnp
from jax import lax
from jax.sharding import PartitionSpec as P

HEADS = 12
WIN = 64


EPSILON = 1e-05
MASKED = -1e30
NARROW = jnp.bfloat16
SINGLE = jnp.float32


def merged(x, axis, combine):
    everything = jax.tree.map(
        lambda part, kind: lax.all_gather(part.astype(kind), axis),
        x,
        jax.tree.map(lambda a: jnp.bfloat16 if a.dtype == jnp.float32 else a.dtype, x),
    )

    def take(k):
        return jax.tree.map(lambda part, own: part[k].astype(own.dtype), everything, x)

    return lax.fori_loop(
        1, lax.axis_size(axis), lambda k, so_far: combine(so_far, take(k)), take(0)
    )


def layer_norm(tensor, scales, shifts):
    average = jnp.mean(tensor, axis=-1, keepdims=True)
    centred = tensor - average
    spread = jnp.mean(centred * centred, axis=-1, keepdims=True)
    return centred * lax.rsqrt(spread + EPSILON) * scales + shifts


def norm_back(tensor, scales, shifts, upstream):
    unused, pullback = jax.vjp(layer_norm, tensor, scales, shifts)
    return pullback(upstream)


def gelu_exact(tensor):
    return jax.nn.gelu(tensor, approximate=False)


def matmul(former, latter):
    return jnp.dot(former, latter, preferred_element_type=SINGLE)


def weight_grad(inputs, upstream):
    return lax.dot_general(
        inputs, upstream, (((0,), (0,)), ((), ())), preferred_element_type=SINGLE
    )


def input_grad(upstream, weight):
    return lax.dot_general(
        upstream, weight, (((1,), (1,)), ((), ())), preferred_element_type=SINGLE
    )


def split_heads(tensor, head_count):
    return tensor.reshape(tensor.shape[:-1] + (head_count, tensor.shape[-1] // head_count))


def masked_scores(queries_h, keys_h, allowed, scaling):
    products = (
        jnp.einsum("brhe,bkhe->bhrk", queries_h, keys_h, preferred_element_type=SINGLE) * scaling
    )
    return jnp.where(allowed, products, MASKED)


def attend_forward(queries_h, keys_h, values_h, allowed, scaling):
    scores = masked_scores(queries_h, keys_h, allowed, scaling)
    probabilities = jax.nn.softmax(scores, axis=-1)
    attended = jnp.einsum(
        "bhrk,bkhe->brhe", probabilities.astype(NARROW), values_h, preferred_element_type=SINGLE
    )
    return (attended, jax.nn.logsumexp(scores, axis=-1))


def attend_backward(queries_h, keys_h, values_h, allowed, scaling, logsum, upstream):
    probabilities = jnp.exp(masked_scores(queries_h, keys_h, allowed, scaling) - logsum[..., None])
    grad_probs = jnp.einsum("brhe,bkhe->bhrk", upstream, values_h, preferred_element_type=SINGLE)
    grad_scores = probabilities * (
        grad_probs - jnp.sum(grad_probs * probabilities, axis=-1, keepdims=True)
    )
    rounded = grad_scores.astype(NARROW)
    grad_queries = (
        jnp.einsum("bhrk,bkhe->brhe", rounded, keys_h, preferred_element_type=SINGLE) * scaling
    )
    grad_keys = (
        jnp.einsum("bhrk,brhe->bkhe", rounded, queries_h, preferred_element_type=SINGLE) * scaling
    )
    grad_values = jnp.einsum(
        "bhrk,brhe->bkhe", probabilities.astype(NARROW), upstream, preferred_element_type=SINGLE
    )
    return (grad_queries, grad_keys, grad_values)


def branch_forward(normed, w_in, w_out, head_count, groups, allowed, scaling):
    row_count, features = normed.shape
    project = matmul(normed, w_in).astype(NARROW)
    columns = project.reshape(groups, row_count // groups, 3, head_count, features // head_count)
    attended, logsum = attend_forward(
        columns[:, :, 0], columns[:, :, 1], columns[:, :, 2], allowed, scaling
    )
    attended = attended.reshape(row_count, features).astype(NARROW)
    return (matmul(attended, w_out), (project, attended, logsum))


def branch_backward(normed, w_in, w_out, head_count, groups, allowed, scaling, stored, upstream):
    project, attended, logsum = stored
    row_count, features = normed.shape
    grad_out_weight = weight_grad(attended, upstream)
    grad_attended = (
        input_grad(upstream, w_out)
        .astype(NARROW)
        .reshape(groups, row_count // groups, head_count, features // head_count)
    )
    columns = project.reshape(groups, row_count // groups, 3, head_count, features // head_count)
    grads = attend_backward(
        columns[:, :, 0],
        columns[:, :, 1],
        columns[:, :, 2],
        allowed,
        scaling,
        logsum,
        grad_attended,
    )
    grad_project = jnp.stack(grads, axis=2).reshape(row_count, 3 * features).astype(NARROW)
    return (input_grad(grad_project, w_in), weight_grad(normed, grad_project), grad_out_weight)


def mlp_forward(normed, w_up, w_down):
    preact = matmul(normed, w_up)
    hidden = gelu_exact(preact).astype(NARROW)
    return (matmul(hidden, w_down), (preact, hidden))


def mlp_backward(normed, w_up, w_down, stored, upstream):
    preact, hidden = stored
    grad_down = weight_grad(hidden, upstream)
    unused, pullback = jax.vjp(gelu_exact, preact)
    grad_preact = pullback(input_grad(upstream, w_down))[0].astype(NARROW)
    return (input_grad(grad_preact, w_up), weight_grad(normed, grad_preact), grad_down)


def combine(former, latter):
    peak = jnp.maximum(former[0], latter[0])
    first_factor = jnp.exp(former[0] - peak)
    second_factor = jnp.exp(latter[0] - peak)
    return (
        peak,
        former[1] * first_factor + latter[1] * second_factor,
        former[2] * first_factor[..., None] + latter[2] * second_factor[..., None],
    )


def block_stats(query_heads, key_rows, value_rows, flag_rows, scaling):
    head_count = query_heads.shape[1]
    scores = (
        jnp.einsum(
            "qhe,khe->hqk",
            query_heads,
            split_heads(key_rows, head_count),
            preferred_element_type=SINGLE,
        )
        * scaling
    )
    scores = jnp.where(flag_rows[None, None, :] > 0, scores, MASKED)
    peak = jnp.max(scores, axis=-1)
    weights = jnp.exp(scores - peak[..., None])
    accumulated = jnp.einsum(
        "hqk,khe->hqe",
        weights.astype(NARROW),
        split_heads(value_rows, head_count),
        preferred_element_type=SINGLE,
    )
    return (peak, jnp.sum(weights, axis=-1), accumulated)


def body(
    patches,
    queries,
    window_valid,
    answer_length,
    norm_gain,
    norm_bias,
    attn_in,
    attn_out,
    mlp_in,
    mlp_out,
    cot_patches,
    cot_queries,
):
    features = patches.shape[2]
    head_count = HEADS
    head_size = features // head_count
    scaling = 1.0 / math.sqrt(head_size)
    patch_rows = patches[0].astype(SINGLE)
    query_rows = queries[0].astype(SINGLE)
    patch_count = patch_rows.shape[0]
    query_count = query_rows.shape[0]
    length = answer_length[0]
    flag_rows = jnp.repeat(window_valid[0], WIN).astype(NARROW)
    positions = jnp.arange(query_count, dtype=jnp.int32)
    causal = (positions[None, :] <= positions[:, None])[None, None]
    reaching = (positions < length)[None, None, None, :]
    leader = (lax.axis_index("blk") == 0).astype(SINGLE)
    normed_zero = layer_norm(patch_rows, norm_gain[0], norm_bias[0]).astype(NARROW)
    window_out, window_kept = branch_forward(
        normed_zero, attn_in[0], attn_out[0], head_count, patch_count // WIN, True, scaling
    )
    patch_one = patch_rows + window_out
    normed_one = layer_norm(query_rows, norm_gain[1], norm_bias[1]).astype(NARROW)
    causal_out, causal_kept = branch_forward(
        normed_one, attn_in[1], attn_out[1], head_count, 1, causal, scaling
    )
    query_one = query_rows + causal_out
    normed_q = layer_norm(query_one, norm_gain[2], norm_bias[2]).astype(NARROW)
    normed_x = layer_norm(patch_one, norm_gain[3], norm_bias[3]).astype(NARROW)
    cross_weights = attn_in[2]
    query_heads = split_heads(
        matmul(normed_q, cross_weights[:, :features]).astype(NARROW), head_count
    )
    patch_kv = matmul(normed_x, cross_weights[:, features:]).astype(NARROW)
    key_local = patch_kv[:, :features]
    value_local = patch_kv[:, features:]
    peaks, totals, accumulated = merged(
        block_stats(query_heads, key_local, value_local, flag_rows, scaling), "blk", combine
    )
    cross_logsum = peaks + jnp.log(totals)
    cross_out = jnp.transpose(accumulated / totals[..., None], (1, 0, 2)).reshape(
        query_count, features
    )
    cross_mixed = cross_out.astype(NARROW)
    query_two = query_one + matmul(cross_mixed, attn_out[2])
    reverse_weights = attn_in[3]
    patch_query = split_heads(
        matmul(normed_x, reverse_weights[:, :features]).astype(NARROW), head_count
    )[None]
    query_kv = matmul(normed_q, reverse_weights[:, features:]).astype(NARROW)
    reverse_keys = split_heads(query_kv[:, :features], head_count)[None]
    reverse_values = split_heads(query_kv[:, features:], head_count)[None]
    reverse_mixed, reverse_logsum = attend_forward(
        patch_query, reverse_keys, reverse_values, reaching, scaling
    )
    reverse_mixed = reverse_mixed.reshape(patch_count, features).astype(NARROW)
    patch_two = patch_one + matmul(reverse_mixed, attn_out[3])
    normed_four = layer_norm(query_two, norm_gain[4], norm_bias[4]).astype(NARROW)
    query_mlp, query_kept = mlp_forward(normed_four, mlp_in[1], mlp_out[1])
    query_three = query_two + query_mlp
    normed_five = layer_norm(patch_two, norm_gain[5], norm_bias[5]).astype(NARROW)
    patch_mlp, patch_kept = mlp_forward(normed_five, mlp_in[0], mlp_out[0])
    patch_three = patch_two + patch_mlp
    grad_x_three = cot_patches[0].astype(SINGLE)
    grad_q_three = cot_queries[0].astype(SINGLE)
    normed_grad, up_grad, down_grad = mlp_backward(
        normed_five, mlp_in[0], mlp_out[0], patch_kept, grad_x_three.astype(NARROW)
    )
    input_part, gain_five, bias_five = norm_back(patch_two, norm_gain[5], norm_bias[5], normed_grad)
    grad_x_two = grad_x_three + input_part
    patch_mlp_grads = (up_grad, down_grad, gain_five, bias_five)
    normed_grad, up_grad, down_grad = mlp_backward(
        normed_four, mlp_in[1], mlp_out[1], query_kept, grad_q_three.astype(NARROW)
    )
    input_part, gain_four, bias_four = norm_back(query_two, norm_gain[4], norm_bias[4], normed_grad)
    grad_q_two = grad_q_three + input_part
    query_mlp_grads = (up_grad * leader, down_grad * leader, gain_four * leader, bias_four * leader)
    reverse_upstream = grad_x_two.astype(NARROW)
    reverse_out_grad = weight_grad(reverse_mixed, reverse_upstream)
    reverse_mixed_grad = (
        input_grad(reverse_upstream, attn_out[3])
        .astype(NARROW)
        .reshape(1, patch_count, head_count, head_size)
    )
    patch_q_grad, query_k_grad, query_v_grad = attend_backward(
        patch_query,
        reverse_keys,
        reverse_values,
        reaching,
        scaling,
        reverse_logsum,
        reverse_mixed_grad,
    )
    patch_q_grad = patch_q_grad.reshape(patch_count, features).astype(NARROW)
    reverse_q_weight = weight_grad(normed_x, patch_q_grad)
    normed_x_grad = input_grad(patch_q_grad, reverse_weights[:, :features])
    query_kv_part = jnp.concatenate(
        (query_k_grad.reshape(query_count, features), query_v_grad.reshape(query_count, features)),
        axis=1,
    )
    cross_upstream = grad_q_two.astype(NARROW)
    cross_out_grad = weight_grad(cross_mixed, cross_upstream)
    cross_heads_grad = jnp.transpose(
        split_heads(input_grad(cross_upstream, attn_out[2]).astype(NARROW), head_count), (1, 0, 2)
    )
    key_heads = split_heads(key_local, head_count)
    scores = (
        jnp.einsum("qhe,khe->hqk", query_heads, key_heads, preferred_element_type=SINGLE) * scaling
    )
    scores = jnp.where(flag_rows[None, None, :] > 0, scores, MASKED)
    local_peak = jnp.max(scores, axis=-1)
    weights = jnp.exp(scores - local_peak[..., None])
    factor = jnp.exp(local_peak - cross_logsum)
    delta = jnp.sum(
        cross_heads_grad.astype(SINGLE)
        * jnp.transpose(split_heads(cross_out, head_count), (1, 0, 2)),
        axis=-1,
    )
    block_grad = (cross_heads_grad.astype(SINGLE) * factor[..., None]).astype(NARROW)
    weight_upstream = jnp.einsum(
        "hqe,khe->hqk",
        block_grad,
        split_heads(value_local, head_count),
        preferred_element_type=SINGLE,
    )
    score_grad = (weights * weight_upstream - weights * (factor * delta)[..., None]).astype(NARROW)
    query_part = (
        jnp.einsum("hqk,khe->qhe", score_grad, key_heads, preferred_element_type=SINGLE).reshape(
            query_count, features
        )
        * scaling
    )
    key_grad = (
        jnp.einsum("hqk,qhe->khe", score_grad, query_heads, preferred_element_type=SINGLE).reshape(
            patch_count, features
        )
        * scaling
    )
    value_grad = jnp.einsum(
        "hqk,hqe->khe", weights.astype(NARROW), block_grad, preferred_element_type=SINGLE
    ).reshape(patch_count, features)
    patch_kv_grad = jnp.concatenate((key_grad, value_grad), axis=1).astype(NARROW)
    cross_kv_weight = weight_grad(normed_x, patch_kv_grad)
    normed_x_grad = normed_x_grad + input_grad(patch_kv_grad, cross_weights[:, features:])
    query_share, query_kv_share = (
        lax.psum_scatter(query_part, "blk", scatter_dimension=1, tiled=True),
        lax.psum_scatter(query_kv_part, "blk", scatter_dimension=1, tiled=True),
    )
    query_sum, query_kv_sum = (
        lax.all_gather(query_share.astype(NARROW), "blk", axis=1, tiled=True),
        lax.all_gather(query_kv_share.astype(NARROW), "blk", axis=1, tiled=True),
    )
    cross_q_weight = weight_grad(normed_q, query_sum)
    reverse_kv_weight = weight_grad(normed_q, query_kv_sum)
    normed_q_grad = input_grad(query_sum, cross_weights[:, :features]) + input_grad(
        query_kv_sum, reverse_weights[:, features:]
    )
    input_part, gain_two, bias_two = norm_back(query_one, norm_gain[2], norm_bias[2], normed_q_grad)
    grad_q_one = grad_q_two + input_part
    input_part, gain_three, bias_three = norm_back(
        patch_one, norm_gain[3], norm_bias[3], normed_x_grad
    )
    grad_x_one = grad_x_two + input_part
    cross_grads = (
        jnp.concatenate((cross_q_weight * leader, cross_kv_weight), axis=1),
        jnp.concatenate((reverse_q_weight, reverse_kv_weight * leader), axis=1),
        cross_out_grad * leader,
        reverse_out_grad,
        gain_two * leader,
        bias_two * leader,
        gain_three,
        bias_three,
    )
    normed_grad, causal_in_grad, causal_out_grad = branch_backward(
        normed_one,
        attn_in[1],
        attn_out[1],
        head_count,
        1,
        causal,
        scaling,
        causal_kept,
        grad_q_one.astype(NARROW),
    )
    input_part, gain_one, bias_one = norm_back(query_rows, norm_gain[1], norm_bias[1], normed_grad)
    grad_q_zero = grad_q_one + input_part
    causal_grads = (
        causal_in_grad * leader,
        causal_out_grad * leader,
        gain_one * leader,
        bias_one * leader,
    )
    normed_grad, window_in_grad, window_out_grad = branch_backward(
        normed_zero,
        attn_in[0],
        attn_out[0],
        head_count,
        patch_count // WIN,
        True,
        scaling,
        window_kept,
        grad_x_one.astype(NARROW),
    )
    input_part, gain_zero, bias_zero = norm_back(
        patch_rows, norm_gain[0], norm_bias[0], normed_grad
    )
    grad_x_zero = grad_x_one + input_part
    window_grads = (window_in_grad, window_out_grad, gain_zero, bias_zero)
    stacked = (
        jnp.stack((window_grads[0], causal_grads[0], cross_grads[0], cross_grads[1])),
        jnp.stack((window_grads[1], causal_grads[1], cross_grads[2], cross_grads[3])),
        jnp.stack((patch_mlp_grads[0], query_mlp_grads[0])),
        jnp.stack((patch_mlp_grads[1], query_mlp_grads[1])),
        jnp.stack(
            (
                window_grads[2],
                causal_grads[2],
                cross_grads[4],
                cross_grads[6],
                query_mlp_grads[2],
                patch_mlp_grads[2],
            )
        ),
        jnp.stack(
            (
                window_grads[3],
                causal_grads[3],
                cross_grads[5],
                cross_grads[7],
                query_mlp_grads[3],
                patch_mlp_grads[3],
            )
        ),
    )
    stacked = (
        lax.psum_scatter(stacked[0], "blk", scatter_dimension=1, tiled=True),
        lax.psum_scatter(stacked[1], "blk", scatter_dimension=1, tiled=True),
        lax.psum_scatter(stacked[2], "blk", scatter_dimension=1, tiled=True),
        lax.psum_scatter(stacked[3], "blk", scatter_dimension=1, tiled=True),
        lax.psum_scatter(stacked[4], "blk", scatter_dimension=1, tiled=True),
        lax.psum_scatter(stacked[5], "blk", scatter_dimension=1, tiled=True),
    )
    stacked = (
        lax.psum(stacked[0].astype(jnp.bfloat16), "rep").astype(jnp.float32),
        lax.psum(stacked[1].astype(jnp.bfloat16), "rep").astype(jnp.float32),
        lax.psum(stacked[2].astype(jnp.bfloat16), "rep").astype(jnp.float32),
        lax.psum(stacked[3].astype(jnp.bfloat16), "rep").astype(jnp.float32),
        lax.psum(stacked[4].astype(jnp.bfloat16), "rep").astype(jnp.float32),
        lax.psum(stacked[5].astype(jnp.bfloat16), "rep").astype(jnp.float32),
    )
    share = features // lax.axis_size("blk")
    column = lax.axis_index("blk") * share
    query_slice = lax.dynamic_slice_in_dim(query_three, column, share, 1)
    query_grad_slice = lax.dynamic_slice_in_dim(grad_q_zero, column, share, 1)
    return (
        patch_three.astype(NARROW)[None],
        query_slice.astype(NARROW)[None],
        grad_x_zero[None],
        query_grad_slice[None],
        stacked[4],
        stacked[5],
        stacked[0],
        stacked[1],
        stacked[2],
        stacked[3],
    )


def solution(mesh):
    placed = (
        P("rep", "blk", None),
        P("rep", None, None),
        P("rep", "blk"),
        P("rep"),
        P(),
        P(),
        P(),
        P(),
        P(),
        P(),
        P("rep", "blk", None),
        P("rep", None, None),
    )
    return jax.shard_map(
        body,
        mesh=mesh,
        in_specs=placed,
        out_specs=(
            P("rep", "blk", None),
            P("rep", None, "blk"),
            P("rep", "blk", None),
            P("rep", None, "blk"),
            P(None, "blk"),
            P(None, "blk"),
            P(None, "blk", None),
            P(None, "blk", None),
            P(None, "blk", None),
            P(None, "blk", None),
        ),
        check_vma=False,
    )
```

profile of v0, /device:TPU:0, one launch (start us, length us, event | category | flops | bytes accessed | tf_op | source)
XLA Modules:
  0.0 2316.9 jit_solution(18331117882950819086)
XLA Ops:
  13.9 6.6 slice_bitcast_fusion
  21.7 5.6 convolution_convert_fusion.1
  52.9 7.0 convolution_convert_fusion
  59.9 6.5 copy.116
  70.8 18.6 fusion.212
  89.4 16.2 exponential_reduce_fusion
  105.6 14.8 fusion.99
  140.2 6.9 exponential_reduce_fusion.1
  154.0 19.9 multiply_convert_fusion.3
  173.9 7.5 add_convert_fusion.1
  181.4 7.1 multiply_reduce_fusion.11
  194.0 8.2 fusion.15
  202.2 12.6 multiply_reduce_fusion.1
  214.8 14.0 multiply_convert_fusion.1
  250.7 6.7 copy-done.4
  257.3 6.4 convolution_convert_fusion.6
  263.8 34.3 %all-gather.3 = bf16[8,12,800]{2,1,0:T(8,128)(2,1)S(1)} all-gather(bf16[1,12,800]{2,1,0:T(8,128)(2,1)S(1)} %convert_bitcast_fusion.3), channel_id=2, replica_groups=mesh['blk'=8,'rep'=4] {'blk'}, dimensions={0}, use_global_device_ids=true | all-gather | bytes 172800 | tf_op jit(solution)/shard_map/all_gather | solution.py:20
  298.2 10.0 fusion.13
  308.1 31.9 %all-gather.4 = bf16[8,12,800]{2,1,0:T(8,128)(2,1)S(1)} all-gather(bf16[1,12,800]{2,1,0:T(8,128)(2,1)S(1)} %bitcast.475), channel_id=3, replica_groups=mesh['blk'=8,'rep'=4] {'blk'}, dimensions={0}, use_global_device_ids=true | all-gather | bytes 172800 | tf_op jit(solution)/shard_map/all_gather | solution.py:20
  340.1 8.5 reduce-scatter.15.cloned.1.call-done
  350.7 158.1 %all-gather.13.cloned.1.call-done = bf16[96,800,64]{1,2,0:T(8,128)(2,1)} async-done(((bf16[12,800,64]{1,2,0:T(8,128)(2,1)}), bf16[96,800,64]{1,2,0:T(8,128)(2,1)}) %all-gather.13.cloned.1.call-update) | async-done | bytes 9830416 | tf_op jit(solution)/shard_map/all_gather | solution.py:20
  514.1 88.7 %while.19 = (s32[]{:T(128)}, f32[12,800]{1,0:T(8,128)S(1)}, f32[12,800]{1,0:T(8,128)S(1)}, f32[12,800,64]{2,1,0:T(8,128)}, bf16[8,12,800]{2,1,0:T(8,128)(2,1)S(1...) while((s32[]{:T(128)}, f32[12,800]{1,0:T(8,128)S(1)}, ...), condition=%wide.region_19.20_spmd, body=%wide.region_18.19_spmd.sunk | while | flops 2534405 | bytes 11404943 | solution.py:28
  519.5 7.2 fusion.286
  532.2 7.2 fusion.286
  544.9 7.2 fusion.286
  557.6 7.2 fusion.286
  570.2 7.2 fusion.286
  582.9 7.2 fusion.286
  595.5 7.2 fusion.286
  612.0 29.0 %multiply_convert_fusion.2 = (bf16[800,3072]{1,0:T(8,128)(2,1)}, f32[800,3072]{1,0:T(8,128)}, f32[800,3072]{1,0:T(8,128)}) fusion(bf16[2,768,3072]{2,1,0:T(8,128)(2,1)} %param.22, f32[800,768]{1,0:T(8,128)S(1)} %get-tuple-element.344, f32[768]{0:T(1024)S(1)} %copy-done.96, f32[768]{0:T(1024)S(1)} %copy-done.93, f32[800]{0:T(1024)S(1)} %fusion.182, ...), kind=kOutput, calls=%fused_computation.44 | convolution fusion | flops 3937689600 | bytes 31764736 | tf_op jit(solution)/shard_map/dot_general | solution.py:50
  641.0 11.7 add_convert_fusion
  652.8 9.2 multiply_reduce_fusion.4
  675.6 15.1 subtract_convert_fusion
  690.7 8.4 convolution_multiply_fusion.2
  702.7 6.1 multiply_convert_fusion.11
  708.8 6.5 fusion.87
  715.4 6.1 multiply_convert_fusion.10
  721.8 5.9 convolution_convert_fusion.10
  732.3 36.4 %reduce-scatter.13.cloned.1.call-done = f32[800,96]{0,1:T(8,128)} async-done(((f32[800,768]{0,1:T(8,128)}), f32[800,96]{0,1:T(8,128)}) %reduce-scatter.13.cloned.1.call-update) | async-done | bytes 307216 | tf_op jit(solution)/shard_map/reduce_scatter | solution.py:342
  782.6 30.3 %all-gather.9.cloned.1.call-done = bf16[800,768]{0,1:T(8,128)(2,1)} async-done(((bf16[800,96]{0,1:T(8,128)(2,1)}), bf16[800,768]{0,1:T(8,128)(2,1)}) %all-gather.9.cloned.1.call-update) | async-done | bytes 1228816 | tf_op jit(solution)/shard_map/all_gather | solution.py:346
  829.9 5.3 convolution_bitcast_fusion.2
  835.3 7.8 multiply_bitcast_fusion.1
  843.1 6.7 pad_maximum_fusion.1
  855.6 7.1 multiply_bitcast_fusion
  862.7 7.0 pad_maximum_fusion.2
  900.6 7.0 copy.142
  907.6 7.7 convert_element_type.477
  929.7 26.0 %multiply_reduce_fusion = (f32[12,800]{1,0:T(8,128)S(1)}, f32[12,800,800]{1,2,0:T(8,128)}) fusion(f32[12,800,800]{1,2,0:T(8,128)} %get-tuple-element.331, f32[12,800]{1,0:T(8,128)S(1)} %log_add_fusion.1, bf16[800,12,64]{0,2,1:T(8,128)(2,1)S(1)} %bitcast.437, bf16[1,800,3,12,64]{1,4,3,2,0:T(8,128)(2,1)} %bitcast.430), kind=kOutput, calls=%fused_computation.10 | convolution fusion | flops 1006070400 | bytes 67808256 | tf_op jit(solution)/shard_map/brhe,bkhe->bhrk/dot_general | solution.py:87
  955.6 29.4 %multiply_convert_fusion = bf16[12,800,800]{1,2,0:T(8,128)(2,1)} fusion(f32[12,800,800]{1,2,0:T(8,128)} %get-tuple-element.356, f32[12,800,800]{1,2,0:T(8,128)} %get-tuple-element.331, f32[12,800]{1,0:T(8,128)S(1)} %get-tuple-element.355, f32[12,800]{1,0:T(8,128)S(1)} %log_add_fusion.1), kind=kLoop, calls=%fused_computation.9 | loop fusion | flops 30720000 | bytes 76876800 | tf_op jit(solution)/shard_map/convert_element_type | solution.py:91
  985.0 12.8 fusion.132
  997.8 11.5 fusion.131
  1009.3 14.9 fusion.128
  1032.6 6.8 multiply_bitcast_fusion.2
  1039.4 15.8 pad_maximum_fusion
  1062.4 7.6 fusion.78
  1072.4 7.0 fusion.137
  1081.7 226.3 %reduce-scatter.21.cloned.1.call-done = f32[2,96,3072]{2,1,0:T(8,128)} async-done(((f32[2,768,3072]{2,1,0:T(8,128)}), f32[2,96,3072]{2,1,0:T(8,128)}) %reduce-scatter.21.cloned.1.call-update) | async-done | bytes 2359312 | tf_op jit(solution)/shard_map/reduce_scatter | solution.py:434
  1310.9 314.0 %reduce-scatter.23.cloned.1.call-done = f32[2,384,768]{2,1,0:T(8,128)} async-done(((f32[2,3072,768]{2,1,0:T(8,128)}), f32[2,384,768]{2,1,0:T(8,128)}) %reduce-scatter.23.cloned.1.call-update) | async-done | bytes 2359312 | tf_op jit(solution)/shard_map/reduce_scatter | solution.py:435
  1627.6 449.7 %reduce-scatter.17.cloned.1.call-done = f32[4,96,2304]{2,1,0:T(8,128)} async-done(((f32[4,768,2304]{2,1,0:T(8,128)}), f32[4,96,2304]{2,1,0:T(8,128)}) %reduce-scatter.17.cloned.1.call-update) | async-done | bytes 3538960 | tf_op jit(solution)/shard_map/reduce_scatter | solution.py:432
  2080.7 7.4 fusion.32
  2097.2 43.9 %reduce-scatter.25.cloned.1.call-done = f32[96,6]{1,0:T(8,128)} async-done(((f32[768,6]{1,0:T(8,128)}), f32[96,6]{1,0:T(8,128)}) %reduce-scatter.25.cloned.1.call-update) | async-done | bytes 2320
  2141.9 62.9 %reduce-scatter.27.cloned.1.call-done = f32[96,6]{1,0:T(8,128)} async-done(((f32[768,6]{1,0:T(8,128)}), f32[96,6]{1,0:T(8,128)}) %reduce-scatter.27.cloned.1.call-update) | async-done | bytes 2320
  2205.6 5.7 all-reduce
  2212.5 89.4 %all-reduce.4.cloned.1.call-done = (bf16[4,96,2304]{2,1,0:T(8,128)(2,1)}, bf16[4,96,768]{2,1,0:T(8,128)(2,1)}, bf16[2,96,3072]{2,1,0:T(8,128)(2,1)}, bf16[2,384,768]{2,1,0:T(8,128)(2,1)}) async-done(((bf16[4,96,2304]{2,1,0:T(8,128)(2,1)}, bf16[4,96,768]{2,1,0:T(8,128)(2,1)}, bf16[2,96,3072]{2,1,0:T(8,128)(2,1)}, bf16[2,384,768]{2,1,0:T(8,128)(2,1)}), (bf16[4,96,2304]{2,1,0:T(8,128)(2,1)}, ...) | async-done | bytes 4718608 | tf_op jit(solution)/shard_map/psum | solution.py:440
  (566 shorter events, 297.2 us)
Async XLA Ops:
  7.2 341.4 %reduce-scatter.15.cloned.1.call-start = ((), (), s32[]{:S(2)}) async-start(), calls=%async_computation.10 | async-start | bytes 6193152 | tf_op jit(solution)/shard_map/reduce_scatter | solution.py:343
  10.3 10.8 copy-start.113
  12.4 8.7 copy-start.117
  12.7 40.1 %copy-start.109 = (f32[800]{0:T(1024)}, f32[800]{0:T(1024)S(1)}, u32[]{:S(2)}) copy-start(f32[800]{0:T(1024)S(1)} %broadcast_multiply_fusion.8) | copy-start | bytes 9604
  13.8 39.0 %copy-start.129 = (f32[800]{0:T(1024)}, f32[800]{0:T(1024)S(1)}, u32[]{:S(2)}) copy-start(f32[800]{0:T(1024)S(1)} %fusion.180) | copy-start | bytes 9604
  13.8 7.9 copy-start.29
  21.1 31.7 %copy-start.131 = (f32[768]{0:T(1024)}, f32[768]{0:T(1024)S(1)}, u32[]{:S(2)}) copy-start(f32[768]{0:T(1024)S(1)} %get-tuple-element.360) | copy-start | bytes 9220
  21.1 31.7 %copy-start.147 = (f32[768]{0:T(1024)}, f32[768]{0:T(1024)S(1)}, u32[]{:S(2)}) copy-start(f32[768]{0:T(1024)S(1)} %get-tuple-element.276) | copy-start | bytes 9220
  21.1 45.3 %copy-start.111 = (f32[768]{0:T(1024)}, f32[768]{0:T(1024)S(1)}, u32[]{:S(2)}) copy-start(f32[768]{0:T(1024)S(1)} %get-tuple-element.362) | copy-start | bytes 9220
  21.1 102.9 %copy-start.103 = (f32[768]{0:T(1024)}, f32[768]{0:T(1024)S(1)}, u32[]{:S(2)}) copy-start(f32[768]{0:T(1024)S(1)} %get-tuple-element.361) | copy-start | bytes 9220
  21.1 132.8 %copy-start.151 = (f32[768]{0:T(1024)}, f32[768]{0:T(1024)S(1)}, u32[]{:S(2)}) copy-start(f32[768]{0:T(1024)S(1)} %get-tuple-element.278) | copy-start | bytes 9220
  21.1 167.4 %copy-start.133 = (f32[768]{0:T(1024)}, f32[768]{0:T(1024)S(1)}, u32[]{:S(2)}) copy-start(f32[768]{0:T(1024)S(1)} %get-tuple-element.358) | copy-start | bytes 9220
  52.5 98.6 %copy-start.5 = (f32[512,768]{1,0:T(8,128)}, f32[512,768]{1,0:T(8,128)S(1)}, u32[]{:S(2)}) copy-start(f32[512,768]{1,0:T(8,128)S(1)} %get-tuple-element.335) | copy-start | bytes 4718596
  52.5 13.9 copy-start.115
  52.8 13.6 copy-start.121
  89.4 16.2 copy-start.87
  105.6 14.8 copy-start.34
  131.9 8.2 copy-start.15
  151.1 22.8 slice-start.9
  153.6 34.9 %copy-start.18 = (f32[512,768]{1,0:T(8,128)}, f32[512,768]{1,0:T(8,128)S(1)}, u32[]{:S(2)}) copy-start(f32[512,768]{1,0:T(8,128)S(1)} %get-tuple-element.339) | copy-start | bytes 4718596
  153.6 34.9 %copy-start.119 = (f32[512]{0:T(512)}, f32[512]{0:T(512)S(1)}, u32[]{:S(2)}) copy-start(f32[512]{0:T(512)S(1)} %broadcast_multiply_fusion.9) | copy-start | bytes 6148
  153.9 34.6 %copy-start.137 = (f32[512]{0:T(512)}, f32[512]{0:T(512)S(1)}, u32[]{:S(2)}) copy-start(f32[512]{0:T(512)S(1)} %fusion.185) | copy-start | bytes 6148
  154.0 19.9 copy-start.63
  154.0 19.9 slice-start.10
  154.0 19.9 slice-start.11
  181.4 7.1 copy-start.160
  214.8 14.0 copy-start.43
  235.4 273.4 %all-gather.13.cloned.1.call-start = ((), (), s32[]{:S(2)}) async-start(), calls=%async_computation.16 | async-start | bytes 12386304 | tf_op jit(solution)/shard_map/all_gather | solution.py:20
  236.2 62.0 %copy-start.153 = (pred[512]{0:T(512)(128)(4,1)}, pred[512]{0:T(512)(128)(4,1)S(1)}, u32[]{:S(2)}) copy-start(pred[512]{0:T(512)(128)(4,1)S(1)} %gt.18) | copy-start | bytes 1540
  250.7 47.5 %copy-start.89 = (f32[12,800]{1,0:T(8,128)}, f32[12,800]{1,0:T(8,128)S(1)}, u32[]{:S(2)}) copy-start(f32[12,800]{1,0:T(8,128)S(1)} %get-tuple-element.341) | copy-start | bytes 115204
  263.8 445.0 %all-gather.11.cloned.1.call-start = ((), (), s32[]{:S(2)}) async-start(), calls=%async_computation.11 | async-start | bytes 3096576 | tf_op jit(solution)/shard_map/all_gather | solution.py:347
  350.5 418.2 %reduce-scatter.13.cloned.1.call-start = ((), (), s32[]{:S(2)}) async-start(), calls=%async_computation.8 | async-start | bytes 3096576 | tf_op jit(solution)/shard_map/reduce_scatter | solution.py:342
  611.4 50.6 %copy-start.7 = (f32[800,768]{1,0:T(8,128)}, f32[800,768]{1,0:T(8,128)S(1)}, u32[]{:S(2)}) copy-start(f32[800,768]{1,0:T(8,128)S(1)} %get-tuple-element.344) | copy-start | bytes 7372804
  612.0 29.0 %copy-start.55 = (bf16[1,800,768]{2,1,0:T(8,128)(2,1)S(1)}, bf16[1,800,768]{2,1,0:T(8,128)(2,1)}, u32[]{:S(2)}) copy-start(bf16[1,800,768]{2,1,0:T(8,128)(2,1)} %param.25) | copy-start | bytes 3686404
  652.7 9.3 copy-start.54
  675.6 15.1 copy-start.42
  699.2 113.7 %all-gather.9.cloned.1.call-start = ((), (), s32[]{:S(2)}) async-start(), calls=%async_computation.9 | async-start | bytes 1548288 | tf_op jit(solution)/shard_map/all_gather | solution.py:346
  708.8 12.7 slice-start
  708.8 12.7 slice-start.1
  708.8 12.7 slice-start.2
  727.7 43.0 %copy-start.6 = (f32[512,768]{1,0:T(8,128)S(1)}, f32[512,768]{1,0:T(8,128)}, u32[]{:S(2)}) copy-start(f32[512,768]{1,0:T(8,128)} %copy-done.5) | copy-start | bytes 4718596
  727.7 43.0 %copy-start.112 = (f32[768]{0:T(1024)S(1)}, f32[768]{0:T(1024)}, u32[]{:S(2)}) copy-start(f32[768]{0:T(1024)} %copy-done.111) | copy-start | bytes 9220
  727.7 43.0 %copy-start.116 = (f32[512]{0:T(512)S(1)}, f32[512]{0:T(512)}, u32[]{:S(2)}) copy-start(f32[512]{0:T(512)} %copy-done.115) | copy-start | bytes 6148
  727.7 43.0 %copy-start.122 = (f32[512]{0:T(512)S(1)}, f32[512]{0:T(512)}, u32[]{:S(2)}) copy-start(f32[512]{0:T(512)} %copy-done.121) | copy-start | bytes 6148
  770.4 309.1 %reduce-scatter.19.cloned.1.call-start = ((), (), s32[]{:S(2)}) async-start(), calls=%async_computation.13 | async-start | bytes 10616832 | tf_op jit(solution)/shard_map/reduce_scatter | solution.py:433
  779.8 33.2 %copy-start.11 = (f32[800,768]{1,0:T(8,128)S(1)}, f32[800,768]{1,0:T(8,128)}, u32[]{:S(2)}) copy-start(f32[800,768]{1,0:T(8,128)} %copy-done.9) | copy-start | bytes 7372804
  779.8 33.2 %copy-start.98 = (f32[800]{0:T(1024)S(1)}, f32[800]{0:T(1024)}, u32[]{:S(2)}) copy-start(f32[800]{0:T(1024)} %copy-done.97) | copy-start | bytes 9604
  779.8 33.2 %copy-start.100 = (f32[800]{0:T(1024)S(1)}, f32[800]{0:T(1024)}, u32[]{:S(2)}) copy-start(f32[800]{0:T(1024)} %copy-done.99) | copy-start | bytes 9604
  779.8 33.1 %copy-start.104 = (f32[768]{0:T(1024)S(1)}, f32[768]{0:T(1024)}, u32[]{:S(2)}) copy-start(f32[768]{0:T(1024)} %copy-done.103) | copy-start | bytes 9220
  782.6 35.4 %copy-start.108 = (f32[800]{0:T(1024)S(1)}, f32[800]{0:T(1024)}, u32[]{:S(2)}) copy-start(f32[800]{0:T(1024)} %copy-done.107) | copy-start | bytes 9604
  829.3 478.7 %reduce-scatter.21.cloned.1.call-start = ((), (), s32[]{:S(2)}) async-start(), calls=%async_computation.14 | async-start | bytes 21233664 | tf_op jit(solution)/shard_map/reduce_scatter | solution.py:434
  849.8 775.0 %reduce-scatter.23.cloned.1.call-start = ((), (), s32[]{:S(2)}) async-start(), calls=%async_computation.15 | async-start | bytes 21233664 | tf_op jit(solution)/shard_map/reduce_scatter | solution.py:435
  869.8 1207.5 %reduce-scatter.17.cloned.1.call-start = ((), (), s32[]{:S(2)}) async-start(), calls=%async_computation.12 | async-start | bytes 31850496 | tf_op jit(solution)/shard_map/reduce_scatter | solution.py:432
  881.5 8.0 copy-start.3
  907.6 7.7 copy-start.47
  907.6 7.7 copy-start.53
  907.6 7.8 copy-start.92
  1030.2 9.2 slice-start.5
  1055.2 1085.8 %reduce-scatter.25.cloned.1.call-start = ((), (), s32[]{:S(2)}) async-start(), calls=%async_computation.17 | async-start | bytes 442368
  1062.4 8.6 copy-start.145
  1062.4 10.1 copy-start.19
  1071.0 1133.8 %reduce-scatter.27.cloned.1.call-start = ((), (), s32[]{:S(2)}) async-start(), calls=%async_computation.18 | async-start | bytes 442368
  1072.1 1229.8 %all-reduce.4.cloned.1.call-start = ((), (), s32[]{:S(2)}) async-start(), calls=%async_computation.19 | async-start | bytes 9437184 | tf_op jit(solution)/shard_map/psum | solution.py:440
  2080.7 9.6 copy-start.26
  (121 other events, 338.1 us)
Sparse Core Ops, SparseCore 0:
  235.5 113.0 reduce-scatter.14
  351.6 157.1 all-gather.12
  511.8 54.2 all-gather.10
  699.3 69.3 reduce-scatter.12
  771.6 41.3 all-gather.8
  829.4 161.8 reduce-scatter.18
  995.7 312.3 reduce-scatter.20
  1312.4 312.3 reduce-scatter.22
  1629.3 447.9 reduce-scatter.16
  2080.4 60.5 reduce-scatter.24
  2144.3 60.4 reduce-scatter.26
  2208.3 93.5 all-reduce.3
where the time goes:
time: 2320 us
  waiting for transfers between devices  1420 us (61%)
  matrix products  425 us (18%)
  other arithmetic  226 us (10%)
  local copies, waits for them, and re-layouts  155 us (7%)
  blocking collectives  71.9 us (3%)
    reduce_scatter x1, waiting for transfers between devices, body(): lax.psum_scatter(stacked[0], 'blk', scatter_dimension=1, tiled=True)  450 us
    reduce_scatter x1, waiting for transfers between devices, body(): lax.psum_scatter(stacked[3], 'blk', scatter_dimension=1, tiled=True)  314 us
    reduce_scatter x1, waiting for transfers between devices, body(): lax.psum_scatter(stacked[2], 'blk', scatter_dimension=1, tiled=True)  226 us
    all_gather x1, waiting for transfers between devices, merged(): lax.all_gather(part.astype(kind), axis)  158 us
    unnamed x14, waiting for transfers between devices  107 us
    dot_general x14, matrix products, matmul(): return jnp.dot(former, latter, preferred_element_type=SINGLE)  96.7 us
    psum x1, waiting for transfers between devices, body(): lax.psum(stacked[0].astype(jnp.bfloat16), 'rep').astype(jnp.float32)  89.4 us
    dot_general x14, matrix products, input_grad(): lax.dot_general(upstream, weight, (((1,), (1,)), ((), ())), preferred_ele...  80.7 us
  transfers between devices with their start and end apart: 12, of which 10 were waited for; matrix products, arithmetic and copies ran while one was open for 23% of the time, Pallas kernels for 0%

commit v1 on v0

--- a/solution.py
+++ b/solution.py
@@ -15,19 +15,81 @@
 SINGLE = jnp.float32
 
 
-def merged(x, axis, combine):
-    everything = jax.tree.map(
-        lambda part, kind: lax.all_gather(part.astype(kind), axis),
-        x,
-        jax.tree.map(lambda a: jnp.bfloat16 if a.dtype == jnp.float32 else a.dtype, x),
-    )
-
-    def take(k):
-        return jax.tree.map(lambda part, own: part[k].astype(own.dtype), everything, x)
-
-    return lax.fori_loop(
-        1, lax.axis_size(axis), lambda k, so_far: combine(so_far, take(k)), take(0)
-    )
+def bits_of(count):
+    return max(count - 1, 0).bit_length()
+
+
+def swap(tensor, axis, bit):
+    count = lax.axis_size(axis)
+    return lax.ppermute(tensor, axis, [(i, i ^ (1 << bit)) for i in range(count)])
+
+
+def pick(tensor, place, dim):
+    return lax.dynamic_index_in_dim(tensor, place, dim, keepdims=False)
+
+
+def fold(tensor, axis, bit, dim):
+    own = (lax.axis_index(axis) >> bit) & 1
+    arrived = swap(pick(tensor, 1 - own, dim).astype(NARROW), axis, bit)
+    return pick(tensor, own, dim).astype(SINGLE) + arrived.astype(SINGLE)
+
+
+def unfold(tensor, axis, bit, dim):
+    own = (lax.axis_index(axis) >> bit) & 1
+    arrived = swap(tensor, axis, bit)
+    return jnp.where(
+        own == 0,
+        jnp.stack((tensor, arrived), axis=dim),
+        jnp.stack((arrived, tensor), axis=dim),
+    )
+
+
+def scatter_blk(tensor):
+    bits = bits_of(lax.axis_size("blk"))
+    tensor = tensor.reshape((2,) * bits + tensor.shape[1:])
+    for bit in range(bits):
+        tensor = fold(tensor, "blk", bit, bits - 1 - bit)
+    return tensor
+
+
+def gather_blk(tensor):
+    bits = bits_of(lax.axis_size("blk"))
+    tail = tensor.shape
+    for bit in reversed(range(bits)):
+        tensor = unfold(tensor, "blk", bit, 0)
+    order = tuple(reversed(range(bits))) + tuple(range(bits, bits + len(tail)))
+    return jnp.transpose(tensor, order).reshape((2**bits,) + tail)
+
+
+def sum_rep_scatter(tensor, dim):
+    bits = bits_of(lax.axis_size("rep"))
+    shape = tensor.shape
+    tensor = tensor.reshape(
+        shape[:dim] + (2,) * bits + (shape[dim] // 2**bits,) + shape[dim + 1 :]
+    )
+    for bit in range(bits):
+        tensor = fold(tensor, "rep", bit, dim)
+    return tensor
+
+
+def gather_rep(tensor, dim):
+    bits = bits_of(lax.axis_size("rep"))
+    for bit in reversed(range(bits)):
+        tensor = unfold(tensor, "rep", bit, dim)
+    shape = tensor.shape
+    return tensor.reshape(shape[:dim] + (-1,) + shape[dim + bits + 1 :])
+
+
+def reduce_all(tensor):
+    count = lax.axis_size("blk")
+    tensor = tensor.reshape(count, tensor.shape[0] // count, tensor.shape[1])
+    tensor = sum_rep_scatter(tensor, 1)
+    tensor = scatter_blk(tensor).astype(NARROW)
+    return gather_rep(tensor, 0)
+
+
+def reduce_rep(tensor):
+    return gather_rep(sum_rep_scatter(tensor, 0).astype(NARROW), 0)
 
 
 def layer_norm(tensor, scales, shifts):
@@ -147,17 +209,6 @@
     unused, pullback = jax.vjp(gelu_exact, preact)
     grad_preact = pullback(input_grad(upstream, w_down))[0].astype(NARROW)
     return (input_grad(grad_preact, w_up), weight_grad(normed, grad_preact), grad_down)
-
-
-def combine(former, latter):
-    peak = jnp.maximum(former[0], latter[0])
-    first_factor = jnp.exp(former[0] - peak)
-    second_factor = jnp.exp(latter[0] - peak)
-    return (
-        peak,
-        former[1] * first_factor + latter[1] * second_factor,
-        former[2] * first_factor[..., None] + latter[2] * second_factor[..., None],
-    )
 
 
 def block_stats(query_heads, key_rows, value_rows, flag_rows, scaling):
@@ -201,16 +252,32 @@
     head_count = HEADS
     head_size = features // head_count
     scaling = 1.0 / math.sqrt(head_size)
+    blocks = lax.axis_size("blk")
+    place = lax.axis_index("blk")
+    share = features // blocks
+    hidden = mlp_in.shape[2]
     patch_rows = patches[0].astype(SINGLE)
     query_rows = queries[0].astype(SINGLE)
     patch_count = patch_rows.shape[0]
     query_count = query_rows.shape[0]
+    part = -(-query_count // (blocks * 8)) * 8
+    padded = part * blocks
     length = answer_length[0]
     flag_rows = jnp.repeat(window_valid[0], WIN).astype(NARROW)
     positions = jnp.arange(query_count, dtype=jnp.int32)
     causal = (positions[None, :] <= positions[:, None])[None, None]
     reaching = (positions < length)[None, None, None, :]
-    leader = (lax.axis_index("blk") == 0).astype(SINGLE)
+    leader = (place == 0).astype(SINGLE)
+
+    def own_columns(tensor, width=share):
+        return lax.dynamic_slice_in_dim(tensor, place * width, width, 1)
+
+    def pad_rows(tensor):
+        return jnp.pad(tensor, ((0, padded - query_count), (0, 0)))
+
+    def own_rows(tensor):
+        return lax.dynamic_slice_in_dim(pad_rows(tensor), place * part, part, 0)
+
     normed_zero = layer_norm(patch_rows, norm_gain[0], norm_bias[0]).astype(NARROW)
     window_out, window_kept = branch_forward(
         normed_zero, attn_in[0], attn_out[0], head_count, patch_count // WIN, True, scaling
@@ -230,14 +297,23 @@
     patch_kv = matmul(normed_x, cross_weights[:, features:]).astype(NARROW)
     key_local = patch_kv[:, :features]
     value_local = patch_kv[:, features:]
-    peaks, totals, accumulated = merged(
-        block_stats(query_heads, key_local, value_local, flag_rows, scaling), "blk", combine
-    )
-    cross_logsum = peaks + jnp.log(totals)
-    cross_out = jnp.transpose(accumulated / totals[..., None], (1, 0, 2)).reshape(
+    local_peak, local_total, local_out = block_stats(
+        query_heads, key_local, value_local, flag_rows, scaling
+    )
+    local_log = local_peak + jnp.log(local_total)
+    local_mean = jnp.transpose(local_out / local_total[..., None], (1, 0, 2)).reshape(
         query_count, features
     )
-    cross_mixed = cross_out.astype(NARROW)
+    logs = lax.all_gather(jnp.transpose(local_log, (1, 0)), "blk")
+    cross_logsum = jax.nn.logsumexp(logs, axis=0)
+    weighting = jnp.exp(jnp.transpose(local_log, (1, 0)) - cross_logsum)
+    weighted = (split_heads(local_mean, head_count) * weighting[..., None]).reshape(
+        query_count, features
+    )
+    cross_share = scatter_blk(pad_rows(weighted.astype(NARROW)).reshape(blocks, part, features))
+    cross_out = gather_blk(cross_share.astype(NARROW)).reshape(padded, features)[:query_count]
+    cross_logsum = jnp.transpose(cross_logsum, (1, 0))
+    cross_mixed = cross_out
     query_two = query_one + matmul(cross_mixed, attn_out[2])
     reverse_weights = attn_in[3]
     patch_query = split_heads(
@@ -251,9 +327,6 @@
     )
     reverse_mixed = reverse_mixed.reshape(patch_count, features).astype(NARROW)
     patch_two = patch_one + matmul(reverse_mixed, attn_out[3])
-    normed_four = layer_norm(query_two, norm_gain[4], norm_bias[4]).astype(NARROW)
-    query_mlp, query_kept = mlp_forward(normed_four, mlp_in[1], mlp_out[1])
-    query_three = query_two + query_mlp
     normed_five = layer_norm(patch_two, norm_gain[5], norm_bias[5]).astype(NARROW)
     patch_mlp, patch_kept = mlp_forward(normed_five, mlp_in[0], mlp_out[0])
     patch_three = patch_two + patch_mlp
@@ -262,15 +335,10 @@
     normed_grad, up_grad, down_grad = mlp_backward(
         normed_five, mlp_in[0], mlp_out[0], patch_kept, grad_x_three.astype(NARROW)
     )
+    patch_up_grad = reduce_all(up_grad.astype(NARROW))
+    patch_down_grad = reduce_all(down_grad.astype(NARROW))
     input_part, gain_five, bias_five = norm_back(patch_two, norm_gain[5], norm_bias[5], normed_grad)
     grad_x_two = grad_x_three + input_part
-    patch_mlp_grads = (up_grad, down_grad, gain_five, bias_five)
-    normed_grad, up_grad, down_grad = mlp_backward(
-        normed_four, mlp_in[1], mlp_out[1], query_kept, grad_q_three.astype(NARROW)
-    )
-    input_part, gain_four, bias_four = norm_back(query_two, norm_gain[4], norm_bias[4], normed_grad)
-    grad_q_two = grad_q_three + input_part
-    query_mlp_grads = (up_grad * leader, down_grad * leader, gain_four * leader, bias_four * leader)
     reverse_upstream = grad_x_two.astype(NARROW)
     reverse_out_grad = weight_grad(reverse_mixed, reverse_upstream)
     reverse_mixed_grad = (
@@ -294,8 +362,22 @@
         (query_k_grad.reshape(query_count, features), query_v_grad.reshape(query_count, features)),
         axis=1,
     )
+    query_kv_share = scatter_blk(
+        pad_rows(query_kv_part.astype(NARROW)).reshape(blocks, part, 2 * features)
+    )
+    normed_four = layer_norm(query_two, norm_gain[4], norm_bias[4]).astype(NARROW)
+    query_mlp, (preact, hidden_q) = mlp_forward(normed_four, mlp_in[1], mlp_out[1])
+    query_three = query_two + query_mlp
+    upstream = grad_q_three.astype(NARROW)
+    unused, pullback = jax.vjp(gelu_exact, preact)
+    grad_preact = pullback(input_grad(upstream, mlp_out[1]))[0].astype(NARROW)
+    normed_grad = input_grad(grad_preact, mlp_in[1])
+    query_up_grad = reduce_rep(weight_grad(own_columns(normed_four), grad_preact))
+    query_down_grad = reduce_rep(weight_grad(own_columns(hidden_q, hidden // blocks), upstream))
+    input_part, gain_four, bias_four = norm_back(query_two, norm_gain[4], norm_bias[4], normed_grad)
+    grad_q_two = grad_q_three + input_part
     cross_upstream = grad_q_two.astype(NARROW)
-    cross_out_grad = weight_grad(cross_mixed, cross_upstream)
+    cross_out_grad = weight_grad(own_columns(cross_mixed), cross_upstream)
     cross_heads_grad = jnp.transpose(
         split_heads(input_grad(cross_upstream, attn_out[2]).astype(NARROW), head_count), (1, 0, 2)
     )
@@ -304,12 +386,11 @@
         jnp.einsum("qhe,khe->hqk", query_heads, key_heads, preferred_element_type=SINGLE) * scaling
     )
     scores = jnp.where(flag_rows[None, None, :] > 0, scores, MASKED)
-    local_peak = jnp.max(scores, axis=-1)
     weights = jnp.exp(scores - local_peak[..., None])
     factor = jnp.exp(local_peak - cross_logsum)
     delta = jnp.sum(
         cross_heads_grad.astype(SINGLE)
-        * jnp.transpose(split_heads(cross_out, head_count), (1, 0, 2)),
+        * jnp.transpose(split_heads(cross_out, head_count), (1, 0, 2)).astype(SINGLE),
         axis=-1,
     )
     block_grad = (cross_heads_grad.astype(SINGLE) * factor[..., None]).astype(NARROW)
@@ -326,6 +407,7 @@
         )
         * scaling
     )
+    query_share = scatter_blk(pad_rows(query_part.astype(NARROW)).reshape(blocks, part, features))
     key_grad = (
         jnp.einsum("hqk,qhe->khe", score_grad, query_heads, preferred_element_type=SINGLE).reshape(
             patch_count, features
@@ -337,55 +419,16 @@
     ).reshape(patch_count, features)
     patch_kv_grad = jnp.concatenate((key_grad, value_grad), axis=1).astype(NARROW)
     cross_kv_weight = weight_grad(normed_x, patch_kv_grad)
+    cross_total = reduce_all(
+        jnp.concatenate(
+            (cross_kv_weight, reverse_q_weight, reverse_out_grad), axis=1
+        ).astype(NARROW)
+    )
     normed_x_grad = normed_x_grad + input_grad(patch_kv_grad, cross_weights[:, features:])
-    query_share, query_kv_share = (
-        lax.psum_scatter(query_part, "blk", scatter_dimension=1, tiled=True),
-        lax.psum_scatter(query_kv_part, "blk", scatter_dimension=1, tiled=True),
-    )
-    query_sum, query_kv_sum = (
-        lax.all_gather(query_share.astype(NARROW), "blk", axis=1, tiled=True),
-        lax.all_gather(query_kv_share.astype(NARROW), "blk", axis=1, tiled=True),
-    )
-    cross_q_weight = weight_grad(normed_q, query_sum)
-    reverse_kv_weight = weight_grad(normed_q, query_kv_sum)
-    normed_q_grad = input_grad(query_sum, cross_weights[:, :features]) + input_grad(
-        query_kv_sum, reverse_weights[:, features:]
-    )
-    input_part, gain_two, bias_two = norm_back(query_one, norm_gain[2], norm_bias[2], normed_q_grad)
-    grad_q_one = grad_q_two + input_part
     input_part, gain_three, bias_three = norm_back(
         patch_one, norm_gain[3], norm_bias[3], normed_x_grad
     )
     grad_x_one = grad_x_two + input_part
-    cross_grads = (
-        jnp.concatenate((cross_q_weight * leader, cross_kv_weight), axis=1),
-        jnp.concatenate((reverse_q_weight, reverse_kv_weight * leader), axis=1),
-        cross_out_grad * leader,
-        reverse_out_grad,
-        gain_two * leader,
-        bias_two * leader,
-        gain_three,
-        bias_three,
-    )
-    normed_grad, causal_in_grad, causal_out_grad = branch_backward(
-        normed_one,
-        attn_in[1],
-        attn_out[1],
-        head_count,
-        1,
-        causal,
-        scaling,
-        causal_kept,
-        grad_q_one.astype(NARROW),
-    )
-    input_part, gain_one, bias_one = norm_back(query_rows, norm_gain[1], norm_bias[1], normed_grad)
-    grad_q_zero = grad_q_one + input_part
-    causal_grads = (
-        causal_in_grad * leader,
-        causal_out_grad * leader,
-        gain_one * leader,
-        bias_one * leader,
-    )
     normed_grad, window_in_grad, window_out_grad = branch_backward(
         normed_zero,
         attn_in[0],
@@ -401,64 +444,96 @@
         patch_rows, norm_gain[0], norm_bias[0], normed_grad
     )
     grad_x_zero = grad_x_one + input_part
-    window_grads = (window_in_grad, window_out_grad, gain_zero, bias_zero)
-    stacked = (
-        jnp.stack((window_grads[0], causal_grads[0], cross_grads[0], cross_grads[1])),
-        jnp.stack((window_grads[1], causal_grads[1], cross_grads[2], cross_grads[3])),
-        jnp.stack((patch_mlp_grads[0], query_mlp_grads[0])),
-        jnp.stack((patch_mlp_grads[1], query_mlp_grads[1])),
-        jnp.stack(
-            (
-                window_grads[2],
-                causal_grads[2],
-                cross_grads[4],
-                cross_grads[6],
-                query_mlp_grads[2],
-                patch_mlp_grads[2],
-            )
-        ),
-        jnp.stack(
-            (
-                window_grads[3],
-                causal_grads[3],
-                cross_grads[5],
-                cross_grads[7],
-                query_mlp_grads[3],
-                patch_mlp_grads[3],
-            )
-        ),
-    )
-    stacked = (
-        lax.psum_scatter(stacked[0], "blk", scatter_dimension=1, tiled=True),
-        lax.psum_scatter(stacked[1], "blk", scatter_dimension=1, tiled=True),
-        lax.psum_scatter(stacked[2], "blk", scatter_dimension=1, tiled=True),
-        lax.psum_scatter(stacked[3], "blk", scatter_dimension=1, tiled=True),
-        lax.psum_scatter(stacked[4], "blk", scatter_dimension=1, tiled=True),
-        lax.psum_scatter(stacked[5], "blk", scatter_dimension=1, tiled=True),
-    )
-    stacked = (
-        lax.psum(stacked[0].astype(jnp.bfloat16), "rep").astype(jnp.float32),
-        lax.psum(stacked[1].astype(jnp.bfloat16), "rep").astype(jnp.float32),
-        lax.psum(stacked[2].astype(jnp.bfloat16), "rep").astype(jnp.float32),
-        lax.psum(stacked[3].astype(jnp.bfloat16), "rep").astype(jnp.float32),
-        lax.psum(stacked[4].astype(jnp.bfloat16), "rep").astype(jnp.float32),
-        lax.psum(stacked[5].astype(jnp.bfloat16), "rep").astype(jnp.float32),
-    )
-    share = features // lax.axis_size("blk")
-    column = lax.axis_index("blk") * share
-    query_slice = lax.dynamic_slice_in_dim(query_three, column, share, 1)
-    query_grad_slice = lax.dynamic_slice_in_dim(grad_q_zero, column, share, 1)
+    window_total = reduce_all(
+        jnp.concatenate((window_in_grad, window_out_grad), axis=1).astype(NARROW)
+    )
+    query_sum = query_share.astype(NARROW)
+    query_kv_sum = query_kv_share.astype(NARROW)
+    share_normed = own_rows(normed_q)
+    shared_total = reduce_all(
+        weight_grad(share_normed, jnp.concatenate((query_sum, query_kv_sum), axis=1)).astype(NARROW)
+    )
+    normed_q_grad = input_grad(query_sum, cross_weights[:, :features]) + input_grad(
+        query_kv_sum, reverse_weights[:, features:]
+    )
+    input_part, gain_two, bias_two = norm_back(
+        own_rows(query_one), norm_gain[2], norm_bias[2], normed_q_grad
+    )
+    input_part = gather_blk(input_part.astype(NARROW)).reshape(padded, features)[:query_count]
+    grad_q_one = grad_q_two + input_part.astype(SINGLE)
+    project, attended, logsum = causal_kept
+    upstream = grad_q_one.astype(NARROW)
+    causal_out_grad = weight_grad(own_columns(attended), upstream)
+    grad_attended = (
+        input_grad(upstream, attn_out[1])
+        .astype(NARROW)
+        .reshape(1, query_count, head_count, head_size)
+    )
+    columns = project.reshape(1, query_count, 3, head_count, head_size)
+    grads = attend_backward(
+        columns[:, :, 0],
+        columns[:, :, 1],
+        columns[:, :, 2],
+        causal,
+        scaling,
+        logsum,
+        grad_attended,
+    )
+    grad_project = jnp.stack(grads, axis=2).reshape(query_count, 3 * features).astype(NARROW)
+    normed_grad = input_grad(grad_project, attn_in[1])
+    causal_in_grad = weight_grad(own_columns(normed_one), grad_project)
+    input_part, gain_one, bias_one = norm_back(query_rows, norm_gain[1], norm_bias[1], normed_grad)
+    grad_q_zero = grad_q_one + input_part
+    query_total = reduce_rep(
+        jnp.concatenate((causal_in_grad, causal_out_grad, cross_out_grad), axis=1)
+    )
+    norms = jnp.stack(
+        (
+            gain_zero,
+            gain_one * leader,
+            gain_two,
+            gain_three,
+            gain_four * leader,
+            gain_five,
+            bias_zero,
+            bias_one * leader,
+            bias_two,
+            bias_three,
+            bias_four * leader,
+            bias_five,
+        )
+    )
+    norms = own_columns(lax.psum(norms, ("blk", "rep")))
+    wide = 3 * features
+    grad_attn_in = jnp.stack(
+        (
+            window_total[:, :wide],
+            query_total[:, :wide],
+            jnp.concatenate((shared_total[:, :features], cross_total[:, : 2 * features]), axis=1),
+            jnp.concatenate(
+                (cross_total[:, 2 * features : wide], shared_total[:, features:]), axis=1
+            ),
+        )
+    )
+    grad_attn_out = jnp.stack(
+        (
+            window_total[:, wide:],
+            query_total[:, wide : wide + features],
+            query_total[:, wide + features :],
+            cross_total[:, wide:],
+        )
+    )
     return (
         patch_three.astype(NARROW)[None],
-        query_slice.astype(NARROW)[None],
+        own_columns(query_three).astype(NARROW)[None],
         grad_x_zero[None],
-        query_grad_slice[None],
-        stacked[4],
-        stacked[5],
-        stacked[0],
-        stacked[1],
-        stacked[2],
-        stacked[3],
+        own_columns(grad_q_zero)[None],
+        norms[:6],
+        norms[6:],
+        grad_attn_in.astype(SINGLE),
+        grad_attn_out.astype(SINGLE),
+        jnp.stack((patch_up_grad, query_up_grad)).astype(SINGLE),
+        jnp.stack((patch_down_grad, query_down_grad)).astype(SINGLE),
     )
 
 

time: 2320 us -> 1070 us (0.46)
  waiting for transfers between devices: 1420 us -> 240 us
  other arithmetic: 226 us -> 148 us
  starting transfers between devices: 2.16 us -> 54.8 us
  matrix products: 425 us -> 379 us
    reduce_scatter x6 -> x0, waiting for transfers between devices: 1030 us -> none  [the longest x1 450 us: body(): lax.psum_scatter(stacked[0], 'blk', scatter_dimension=1, tiled=True)]
    ppermute x0 -> x62, waiting for transfers between devices: none -> 240 us  [swap(): return lax.ppermute(tensor, axis, [(i, i ^ 1 << bit) for i in range(count)])]
    all_gather x3 -> x0, waiting for transfers between devices: 188 us -> none  [the longest x1 158 us: merged(): lax.all_gather(part.astype(kind), axis)]
    unnamed x14 -> x0, waiting for transfers between devices: 107 us -> none
    psum x1 -> x0, waiting for transfers between devices: 89.4 us -> none  [body(): lax.psum(stacked[0].astype(jnp.bfloat16), 'rep').astype(jnp.float32)]
    ppermute x0 -> x62, starting transfers between devices: none -> 54.8 us  [swap(): return lax.ppermute(tensor, axis, [(i, i ^ 1 << bit) for i in range(count)])]
    another operation x6, other arithmetic: 39.1 us -> 0.3 us  [the longest x4 0.23 us: unfold(): jnp.stack((tensor, arrived), axis=dim)]
    psum x1, blocking collectives: 5.65 us -> 40.8 us  [body(): norms = own_columns(lax.psum(norms, ('blk', 'rep')))]
  transfers between devices with their start and end apart: 12 -> 62, of which waited for: 10 -> 33; matrix products, arithmetic and copies ran while one was open for 23% -> 46% of each run, Pallas kernels for 0% -> 0%
where the time goes in v1:
time: 1070 us; the launch traced here: 1060 us
  matrix products  379 us (35%)
  waiting for transfers between devices  240 us (22%)
  local copies, waits for them, and re-layouts  162 us (15%)
  other arithmetic  148 us (14%)
  blocking collectives  72.5 us (7%)
  starting transfers between devices  54.8 us (5%)
    ppermute x62, waiting for transfers between devices, swap(): return lax.ppermute(tensor, axis, [(i, i ^ 1 << bit) for i in range(count)])  240 us
    dot_general x14, matrix products, matmul(): return jnp.dot(former, latter, preferred_element_type=SINGLE)  91.4 us
    dot_general x14, matrix products, input_grad(): lax.dot_general(upstream, weight, (((1,), (1,)), ((), ())), preferred_ele...  64.1 us
    ppermute x62, starting transfers between devices, swap(): return lax.ppermute(tensor, axis, [(i, i ^ 1 << bit) for i in range(count)])  54.8 us
    convert_element_type x3, other arithmetic, attend_backward(): rounded = grad_scores.astype(NARROW)  43.6 us
    dot_general x3, matrix products, attend_backward(): jnp.einsum('brhe,bkhe->bhrk', upstream, values_h, preferred_element_type=...  41.1 us
    psum x1, blocking collectives, body(): norms = own_columns(lax.psum(norms, ('blk', 'rep')))  40.8 us
    unnamed x398, local copies, waits for them, and re-layouts  36.5 us
  transfers between devices with their start and end apart: 62, of which 33 were waited for; matrix products, arithmetic and copies ran while one was open for 46% of the time, Pallas kernels for 0%

profile of v1, /device:TPU:0, one launch (start us, length us, event | category | flops | bytes accessed | tf_op | source)
XLA Modules:
  0.0 1061.3 jit_solution(9855616548990885716)
XLA Ops:
  5.7 6.5 slice_bitcast_fusion
  13.5 5.6 convolution_convert_fusion.5
  19.0 4.5 copy.199
  23.6 7.1 reshape.1727
  30.6 4.6 fusion.287
  52.8 7.0 convolution_convert_fusion
  59.8 6.8 copy.205
  71.1 18.5 %fusion.292 = (f32[12,800]{1,0:T(8,128)S(1)}, f32[12,800,800]{1,2,0:T(8,128)}) fusion(bf16[1,800,3,12,64]{1,4,3,2,0:T(8,128)(2,1)} %bitcast.725, pred[800,800]{0,1:T(8,128)(4,1)S(1)} %iota_compare_fusion.1), kind=kOutput, calls=%fused_computation.609 | convolution fusion | flops 1006070400 | bytes 34150912 | tf_op jit(solution)/shard_map/brhe,bkhe->bhrk/dot_general | solution.py:133
  89.6 16.2 %exponential_reduce_fusion = (f32[12,800]{1,0:T(8,128)}, f32[12,800]{1,0:T(8,128)S(1)}) fusion(f32[12,800,800]{1,2,0:T(8,128)} %get-tuple-element.132, f32[12,800]{1,0:T(8,128)S(1)} %is-finite_select_fusion.1, f32[12,800]{1,0:T(8,128)S(1)} %get-tuple-element.131), kind=kLoop, calls=%fused_computation.3 | loop fusion | flops 30700800 | bytes 30873600 | tf_op jit(solution)/shard_map/reduce_sum | solution.py:144
  105.9 14.6 %fusion.107 = bf16[12,64,800]{2,1,0:T(8,128)(2,1)S(1)} fusion(f32[12,800,800]{1,2,0:T(8,128)} %get-tuple-element.132, f32[12,800]{1,0:T(8,128)S(1)} %get-tuple-element.51, f32[12,800]{1,0:T(8,128)S(1)} %get-tuple-element.131, bf16[1,800,3,12,64]{1,4,3,2,0:T(8,128)(2,1)} %bitcast.726), kind=kOutput, calls=%fused_computation.220 | convolution fusion | flops 1006694400 | bytes 37088256 | tf_op jit(solution)/shard_map/bhrk,bkhe->brhe/dot_general | solution.py:141
  134.9 5.3 fusion.295
  140.2 6.9 exponential_reduce_fusion.1
  147.2 3.9 fusion.138
  153.9 19.9 %multiply_convert_fusion.3 = (bf16[512,3072]{1,0:T(8,128)(2,1)S(1)}, f32[512,3072]{1,0:T(8,128)}, f32[512,3072]{1,0:T(8,128)}) fusion(bf16[2,768,3072]{2,1,0:T(8,128)(2,1)} %param.20, f32[512,768]{1,0:T(8,128)S(1)} %get-tuple-element.140, f32[768]{0:T(1024)S(1)} %get-tuple-element.86, f32[768]{0:T(1024)S(1)} %get-tuple-element.159, f32[512]{0:T(512)S(1)} %fusion.260, ...), kind=kOutput, calls=%fused_computation.51 | convolution fusion | flops 2520121344 | bytes 22030336 | tf_op jit(solution)/shard_map/dot_general | solution.py:112
  180.5 7.6 add_convert_fusion.1
  194.9 6.2 multiply_reduce_fusion.10
  206.5 10.9 %fusion.104 = bf16[12,64,800]{2,1,0:T(8,128)(2,1)} fusion(bf16[512,12,64]{0,2,1:T(8,128)(2,1)S(1)} %bitcast.760, f32[12,512,800]{1,2,0:T(8,128)} %copy-done, f32[12,512]{1,0:T(8,128)S(1)} %log_add_fusion.2), kind=kOutput, calls=%fused_computation.219 | convolution fusion | flops 639590400 | bytes 21700608 | tf_op jit(solution)/shard_map/bhrk,brhe->bkhe/dot_general | solution.py:160
  217.4 12.8 %multiply_reduce_fusion.1 = (f32[12,512]{1,0:T(8,128)S(1)}, f32[12,512,800]{1,2,0:T(8,128)}) fusion(f32[12,512,800]{1,2,0:T(8,128)} %copy-done, f32[12,512]{1,0:T(8,128)S(1)} %log_add_fusion.2, bf16[512,12,64]{0,2,1:T(8,128)(2,1)S(1)} %bitcast.761, bf16[800,12,64]{0,2,1:T(8,128)(2,1)S(1)} %bitcast.763), kind=kOutput, calls=%fused_computation.11 | convolution fusion | flops 643885056 | bytes 41385984 | tf_op jit(solution)/shard_map/brhe,bkhe->bhrk/dot_general | solution.py:149
  232.6 14.0 %multiply_convert_fusion.1 = bf16[12,512,800]{1,2,0:T(8,128)(2,1)S(1)} fusion(f32[12,512,800]{1,2,0:T(8,128)} %get-tuple-element.150, f32[12,512,800]{1,2,0:T(8,128)} %copy-done, f32[12,512]{1,0:T(8,128)S(1)} %get-tuple-element.149, f32[12,512]{1,0:T(8,128)S(1)} %log_add_fusion.2), kind=kLoop, calls=%fused_computation.10 | loop fusion | flops 19660800 | bytes 49201152 | tf_op jit(solution)/shard_map/convert_element_type | solution.py:153
  259.3 4.3 convolution_convert_fusion.8
  273.1 5.1 fusion.3
  278.2 5.0 fusion.9
  285.0 31.6 %all-gather.1 = f32[8,800,12]{1,2,0:T(8,128)S(1)} all-gather(f32[1,800,12]{1,2,0:T(8,128)S(1)} %fusion.255), channel_id=2, replica_groups=mesh['blk'=8,'rep'=4] {'blk'}, dimensions={0}, use_global_device_ids=true | all-gather | bytes 345600 | tf_op jit(solution)/shard_map/all_gather | solution.py:307
  316.9 9.7 fusion.73
  333.7 6.2 fusion.140
  360.8 3.9 collective-permute-start.2
  366.5 4.6 collective-permute-done.2
  373.4 9.6 collective-permute-done.3
  392.2 7.4 collective-permute-done.11
  411.1 26.2 %multiply_convert_fusion.2 = (bf16[800,3072]{1,0:T(8,128)(2,1)}, f32[800,3072]{1,0:T(8,128)}, f32[800,3072]{1,0:T(8,128)}) fusion(bf16[800,768]{1,0:T(8,128)(2,1)S(1)} %add_convert_fusion.2, bf16[2,768,3072]{2,1,0:T(8,128)(2,1)S(1)} %bitcast.867), kind=kOutput, calls=%fused_computation.32 | convolution fusion | flops 3934617600 | bytes 30523392 | tf_op jit(solution)/shard_map/dot_general | solution.py:112
  437.3 11.5 %add_convert_fusion = bf16[800,3072]{1,0:T(8,128)(2,1)S(1)} fusion(f32[800,3072]{1,0:T(8,128)} %get-tuple-element.100, f32[800,3072]{1,0:T(8,128)} %get-tuple-element.146, bf16[2,3072,768]{2,1,0:T(8,128)(2,1)} %param.21, bf16[1,800,768]{2,1,0:T(8,128)(2,1)S(1)} %copy-done.65), kind=kOutput, calls=%fused_computation.30 | convolution fusion | flops 3809280000 | bytes 30523392 | tf_op jit(solution)/shard_map/dot_general | solution.py:122
  451.1 8.1 multiply_reduce_fusion.4
  467.8 3.9 fusion.124
  478.3 8.9 convolution_convert_fusion.17
  487.2 13.3 %subtract_convert_fusion = bf16[12,800,512]{2,1,0:T(8,128)(2,1)} fusion(f32[12,800,512]{2,1,0:T(8,128)} %copy-done.5, f32[12,800]{1,0:T(8,128)S(1)} %get-tuple-element.95, f32[12,800]{1,0:T(8,128)S(1)} %copy-done.90, pred[512]{0:T(512)(128)(4,1)S(1)} %copy-done.173, bf16[512,12,64]{0,2,1:T(8,128)(2,1)S(1)} %bitcast.831, f32[12,800,64]{1,2,0:T(8,128)S(1)} %bitcast.743, ...), kind=kOutput, calls=%fused_computation.9 | convolution fusion | flops 664780800 | bytes 32850944 | tf_op jit(solution)/shard_map/hqe,khe->hqk/dot_general | solution.py:397
  500.5 6.0 multiply_convert_fusion.10
  507.2 4.2 multiply_convert_fusion.8
  525.9 4.4 copy.230
  542.7 4.0 fusion.31
  565.3 6.9 copy.233
  572.2 7.6 convert_element_type.798
  579.9 5.1 fusion.277
  612.6 26.6 %collective-permute-done.48 = bf16[24,3072]{1,0:T(8,128)(2,1)S(1)} collective-permute-done((bf16[24,3072]{1,0:T(8,128)(2,1)S(1)}, bf16[24,3072]{1,0:T(8,128)(2,1)S(1)}, u32[]{:S(2)}, u32[]{:S(2)}) %collective-permute-start.48) | collective-permute-done | bytes 147488 | tf_op jit(solution)/shard_map/ppermute | solution.py:24
  656.3 9.9 collective-permute-done.7
  670.1 6.8 collective-permute-done.8
  683.9 7.6 collective-permute-done.12
  696.6 5.5 collective-permute-done.13
  702.8 9.2 collective-permute-done.53
  712.7 12.0 %collective-permute-done.42 = bf16[2,2,24,3072]{3,2,0,1:T(8,128)(2,1)S(1)} collective-permute-done((bf16[2,2,24,3072]{3,2,0,1:T(8,128)(2,1)S(1)}, bf16[2,2,24,3072]{3,2,0,1:T(8,128)(2,1)S(1)}, u32[]{:S(2)}, u32[]{:S(2)}) %collective-permute-start.42) | collective-permute-done | bytes 589856 | tf_op jit(solution)/shard_map/ppermute | solution.py:24
  726.2 6.7 collective-permute-done.54
  734.9 6.3 collective-permute-done.43
  755.9 15.1 %fusion.101 = bf16[1,800,1,12,64]{1,4,3,2,0:T(8,128)(2,1)} fusion(bf16[800,12,64]{0,2,1:T(8,128)(2,1)} %bitcast.732, f32[12,800,800]{1,2,0:T(8,128)} %get-tuple-element.132, f32[12,800]{1,0:T(8,128)} %log_add_fusion.1), kind=kOutput, calls=%fused_computation.211 | convolution fusion | flops 998400000 | bytes 33216000 | tf_op jit(solution)/shard_map/bhrk,brhe->bkhe/dot_general | solution.py:160
  771.0 27.1 %multiply_reduce_fusion = (f32[12,800]{1,0:T(8,128)}, f32[12,800,800]{1,2,0:T(8,128)}) fusion(f32[12,800,800]{1,2,0:T(8,128)} %get-tuple-element.132, f32[12,800]{1,0:T(8,128)} %log_add_fusion.1, bf16[800,12,64]{0,2,1:T(8,128)(2,1)} %bitcast.733, bf16[1,800,3,12,64]{1,4,3,2,0:T(8,128)(2,1)} %bitcast.727), kind=kOutput, calls=%fused_computation.1 | convolution fusion | flops 1006070400 | bytes 67974656 | tf_op jit(solution)/shard_map/brhe,bkhe->bhrk/dot_general | solution.py:149
  798.1 28.6 %multiply_convert_fusion = bf16[12,800,800]{1,2,0:T(8,128)(2,1)} fusion(f32[12,800,800]{1,2,0:T(8,128)} %get-tuple-element.157, f32[12,800,800]{1,2,0:T(8,128)} %get-tuple-element.132, f32[12,800]{1,0:T(8,128)} %get-tuple-element.156, f32[12,800]{1,0:T(8,128)} %log_add_fusion.1), kind=kLoop, calls=%fused_computation | loop fusion | flops 30720000 | bytes 76876800 | tf_op jit(solution)/shard_map/convert_element_type | solution.py:153
  826.7 12.8 %multiply_bitcast_fusion = bf16[1,800,1,12,64]{1,4,3,2,0:T(8,128)(2,1)} fusion(bf16[12,800,800]{1,2,0:T(8,128)(2,1)} %multiply_convert_fusion, bf16[1,800,3,12,64]{1,4,3,2,0:T(8,128)(2,1)} %bitcast.728), kind=kOutput, calls=%fused_computation.148 | convolution fusion | flops 984268800 | bytes 19808256 | tf_op jit(solution)/shard_map/bhrk,brhe->bkhe/dot_general | solution.py:158
  839.5 9.7 multiply_bitcast_fusion.1
  850.5 6.3 multiply_reduce_fusion.5
  869.6 40.8 %psum.7 = f32[12,768]{1,0:T(8,128)} all-reduce(f32[12,768]{1,0:T(8,128)} %stack.503), channel_id=1, replica_groups=mesh['blk'=8,'rep'=4] {'blk','rep'}, use_global_device_ids=true, to_apply=%region_55.56 | all-reduce | flops 9216 | bytes 73728 | tf_op jit(solution)/shard_map/psum | solution.py:506
  932.2 45.2 %collective-permute-done.23 = bf16[24,3840]{1,0:T(8,128)(2,1)S(1)} collective-permute-done((bf16[24,3840]{1,0:T(8,128)(2,1)S(1)}, bf16[24,3840]{1,0:T(8,128)(2,1)S(1)}, u32[]{:S(2)}, u32[]{:S(2)}) %collective-permute-start.23) | collective-permute-done | bytes 184352 | tf_op jit(solution)/shard_map/ppermute | solution.py:24
  989.1 13.5 %collective-permute-done.27 = bf16[8,24,2304]{2,1,0:T(8,128)(2,1)S(1)} collective-permute-done((bf16[8,24,2304]{2,1,0:T(8,128)(2,1)S(1)}, bf16[8,24,2304]{2,1,0:T(8,128)(2,1)S(1)}, u32[]{:S(2)}, u32[]{:S(2)}) %collective-permute-start.27) | collective-permute-done | bytes 884768 | tf_op jit(solution)/shard_map/ppermute | solution.py:24
  1004.6 10.9 %collective-permute-done.17 = bf16[2,2,24,3072]{3,2,0,1:T(8,128)(2,1)S(1)} collective-permute-done((bf16[2,2,24,3072]{3,2,0,1:T(8,128)(2,1)S(1)}, bf16[2,2,24,3072]{3,2,0,1:T(8,128)(2,1)S(1)}, u32[]{:S(2)}, u32[]{:S(2)}) %collective-permute-start.17) | collective-permute-done | bytes 589856 | tf_op jit(solution)/shard_map/ppermute | solution.py:24
  1015.7 8.4 collective-permute-done.28
  1027.4 6.7 collective-permute-done.29
  1037.3 7.7 collective-permute-done.30
  (808 shorter events, 356.3 us)
Async XLA Ops:
  12.9 111.2 %copy-start.123 = (f32[768]{0:T(1024)}, f32[768]{0:T(1024)S(1)}, u32[]{:S(2)}) copy-start(f32[768]{0:T(1024)S(1)} %get-tuple-element.162) | copy-start | bytes 9220
  52.4 98.7 %copy-start.11 = (f32[512,768]{1,0:T(8,128)}, f32[512,768]{1,0:T(8,128)S(1)}, u32[]{:S(2)}) copy-start(f32[512,768]{1,0:T(8,128)S(1)} %get-tuple-element.136) | copy-start | bytes 4718596
  180.0 420.6 %collective-permute-start.51 = (bf16[8,2,96,768]{3,2,0,1:T(8,128)(2,1)}, bf16[8,2,96,768]{3,2,0,1:T(8,128)(2,1)}, u32[]{:S(2)}, u32[]{:S(2)}) collective-permute-start(bf16[8,2,96,768]{3,2,0,1:T(8,128)(2,1)} %bitcast.719), channel_id=1, source_target_pairs={{0,1},{1,0},{2,3},{3,2},{4,5},{5,4},{6,7},{7,6},{8,9},{9,8},{10,11... | collective-permute-start | bytes 7077896 | tf_op jit(solution)/shard_map/ppermute | solution.py:24
  194.9 408.7 %collective-permute-start.40 = (bf16[8,2,24,3072]{3,2,0,1:T(8,128)(2,1)}, bf16[8,2,24,3072]{3,2,0,1:T(8,128)(2,1)}, u32[]{:S(2)}, u32[]{:S(2)}) collective-permute-start(bf16[8,2,24,3072]{3,2,0,1:T(8,128)(2,1)} %bitcast.720), channel_id=1, source_target_pairs={{0,1},{1,0},{2,3},{3,2},{4,5},{5,4},{6,7},{7,6},{8,9},{9,8},{10,11... | collective-permute-start | bytes 7077896 | tf_op jit(solution)/shard_map/ppermute | solution.py:24
  256.4 108.3 %collective-permute-start.9 = (bf16[2,2,104,1536]{3,2,1,0:T(8,128)(2,1)}, bf16[2,2,104,1536]{3,2,1,0:T(8,128)(2,1)}, u32[]{:S(2)}, u32[]{:S(2)}) collective-permute-start(bf16[2,2,104,1536]{3,2,1,0:T(8,128)(2,1)} %dynamic-slice_bitcast_fusion.1), channel_id=1, source_target_pairs={{0,4},{4,0},{8,12},{12,8},{16,20},{20,16},{24,28},{28,24},{1,5},{5... | collective-permute-start | bytes 3833864 | tf_op jit(solution)/shard_map/ppermute | solution.py:24
  330.7 15.8 %collective-permute-start = (bf16[2,2,104,768]{3,2,0,1:T(8,128)(2,1)}, bf16[2,2,104,768]{3,2,0,1:T(8,128)(2,1)}, u32[]{:S(2)}, u32[]{:S(2)}) collective-permute-start(bf16[2,2,104,768]{3,2,0,1:T(8,128)(2,1)} %bitcast.721), channel_id=1, source_target_pairs={{0,4},{4,0},{8,12},{12,8},{16,20},{20,16},{24,28},{28,24},{1,5},{5... | collective-permute-start | bytes 1916936 | tf_op jit(solution)/shard_map/ppermute | solution.py:24
  349.9 9.8 collective-permute-start.1
  360.8 10.3 collective-permute-start.2
  366.4 21.6 %collective-permute-start.10 = (bf16[2,104,1536]{2,1,0:T(8,128)(2,1)S(1)}, bf16[2,104,1536]{2,1,0:T(8,128)(2,1)S(1)}, u32[]{:S(2)}, u32[]{:S(2)}) collective-permute-start(bf16[2,104,1536]{2,1,0:T(8,128)(2,1)S(1)} %fusion.186), channel_id=1, source_target_pairs={{0,8},{4,12},{8,0},{12,4},{16,24},{20,28},{24,16},{28,20},{1,9},{5... | collective-permute-start | bytes 1916936 | tf_op jit(solution)/shard_map/ppermute | solution.py:24
  371.2 11.8 %collective-permute-start.3 = (bf16[104,768]{1,0:T(8,128)(2,1)S(1)}, bf16[104,768]{1,0:T(8,128)(2,1)S(1)}, u32[]{:S(2)}, u32[]{:S(2)}) collective-permute-start(bf16[104,768]{1,0:T(8,128)(2,1)S(1)} %fusion.210), channel_id=1, source_target_pairs={{0,16},{4,20},{8,24},{12,28},{16,0},{20,4},{24,8},{28,12},{1,17},{... | collective-permute-start | bytes 479240 | tf_op jit(solution)/shard_map/ppermute | solution.py:24
  383.0 8.5 collective-permute-start.4
  388.3 11.4 %collective-permute-start.11 = (bf16[104,1536]{1,0:T(8,128)(2,1)S(1)}, bf16[104,1536]{1,0:T(8,128)(2,1)S(1)}, u32[]{:S(2)}, u32[]{:S(2)}) collective-permute-start(bf16[104,1536]{1,0:T(8,128)(2,1)S(1)} %fusion.208), channel_id=1, source_target_pairs={{0,16},{4,20},{8,24},{12,28},{16,0},{20,4},{24,8},{28,12},{1,17},{... | collective-permute-start | bytes 958472 | tf_op jit(solution)/shard_map/ppermute | solution.py:24
  391.6 12.6 %collective-permute-start.5 = (bf16[2,2,104,768]{3,2,1,0:T(8,128)(2,1)S(1)}, bf16[2,2,104,768]{3,2,1,0:T(8,128)(2,1)S(1)}, u32[]{:S(2)}, u32[]{:S(2)}) collective-permute-start(bf16[2,2,104,768]{3,2,1,0:T(8,128)(2,1)S(1)} %maximum_select_fusion.4), channel_id=1, source_target_pairs={{0,4},{4,0},{8,12},{12,8},{16,20},{20,16},{24,28},{28,24},{1,5},{5... | collective-permute-start | bytes 1916936 | tf_op jit(solution)/shard_map/ppermute | solution.py:24
  542.6 65.3 %collective-permute-start.47 = (bf16[2,24,3072]{2,1,0:T(8,128)(2,1)S(1)}, bf16[2,24,3072]{2,1,0:T(8,128)(2,1)}, u32[]{:S(2)}, u32[]{:S(2)}) collective-permute-start(bf16[2,24,3072]{2,1,0:T(8,128)(2,1)S(1)} %fusion.214), channel_id=1, source_target_pairs={{0,1},{1,0},{2,3},{3,2},{4,5},{5,4},{6,7},{7,6},{8,9},{9,8},{10,11... | collective-permute-start | bytes 884744 | tf_op jit(solution)/shard_map/ppermute | solution.py:24
  553.0 57.5 %collective-permute-start.58 = (bf16[2,96,768]{2,1,0:T(8,128)(2,1)}, bf16[2,96,768]{2,1,0:T(8,128)(2,1)}, u32[]{:S(2)}, u32[]{:S(2)}) collective-permute-start(bf16[2,96,768]{2,1,0:T(8,128)(2,1)} %fusion.216), channel_id=1, source_target_pairs={{0,1},{1,0},{2,3},{3,2},{4,5},{5,4},{6,7},{7,6},{8,9},{9,8},{10,11... | collective-permute-start | bytes 884744 | tf_op jit(solution)/shard_map/ppermute | solution.py:24
  555.3 99.6 %collective-permute-start.6 = (bf16[2,2,104,768]{3,2,1,0:T(8,128)(2,1)}, bf16[2,2,104,768]{3,2,1,0:T(8,128)(2,1)}, u32[]{:S(2)}, u32[]{:S(2)}) collective-permute-start(bf16[2,2,104,768]{3,2,1,0:T(8,128)(2,1)} %dynamic-slice_bitcast_fusion.2), channel_id=1, source_target_pairs={{0,4},{4,0},{8,12},{12,8},{16,20},{20,16},{24,28},{28,24},{1,5},{5... | collective-permute-start | bytes 1916936 | tf_op jit(solution)/shard_map/ppermute | solution.py:24
  600.6 315.7 %collective-permute-start.33 = (bf16[8,2,24,3072]{3,2,0,1:T(8,128)(2,1)}, bf16[8,2,24,3072]{3,2,0,1:T(8,128)(2,1)}, u32[]{:S(2)}, u32[]{:S(2)}) collective-permute-start(bf16[8,2,24,3072]{3,2,0,1:T(8,128)(2,1)} %bitcast.718), channel_id=1, source_target_pairs={{0,1},{1,0},{2,3},{3,2},{4,5},{5,4},{6,7},{7,6},{8,9},{9,8},{10,11... | collective-permute-start | bytes 7077896 | tf_op jit(solution)/shard_map/ppermute | solution.py:24
  603.6 316.4 %collective-permute-start.15 = (bf16[8,2,24,3072]{3,2,1,0:T(8,128)(2,1)}, bf16[8,2,24,3072]{3,2,1,0:T(8,128)(2,1)}, u32[]{:S(2)}, u32[]{:S(2)}) collective-permute-start(bf16[8,2,24,3072]{3,2,1,0:T(8,128)(2,1)} %fusion.85), channel_id=1, source_target_pairs={{0,1},{1,0},{2,3},{3,2},{4,5},{5,4},{6,7},{7,6},{8,9},{9,8},{10,11... | collective-permute-start | bytes 7077896 | tf_op jit(solution)/shard_map/ppermute | solution.py:24
  607.8 83.8 %collective-permute-start.52 = (bf16[8,96,768]{2,1,0:T(8,128)(2,1)S(1)}, bf16[8,96,768]{2,1,0:T(8,128)(2,1)S(1)}, u32[]{:S(2)}, u32[]{:S(2)}) collective-permute-start(bf16[8,96,768]{2,1,0:T(8,128)(2,1)S(1)} %fusion.158), channel_id=1, source_target_pairs={{0,2},{1,3},{2,0},{3,1},{4,6},{5,7},{6,4},{7,5},{8,10},{9,11},{10,... | collective-permute-start | bytes 3538952 | tf_op jit(solution)/shard_map/ppermute | solution.py:24
  610.5 28.8 %collective-permute-start.48 = (bf16[24,3072]{1,0:T(8,128)(2,1)S(1)}, bf16[24,3072]{1,0:T(8,128)(2,1)S(1)}, u32[]{:S(2)}, u32[]{:S(2)}) collective-permute-start(bf16[24,3072]{1,0:T(8,128)(2,1)S(1)} %fusion.243), channel_id=1, source_target_pairs={{0,2},{1,3},{2,0},{3,1},{4,6},{5,7},{6,4},{7,5},{8,10},{9,11},{10,... | collective-permute-start | bytes 442376 | tf_op jit(solution)/shard_map/ppermute | solution.py:24
  639.2 5.2 collective-permute-start.59
  644.5 5.1 collective-permute-start.49
  649.6 5.1 collective-permute-start.60
  654.8 11.5 %collective-permute-start.50 = (bf16[2,24,3072]{2,1,0:T(8,128)(2,1)S(1)}, bf16[2,24,3072]{2,1,0:T(8,128)(2,1)S(1)}, u32[]{:S(2)}, u32[]{:S(2)}) collective-permute-start(bf16[2,24,3072]{2,1,0:T(8,128)(2,1)S(1)} %maximum_select_fusion.27), channel_id=1, source_target_pairs={{0,1},{1,0},{2,3},{3,2},{4,5},{5,4},{6,7},{7,6},{8,9},{9,8},{10,11... | collective-permute-start | bytes 884744 | tf_op jit(solution)/shard_map/ppermute | solution.py:24
  656.1 10.0 collective-permute-start.7
  666.1 1.6 collective-permute-start.61
  666.3 10.6 %collective-permute-start.8 = (bf16[104,768]{1,0:T(8,128)(2,1)S(1)}, bf16[104,768]{1,0:T(8,128)(2,1)S(1)}, u32[]{:S(2)}, u32[]{:S(2)}) collective-permute-start(bf16[104,768]{1,0:T(8,128)(2,1)S(1)} %fusion.239), channel_id=1, source_target_pairs={{0,16},{4,20},{8,24},{12,28},{16,0},{20,4},{24,8},{28,12},{1,17},{... | collective-permute-start | bytes 479240 | tf_op jit(solution)/shard_map/ppermute | solution.py:24
  667.7 28.0 %collective-permute-start.41 = (bf16[8,24,3072]{2,1,0:T(8,128)(2,1)S(1)}, bf16[8,24,3072]{2,1,0:T(8,128)(2,1)S(1)}, u32[]{:S(2)}, u32[]{:S(2)}) collective-permute-start(bf16[8,24,3072]{2,1,0:T(8,128)(2,1)S(1)} %fusion.157), channel_id=1, source_target_pairs={{0,2},{1,3},{2,0},{3,1},{4,6},{5,7},{6,4},{7,5},{8,10},{9,11},{10,... | collective-permute-start | bytes 3538952 | tf_op jit(solution)/shard_map/ppermute | solution.py:24
  682.2 9.3 collective-permute-start.12
  691.5 287.8 %collective-permute-start.26 = (bf16[8,2,24,2304]{3,2,1,0:T(8,128)(2,1)}, bf16[8,2,24,2304]{3,2,1,0:T(8,128)(2,1)}, u32[]{:S(2)}, u32[]{:S(2)}) collective-permute-start(bf16[8,2,24,2304]{3,2,1,0:T(8,128)(2,1)} %dynamic-slice_bitcast_fusion), channel_id=1, source_target_pairs={{0,1},{1,0},{2,3},{3,2},{4,5},{5,4},{6,7},{7,6},{8,9},{9,8},{10,11... | collective-permute-start | bytes 5308424 | tf_op jit(solution)/shard_map/ppermute | solution.py:24
  691.7 10.4 collective-permute-start.13
  695.7 16.3 %collective-permute-start.53 = (bf16[2,2,96,768]{3,2,0,1:T(8,128)(2,1)S(1)}, bf16[2,2,96,768]{3,2,0,1:T(8,128)(2,1)S(1)}, u32[]{:S(2)}, u32[]{:S(2)}) collective-permute-start(bf16[2,2,96,768]{3,2,0,1:T(8,128)(2,1)S(1)} %fusion.194), channel_id=1, source_target_pairs={{0,4},{4,0},{8,12},{12,8},{16,20},{20,16},{24,28},{28,24},{1,5},{5... | collective-permute-start | bytes 1769480 | tf_op jit(solution)/shard_map/ppermute | solution.py:24
  702.1 22.6 %collective-permute-start.42 = (bf16[2,2,24,3072]{3,2,0,1:T(8,128)(2,1)S(1)}, bf16[2,2,24,3072]{3,2,0,1:T(8,128)(2,1)S(1)}, u32[]{:S(2)}, u32[]{:S(2)}) collective-permute-start(bf16[2,2,24,3072]{3,2,0,1:T(8,128)(2,1)S(1)} %fusion.193), channel_id=1, source_target_pairs={{0,4},{4,0},{8,12},{12,8},{16,20},{20,16},{24,28},{28,24},{1,5},{5... | collective-permute-start | bytes 1769480 | tf_op jit(solution)/shard_map/ppermute | solution.py:24
  712.0 33.0 %collective-permute-start.14 = (bf16[2,2,104,768]{3,2,1,0:T(8,128)(2,1)S(1)}, bf16[2,2,104,768]{3,2,1,0:T(8,128)(2,1)S(1)}, u32[]{:S(2)}, u32[]{:S(2)}) collective-permute-start(bf16[2,2,104,768]{3,2,1,0:T(8,128)(2,1)S(1)} %maximum_select_fusion.6), channel_id=1, source_target_pairs={{0,4},{4,0},{8,12},{12,8},{16,20},{20,16},{24,28},{28,24},{1,5},{5... | collective-permute-start | bytes 1916936 | tf_op jit(solution)/shard_map/ppermute | solution.py:24
  724.6 8.3 collective-permute-start.54
  732.9 8.3 collective-permute-start.43
  741.2 170.6 %collective-permute-start.55 = (bf16[96,768]{1,0:T(8,128)(2,1)}, bf16[96,768]{1,0:T(8,128)(2,1)}, u32[]{:S(2)}, u32[]{:S(2)}) collective-permute-start(bf16[96,768]{1,0:T(8,128)(2,1)} %fusion.244), channel_id=1, source_target_pairs={{0,16},{4,20},{8,24},{12,28},{16,0},{20,4},{24,8},{28,12},{1,17},{... | collective-permute-start | bytes 442376 | tf_op jit(solution)/shard_map/ppermute | solution.py:24
  745.0 167.9 %collective-permute-start.44 = (bf16[24,3072]{1,0:T(8,128)(2,1)}, bf16[24,3072]{1,0:T(8,128)(2,1)}, u32[]{:S(2)}, u32[]{:S(2)}) collective-permute-start(bf16[24,3072]{1,0:T(8,128)(2,1)} %fusion.242), channel_id=1, source_target_pairs={{0,16},{4,20},{8,24},{12,28},{16,0},{20,4},{24,8},{28,12},{1,17},{... | collective-permute-start | bytes 442376 | tf_op jit(solution)/shard_map/ppermute | solution.py:24
  911.8 14.2 %collective-permute-start.22 = (bf16[2,24,3840]{2,1,0:T(8,128)(2,1)}, bf16[2,24,3840]{2,1,0:T(8,128)(2,1)S(1)}, u32[]{:S(2)}, u32[]{:S(2)}) collective-permute-start(bf16[2,24,3840]{2,1,0:T(8,128)(2,1)} %fusion.204), channel_id=1, source_target_pairs={{0,1},{1,0},{2,3},{3,2},{4,5},{5,4},{6,7},{7,6},{8,9},{9,8},{10,11... | collective-permute-start | bytes 1105928 | tf_op jit(solution)/shard_map/ppermute | solution.py:24
  912.9 11.7 %collective-permute-start.56 = (bf16[96,768]{1,0:T(8,128)(2,1)S(1)}, bf16[96,768]{1,0:T(8,128)(2,1)S(1)}, u32[]{:S(2)}, u32[]{:S(2)}) collective-permute-start(bf16[96,768]{1,0:T(8,128)(2,1)S(1)} %fusion.218), channel_id=1, source_target_pairs={{0,2},{1,3},{2,0},{3,1},{4,6},{5,7},{6,4},{7,5},{8,10},{9,11},{10,... | collective-permute-start | bytes 442376 | tf_op jit(solution)/shard_map/ppermute | solution.py:24
  916.4 9.4 collective-permute-start.45
  920.0 66.2 %collective-permute-start.34 = (bf16[8,24,3072]{2,1,0:T(8,128)(2,1)S(1)}, bf16[8,24,3072]{2,1,0:T(8,128)(2,1)S(1)}, u32[]{:S(2)}, u32[]{:S(2)}) collective-permute-start(bf16[8,24,3072]{2,1,0:T(8,128)(2,1)S(1)} %fusion.156), channel_id=1, source_target_pairs={{0,2},{1,3},{2,0},{3,1},{4,6},{5,7},{6,4},{7,5},{8,10},{9,11},{10,... | collective-permute-start | bytes 3538952 | tf_op jit(solution)/shard_map/ppermute | solution.py:24
  924.7 63.4 %collective-permute-start.16 = (bf16[8,24,3072]{2,1,0:T(8,128)(2,1)S(1)}, bf16[8,24,3072]{2,1,0:T(8,128)(2,1)S(1)}, u32[]{:S(2)}, u32[]{:S(2)}) collective-permute-start(bf16[8,24,3072]{2,1,0:T(8,128)(2,1)S(1)} %fusion.155), channel_id=1, source_target_pairs={{0,2},{1,3},{2,0},{3,1},{4,6},{5,7},{6,4},{7,5},{8,10},{9,11},{10,... | collective-permute-start | bytes 3538952 | tf_op jit(solution)/shard_map/ppermute | solution.py:24
  925.8 4.8 collective-permute-start.57
  926.0 1.9 collective-permute-start.46
  927.9 49.6 %collective-permute-start.23 = (bf16[24,3840]{1,0:T(8,128)(2,1)S(1)}, bf16[24,3840]{1,0:T(8,128)(2,1)S(1)}, u32[]{:S(2)}, u32[]{:S(2)}) collective-permute-start(bf16[24,3840]{1,0:T(8,128)(2,1)S(1)} %fusion.236), channel_id=1, source_target_pairs={{0,2},{1,3},{2,0},{3,1},{4,6},{5,7},{6,4},{7,5},{8,10},{9,11},{10,... | collective-permute-start | bytes 552968 | tf_op jit(solution)/shard_map/ppermute | solution.py:24
  977.5 6.7 collective-permute-start.24
  981.3 21.2 %collective-permute-start.27 = (bf16[8,24,2304]{2,1,0:T(8,128)(2,1)S(1)}, bf16[8,24,2304]{2,1,0:T(8,128)(2,1)S(1)}, u32[]{:S(2)}, u32[]{:S(2)}) collective-permute-start(bf16[8,24,2304]{2,1,0:T(8,128)(2,1)S(1)} %fusion.180), channel_id=1, source_target_pairs={{0,2},{1,3},{2,0},{3,1},{4,6},{5,7},{6,4},{7,5},{8,10},{9,11},{10,... | collective-permute-start | bytes 2654216 | tf_op jit(solution)/shard_map/ppermute | solution.py:24
  984.3 1.8 collective-permute-start.25
  986.6 17.7 %collective-permute-start.35 = (bf16[2,2,24,3072]{3,2,1,0:T(8,128)(2,1)S(1)}, bf16[2,2,24,3072]{3,2,1,0:T(8,128)(2,1)S(1)}, u32[]{:S(2)}, u32[]{:S(2)}) collective-permute-start(bf16[2,2,24,3072]{3,2,1,0:T(8,128)(2,1)S(1)} %fusion.191), channel_id=1, source_target_pairs={{0,4},{4,0},{8,12},{12,8},{16,20},{20,16},{24,28},{28,24},{1,5},{5... | collective-permute-start | bytes 1769480 | tf_op jit(solution)/shard_map/ppermute | solution.py:24
  988.4 27.0 %collective-permute-start.17 = (bf16[2,2,24,3072]{3,2,0,1:T(8,128)(2,1)S(1)}, bf16[2,2,24,3072]{3,2,0,1:T(8,128)(2,1)S(1)}, u32[]{:S(2)}, u32[]{:S(2)}) collective-permute-start(bf16[2,2,24,3072]{3,2,0,1:T(8,128)(2,1)S(1)} %fusion.192), channel_id=1, source_target_pairs={{0,4},{4,0},{8,12},{12,8},{16,20},{20,16},{24,28},{28,24},{1,5},{5... | collective-permute-start | bytes 1769480 | tf_op jit(solution)/shard_map/ppermute | solution.py:24
  1002.8 21.3 %collective-permute-start.28 = (bf16[2,2,24,2304]{3,2,0,1:T(8,128)(2,1)S(1)}, bf16[2,2,24,2304]{3,2,0,1:T(8,128)(2,1)S(1)}, u32[]{:S(2)}, u32[]{:S(2)}) collective-permute-start(bf16[2,2,24,2304]{3,2,0,1:T(8,128)(2,1)S(1)} %fusion.198), channel_id=1, source_target_pairs={{0,4},{4,0},{8,12},{12,8},{16,20},{20,16},{24,28},{28,24},{1,5},{5... | collective-permute-start | bytes 1327112 | tf_op jit(solution)/shard_map/ppermute | solution.py:24
  1004.4 19.9 %collective-permute-start.36 = (bf16[2,24,3072]{2,1,0:T(8,128)(2,1)S(1)}, bf16[2,24,3072]{2,1,0:T(8,128)(2,1)S(1)}, u32[]{:S(2)}, u32[]{:S(2)}) collective-permute-start(bf16[2,24,3072]{2,1,0:T(8,128)(2,1)S(1)} %fusion.212), channel_id=1, source_target_pairs={{0,8},{4,12},{8,0},{12,4},{16,24},{20,28},{24,16},{28,20},{1,9},{5... | collective-permute-start | bytes 884744 | tf_op jit(solution)/shard_map/ppermute | solution.py:24
  1015.6 11.7 %collective-permute-start.18 = (bf16[2,24,3072]{2,1,0:T(8,128)(2,1)S(1)}, bf16[2,24,3072]{2,1,0:T(8,128)(2,1)S(1)}, u32[]{:S(2)}, u32[]{:S(2)}) collective-permute-start(bf16[2,24,3072]{2,1,0:T(8,128)(2,1)S(1)} %fusion.211), channel_id=1, source_target_pairs={{0,8},{4,12},{8,0},{12,4},{16,24},{20,28},{24,16},{28,20},{1,9},{5... | collective-permute-start | bytes 884744 | tf_op jit(solution)/shard_map/ppermute | solution.py:24
  1024.3 9.9 collective-permute-start.29
  1024.5 23.0 %collective-permute-start.37 = (bf16[24,3072]{1,0:T(8,128)(2,1)S(1)}, bf16[24,3072]{1,0:T(8,128)(2,1)S(1)}, u32[]{:S(2)}, u32[]{:S(2)}) collective-permute-start(bf16[24,3072]{1,0:T(8,128)(2,1)S(1)} %fusion.241), channel_id=1, source_target_pairs={{0,16},{4,20},{8,24},{12,28},{16,0},{20,4},{24,8},{28,12},{1,17},{... | collective-permute-start | bytes 442376 | tf_op jit(solution)/shard_map/ppermute | solution.py:24
  1034.2 10.8 %collective-permute-start.30 = (bf16[24,2304]{1,0:T(8,128)(2,1)S(1)}, bf16[24,2304]{1,0:T(8,128)(2,1)S(1)}, u32[]{:S(2)}, u32[]{:S(2)}) collective-permute-start(bf16[24,2304]{1,0:T(8,128)(2,1)S(1)} %fusion.246), channel_id=1, source_target_pairs={{0,16},{4,20},{8,24},{12,28},{16,0},{20,4},{24,8},{28,12},{1,17},{... | collective-permute-start | bytes 331784 | tf_op jit(solution)/shard_map/ppermute | solution.py:24
  1034.6 12.9 %collective-permute-start.19 = (bf16[24,3072]{1,0:T(8,128)(2,1)S(1)}, bf16[24,3072]{1,0:T(8,128)(2,1)S(1)}, u32[]{:S(2)}, u32[]{:S(2)}) collective-permute-start(bf16[24,3072]{1,0:T(8,128)(2,1)S(1)} %fusion.240), channel_id=1, source_target_pairs={{0,16},{4,20},{8,24},{12,28},{16,0},{20,4},{24,8},{28,12},{1,17},{... | collective-permute-start | bytes 442376 | tf_op jit(solution)/shard_map/ppermute | solution.py:24
  1045.0 6.3 collective-permute-start.31
  1047.5 6.8 collective-permute-start.38
  1047.6 8.2 collective-permute-start.20
  1051.3 4.7 collective-permute-start.32
  1054.3 1.9 collective-permute-start.39
  1055.9 1.6 collective-permute-start.21
  (195 other events, 1400.4 us)

commit v2 on v1

v2 whole, which is shorter than its diff:
```python
import functools
import math

import jax
import jax.numpy as jnp
from jax import lax
from jax.experimental import pallas as pl
from jax.experimental.pallas import tpu as pltpu
from jax.sharding import PartitionSpec as P

HEADS = 12
WIN = 64
EPSILON = 1e-05
MASKED = -1e30
NARROW = jnp.bfloat16
SINGLE = jnp.float32
EXACT = lax.Precision.HIGHEST
GROUP = 128
PAIR = 128
HEAD = 64
STRIP = 160
CHUNK = 768


def dot(former, latter, ahead, behind, precision=None):
    return lax.dot_general(
        former,
        latter,
        (((ahead,), (behind,)), ((), ())),
        preferred_element_type=SINGLE,
        precision=precision,
    )


def plain(former, latter):
    return dot(former, latter, 1, 0)


def right_t(former, latter):
    return dot(former, latter, 1, 1)


def left_t(former, latter):
    return dot(former, latter, 0, 0)


def loop(count, action):
    def step(index, nothing):
        action(index)
        return nothing

    lax.fori_loop(0, count, step, 0)


def at(index, size):
    return pl.ds(pl.multiple_of(index * size, size), size)


def iota(shape, dim):
    return lax.broadcasted_iota(jnp.int32, shape, dim)


def statistics(tensor):
    average = jnp.mean(tensor, axis=-1, keepdims=True)
    centred = tensor - average
    spread = jnp.mean(centred * centred, axis=-1, keepdims=True)
    return centred, lax.rsqrt(spread + EPSILON)


def norm(tensor, gain, bias):
    centred, inverse = statistics(tensor)
    return centred * inverse * gain + bias


def norm_back(tensor, gain, upstream):
    centred, inverse = statistics(tensor)
    scaled = centred * inverse
    inner = upstream * gain
    grad = inverse * (
        inner
        - jnp.mean(inner, axis=-1, keepdims=True)
        - scaled * jnp.mean(inner * scaled, axis=-1, keepdims=True)
    )
    return (
        grad,
        jnp.sum(upstream * scaled, axis=0, keepdims=True),
        jnp.sum(upstream, axis=0, keepdims=True),
    )


def gelu_both(tensor):
    size = jnp.abs(tensor)
    ratio = 1.0 / (1.0 + (0.3275911 * math.sqrt(0.5)) * size)
    series = ratio * (
        0.254829592
        + ratio * (-0.284496736 + ratio * (1.421413741 + ratio * (-1.453152027 + ratio * 1.061405429)))
    )
    bell = jnp.exp(-0.5 * (tensor * tensor))
    tail = 0.5 * series * bell
    below = jnp.where(tensor >= 0, 1.0 - tail, tail)
    return tensor * below, below + tensor * bell * (1.0 / math.sqrt(2.0 * math.pi))


def half(which, value=1.0):
    return jnp.where(iota((1, PAIR), 1) // HEAD == which, value, 0.0).astype(NARROW)


def lower_lanes():
    return iota((1, PAIR), 1) < HEAD


def attend(queries, keys, values, mask):
    outs, logs = [], []
    for which in range(2):
        scores = mask(right_t(queries * half(which, 1.0 / math.sqrt(HEAD)), keys))
        peak = jnp.max(scores, axis=-1, keepdims=True)
        weights = jnp.exp(scores - peak)
        total = jnp.sum(weights, axis=-1, keepdims=True)
        outs.append(plain(weights.astype(NARROW), values) * (1.0 / total))
        logs.append(peak + jnp.log(total))
    return jnp.where(lower_lanes(), outs[0], outs[1]), logs


def attend_back(queries, keys, values, upstream, logs, deltas, mask):
    scaled = queries * jnp.asarray(1.0 / math.sqrt(HEAD), NARROW)
    grads = []
    for which in range(2):
        lanes = half(which)
        scores = mask(right_t(keys * lanes, scaled))
        if logs is None:
            weights = jnp.exp(scores - jnp.max(scores, axis=0, keepdims=True))
            weights = weights * (1.0 / jnp.sum(weights, axis=0, keepdims=True))
        else:
            weights = jnp.exp(scores - logs[which])
        inner = right_t(values * lanes, upstream)
        slope = (weights * (inner - deltas[which])).astype(NARROW)
        grads.append(
            (
                left_t(slope, keys),
                plain(slope, scaled),
                plain(weights.astype(NARROW), upstream),
            )
        )
    return tuple(jnp.where(lower_lanes(), one, two) for one, two in zip(*grads))


def head_rows(tensor):
    features = tensor.shape[1]
    heads = 16
    chosen = jnp.where(
        iota((heads, features), 1) // HEAD == iota((heads, features), 0), 1.0, 0.0
    ).astype(SINGLE)
    return dot(chosen, tensor, 1, 1, EXACT)


def turn(columns):
    same = jnp.where(iota((16, columns.shape[1]), 0) == iota((16, columns.shape[1]), 1), 1.0, 0.0)
    return dot(same.astype(SINGLE), columns, 1, 1, EXACT)


def row_pair(ref, pair, span):
    tensor = ref[:, span]
    index = iota(tensor.shape, 0)
    return [
        jnp.sum(jnp.where(index == 2 * pair + which, tensor, 0.0), axis=0, keepdims=True)
        for which in range(2)
    ]


def chooser(rows, width, start, count):
    row = iota((rows, width), 0)
    hit = jnp.logical_and(iota((rows, width), 1) == row + start, row < count)
    return jnp.where(hit, 1.0, 0.0).astype(NARROW)


def mark(log_ref, rows, head, value):
    log_ref[rows, :] = jnp.where(iota((1, PAIR), 1) == head, value, log_ref[rows, :])


def copies(semaphores, *pairs):
    made = [
        pltpu.make_async_copy(source, target, semaphores.at[k])
        for k, (source, target) in enumerate(pairs)
    ]
    for one in made:
        one.start()
    return made


def keep(scores):
    return scores


def window_forward(
    x_ref, gain_ref, bias_ref, a_in, a_out,
    n0_ref, pw_ref, mw_ref, x1_ref, nx_ref, vq_ref, ckv_ref,
    w_in, w_out, w_q, w_kv, sem,
):
    rows, features = x_ref.shape
    loads = copies(
        sem,
        (a_in.at[0], w_in),
        (a_out.at[0], w_out),
        (a_in.at[3, :, pl.ds(0, features)], w_q),
        (a_in.at[2, :, pl.ds(features, 2 * features)], w_kv),
    )

    def first(i):
        span = at(i, GROUP)
        n0_ref[span, :] = norm(
            x_ref[span, :].astype(SINGLE), gain_ref[0:1, :], bias_ref[0:1, :]
        ).astype(NARROW)

    loop(rows // GROUP, first)
    loads[0].wait()

    def project(j):
        span = at(j, CHUNK)
        pw_ref[:, span] = plain(n0_ref[...], w_in[:, span]).astype(NARROW)

    loop(3 * features // CHUNK, project)
    window = jnp.where(
        iota((GROUP, GROUP), 0) // WIN == iota((GROUP, GROUP), 1) // WIN, 0.0, MASKED
    )

    def group(i):
        span = at(i, GROUP)
        for pair in range(features // PAIR):
            lane = pair * PAIR
            out, unused = attend(
                pw_ref[span, lane : lane + PAIR],
                pw_ref[span, features + lane : features + lane + PAIR],
                pw_ref[span, 2 * features + lane : 2 * features + lane + PAIR],
                lambda scores: scores + window,
            )
            mw_ref[span, lane : lane + PAIR] = out.astype(NARROW)

    loop(rows // GROUP, group)
    loads[1].wait()

    def second(i):
        span = at(i, GROUP)
        total = x_ref[span, :].astype(SINGLE) + plain(mw_ref[span, :], w_out[...])
        x1_ref[span, :] = total
        nx_ref[span, :] = norm(total, gain_ref[3:4, :], bias_ref[3:4, :]).astype(NARROW)

    loop(rows // GROUP, second)
    loads[2].wait()
    vq_ref[...] = plain(nx_ref[...], w_q[...]).astype(NARROW)
    loads[3].wait()

    def third(j):
        span = at(j, CHUNK)
        ckv_ref[:, span] = plain(nx_ref[...], w_kv[:, span]).astype(NARROW)

    loop(2 * features // CHUNK, third)


def causal_forward(
    q_ref, gain_ref, bias_ref, a_in, a_out,
    n1_ref, pq_ref, mq_ref, q1_ref, nq_ref, cq_ref, vkv_ref, log_ref,
    w_in, w_out, w_q, w_kv, logs, sem,
):
    rows, features = q_ref.shape
    loads = copies(
        sem,
        (a_in.at[1], w_in),
        (a_out.at[1], w_out),
        (a_in.at[2, :, pl.ds(0, features)], w_q),
        (a_in.at[3, :, pl.ds(features, 2 * features)], w_kv),
    )

    def first(i):
        span = at(i, STRIP)
        n1_ref[span, :] = norm(
            q_ref[span, :].astype(SINGLE), gain_ref[1:2, :], bias_ref[1:2, :]
        ).astype(NARROW)

    loop(rows // STRIP, first)
    loads[0].wait()

    def project(j):
        span = at(j, CHUNK)
        pq_ref[:, span] = plain(n1_ref[...], w_in[:, span]).astype(NARROW)

    loop(3 * features // CHUNK, project)
    logs[...] = jnp.zeros_like(logs)

    def pair(p):
        for strip in range(rows // STRIP):
            start, end = strip * STRIP, (strip + 1) * STRIP

            def mask(scores, start=start):
                shape = scores.shape
                return jnp.where(iota(shape, 1) <= iota(shape, 0) + start, scores, MASKED)

            out, sums = attend(
                pq_ref[start:end, at(p, PAIR)],
                pq_ref[0:end, at(p + features // PAIR, PAIR)],
                pq_ref[0:end, at(p + 2 * features // PAIR, PAIR)],
                mask,
            )
            mq_ref[start:end, at(p, PAIR)] = out.astype(NARROW)
            for which in range(2):
                mark(logs, slice(start, end), 2 * p + which, sums[which])

    loop(features // PAIR, pair)
    log_ref[...] = turn(logs[...])
    loads[1].wait()

    def second(i):
        span = at(i, STRIP)
        total = q_ref[span, :].astype(SINGLE) + plain(mq_ref[span, :], w_out[...])
        q1_ref[span, :] = total
        nq_ref[span, :] = norm(total, gain_ref[2:3, :], bias_ref[2:3, :]).astype(NARROW)

    loop(rows // STRIP, second)
    loads[2].wait()
    cq_ref[...] = plain(nq_ref[...], w_q[...]).astype(NARROW)
    loads[3].wait()

    def third(j):
        span = at(j, CHUNK)
        vkv_ref[:, span] = plain(nq_ref[...], w_kv[:, span]).astype(NARROW)

    loop(2 * features // CHUNK, third)


def cross_forward(pieces, order_ref, cq_ref, ckv_ref, valid_ref, *rest):
    out_refs, log_refs, (whole, logs) = rest[:pieces], rest[pieces : 2 * pieces], rest[2 * pieces :]
    rows, features = cq_ref.shape
    part = out_refs[0].shape[0]
    logs[...] = jnp.zeros_like(logs)
    if whole.shape[0] > rows:
        whole[rows:, :] = jnp.zeros((whole.shape[0] - rows, features), NARROW)

    def pair(p):
        for strip in range(rows // STRIP):
            span = slice(strip * STRIP, (strip + 1) * STRIP)
            out, sums = attend(
                cq_ref[span, at(p, PAIR)],
                ckv_ref[:, at(p, PAIR)],
                ckv_ref[:, at(p + features // PAIR, PAIR)],
                lambda scores: scores + valid_ref[...],
            )
            whole[span, at(p, PAIR)] = out.astype(NARROW)
            for which in range(2):
                mark(logs, span, 2 * p + which, sums[which])

    loop(features // PAIR, pair)
    for k in range(pieces):
        out_refs[k][...] = whole[at(order_ref[k], part), :]
        log_refs[k][...] = logs[at(order_ref[k], part), :]


def merge_blocks(pieces, *refs):
    outs, logs = refs[:pieces], refs[pieces : 2 * pieces]
    co_ref, log_ref = refs[2 * pieces :]
    features = co_ref.shape[1]
    peak = functools.reduce(jnp.maximum, [one[...] for one in logs])
    total = peak + jnp.log(functools.reduce(jnp.add, [jnp.exp(one[...] - peak) for one in logs]))
    log_ref[...] = total
    spread = jnp.where(
        iota((PAIR, features), 1) // HEAD == iota((PAIR, features), 0), 1.0, 0.0
    ).astype(NARROW)
    result = jnp.zeros(co_ref.shape, SINGLE)
    for k in range(pieces):
        weight = jnp.exp(logs[k][...] - total)
        high = weight.astype(NARROW)
        low = (weight - high.astype(SINGLE)).astype(NARROW)
        result = result + (plain(high, spread) + plain(low, spread)) * outs[k][...].astype(SINGLE)
    co_ref[...] = result.astype(NARROW)


def reverse_forward(
    length_ref, vq_ref, vkv_ref, x1_ref, a_out,
    mv_ref, x2_ref, log_ref,
    w_out, logs, sem,
):
    rows, features = vq_ref.shape
    keys = vkv_ref.shape[0]
    (load,) = copies(sem, (a_out.at[3], w_out))
    logs[...] = jnp.zeros_like(logs)
    bias = jnp.where(iota((1, keys), 1) < length_ref[0], 0.0, MASKED)

    def pair(p):
        for strip in range(rows // GROUP):
            span = slice(strip * GROUP, (strip + 1) * GROUP)
            out, sums = attend(
                vq_ref[span, at(p, PAIR)],
                vkv_ref[:, at(p, PAIR)],
                vkv_ref[:, at(p + features // PAIR, PAIR)],
                lambda scores: scores + bias,
            )
            mv_ref[span, at(p, PAIR)] = out.astype(NARROW)
            for which in range(2):
                mark(logs, span, 2 * p + which, sums[which])

    loop(features // PAIR, pair)
    log_ref[...] = turn(logs[...])
    load.wait()

    def second(i):
        span = at(i, GROUP)
        x2_ref[span, :] = x1_ref[span, :] + plain(mv_ref[span, :], w_out[...])

    loop(rows // GROUP, second)


def feed_forward_step(block, normed, up, down, cot, hidden, slope, out, grad):
    rows = normed.shape[0]

    def strip(i):
        span = at(i, block)
        value, rise = gelu_both(plain(normed[span, :], up[...]))
        hidden[span, :] = value.astype(NARROW)
        slope[span, :] = (right_t(cot[span, :], down[...]) * rise).astype(NARROW)
        out[span, :] += plain(hidden[span, :], down[...])
        grad[span, :] += right_t(slope[span, :], up[...])

    loop(rows // block, strip)


def patch_feed_forward(
    x2_ref, cot_ref, gain_ref, bias_ref, up_ref, down_ref,
    x3_ref, dx2_ref, up_grad_ref, down_grad_ref, norm_ref,
    normed, hidden, slope, out, grad,
):
    rows = x2_ref.shape[0]
    step = pl.program_id(0)

    @pl.when(step == 0)
    def begin():
        def first(i):
            span = at(i, GROUP)
            normed[span, :] = norm(
                x2_ref[span, :], gain_ref[5:6, :], bias_ref[5:6, :]
            ).astype(NARROW)
            out[span, :] = x2_ref[span, :]
            grad[span, :] = jnp.zeros_like(grad[span, :])

        loop(rows // GROUP, first)

    feed_forward_step(
        256, normed, up_ref.at[0], down_ref.at[0], cot_ref, hidden, slope, out, grad
    )
    up_grad_ref[...] = left_t(normed[...], slope[...]).astype(NARROW)
    down_grad_ref[...] = left_t(hidden[...], cot_ref[...]).astype(NARROW)

    @pl.when(step == pl.num_programs(0) - 1)
    def finish():
        norm_ref[...] = jnp.zeros_like(norm_ref)

        def last(i):
            span = at(i, GROUP)
            x3_ref[span, :] = out[span, :].astype(NARROW)
            part, gain, bias = norm_back(x2_ref[span, :], gain_ref[5:6, :], grad[span, :])
            dx2_ref[span, :] = cot_ref[span, :].astype(SINGLE) + part
            norm_ref[0:1, :] += gain
            norm_ref[1:2, :] += bias

        loop(rows // GROUP, last)


def query_feed_forward(
    pieces, share, hidden_share, place_ref, order_ref, q1_ref, cot_ref, gain_ref, bias_ref,
    w_out, up_ref, down_ref, *rest,
):
    parts, rest = rest[:pieces], rest[pieces:]
    (
        q3_ref, dq2_ref, up_grad_ref, down_grad_ref, norm_ref, co_ref,
        q2, normed, chosen, hidden, slope, out, grad,
    ) = rest
    rows, features = q1_ref.shape
    part = parts[0].shape[0]
    width = up_ref.shape[2]
    step = pl.program_id(0)

    @pl.when(step == 0)
    def begin():
        for k in range(pieces):
            co_ref[at(order_ref[k], part), :] = parts[k][...]

        def first(i):
            span = at(i, STRIP)
            total = q1_ref[span, :] + plain(co_ref[span, :], w_out[0])
            q2[span, :] = total
            out[span, :] = total
            normed[span, :] = norm(total, gain_ref[4:5, :], bias_ref[4:5, :]).astype(NARROW)
            grad[span, :] = jnp.zeros_like(grad[span, :])

        loop(rows // STRIP, first)
        chosen[...] = right_t(
            chooser(chosen.shape[0], features, place_ref[0] * share, share), normed[...]
        ).astype(NARROW)

    feed_forward_step(
        STRIP, normed, up_ref.at[0], down_ref.at[0], cot_ref, hidden, slope, out, grad
    )
    up_grad_ref[...] = plain(chosen[...], slope[...]).astype(NARROW)
    begins = place_ref[0] * hidden_share

    @pl.when(begins // width == step)
    def own_hidden():
        taken = right_t(
            chooser(down_grad_ref.shape[0], width, begins - step * width, hidden_share),
            hidden[...],
        ).astype(NARROW)
        down_grad_ref[...] = plain(taken, cot_ref[...]).astype(NARROW)

    @pl.when(step == pl.num_programs(0) - 1)
    def finish():
        norm_ref[...] = jnp.zeros_like(norm_ref)

        def last(i):
            span = at(i, STRIP)
            q3_ref[span, :] = out[span, :].astype(NARROW)
            piece, gain, bias = norm_back(q2[span, :], gain_ref[4:5, :], grad[span, :])
            dq2_ref[span, :] = cot_ref[span, :].astype(SINGLE) + piece
            norm_ref[0:1, :] += gain
            norm_ref[1:2, :] += bias

        loop(rows // STRIP, last)


def reverse_backward(
    pieces, order_ref, length_ref, dx2_ref, mv_ref, vq_ref, vkv_ref, nx_ref, log_ref, a_out,
    *rest,
):
    dvq_ref, weight_ref, rest = rest[0], rest[1], rest[2:]
    kv_refs, (w_out, rounded, dmv, deltas, dkv, sem) = rest[:pieces], rest[pieces:]
    rows, features = vq_ref.shape
    keys = vkv_ref.shape[0]
    part = kv_refs[0].shape[0]
    (load,) = copies(sem, (a_out.at[3], w_out))
    rounded[...] = dx2_ref[...].astype(NARROW)
    load.wait()
    dmv[...] = right_t(rounded[...], w_out[...]).astype(NARROW)
    weight_ref[:, features:] = left_t(mv_ref[...], rounded[...]).astype(NARROW)
    deltas[...] = head_rows(dmv[...].astype(SINGLE) * mv_ref[...].astype(SINGLE))
    if dkv.shape[0] > keys:
        dkv[keys:, :] = jnp.zeros((dkv.shape[0] - keys, 2 * features), SINGLE)
    size = 256

    def pair(p):
        for strip in range(rows // size):
            span = slice(strip * size, (strip + 1) * size)

            def mask(scores):
                return jnp.where(iota(scores.shape, 0) < length_ref[0], scores, MASKED)

            dq, dk, dv = attend_back(
                vq_ref[span, at(p, PAIR)],
                vkv_ref[:, at(p, PAIR)],
                vkv_ref[:, at(p + features // PAIR, PAIR)],
                dmv[span, at(p, PAIR)],
                row_pair(log_ref, p, span),
                row_pair(deltas, p, span),
                mask,
            )
            dvq_ref[span, at(p, PAIR)] = (dq * (1.0 / math.sqrt(HEAD))).astype(NARROW)
            if strip == 0:
                dkv[0:keys, at(p, PAIR)] = dk
                dkv[0:keys, at(p + features // PAIR, PAIR)] = dv
            else:
                dkv[0:keys, at(p, PAIR)] += dk
                dkv[0:keys, at(p + features // PAIR, PAIR)] += dv

    loop(features // PAIR, pair)
    weight_ref[:, 0:features] = left_t(nx_ref[...], dvq_ref[...]).astype(NARROW)
    for k in range(pieces):
        kv_refs[k][...] = dkv[at(order_ref[k], part), :].astype(NARROW)


def cross_backward(
    pieces, share, place_ref, order_ref, dq2_ref, co_ref, cq_ref, ckv_ref, valid_ref, a_out, *rest
):
    log_parts, rest = rest[:pieces], rest[pieces:]
    dckv_ref, weight_ref, rest = rest[0], rest[1], rest[2:]
    q_refs, (w_out, rounded, dco, deltas, logs, turned, dq_all, dkv, sem) = (
        rest[:pieces],
        rest[pieces:],
    )
    rows, features = cq_ref.shape
    part = log_parts[0].shape[0]
    (load,) = copies(sem, (a_out.at[2], w_out))
    for k in range(pieces):
        logs[at(order_ref[k], part), :] = log_parts[k][...]
    turned[...] = turn(logs[0:rows, :])
    rounded[...] = dq2_ref[...].astype(NARROW)
    load.wait()
    dco[...] = right_t(rounded[...], w_out[...]).astype(NARROW)
    taken = right_t(
        chooser(weight_ref.shape[0], features, place_ref[0] * share, share), co_ref[0:rows, :]
    ).astype(NARROW)
    weight_ref[...] = plain(taken, rounded[...]).astype(NARROW)
    deltas[...] = head_rows(dco[...].astype(SINGLE) * co_ref[0:rows, :].astype(SINGLE))
    if dq_all.shape[0] > rows:
        dq_all[rows:, :] = jnp.zeros((dq_all.shape[0] - rows, features), NARROW)
    edges = [(start, min(start + 256, rows)) for start in range(0, rows, 256)]
    if len(edges) > 1 and edges[-1][1] - edges[-1][0] < 128:
        edges[-2:] = [(edges[-2][0], rows)]

    def pair(p):
        for number, (start, end) in enumerate(edges):
            span = slice(start, end)
            dq, dk, dv = attend_back(
                cq_ref[span, at(p, PAIR)],
                ckv_ref[:, at(p, PAIR)],
                ckv_ref[:, at(p + features // PAIR, PAIR)],
                dco[span, at(p, PAIR)],
                row_pair(turned, p, span),
                row_pair(deltas, p, span),
                lambda scores: scores + valid_ref[...],
            )
            dq_all[span, at(p, PAIR)] = (dq * (1.0 / math.sqrt(HEAD))).astype(NARROW)
            if number == 0:
                dkv[:, at(p, PAIR)] = dk
                dkv[:, at(p + features // PAIR, PAIR)] = dv
            else:
                dkv[:, at(p, PAIR)] += dk
                dkv[:, at(p + features // PAIR, PAIR)] += dv

    loop(features // PAIR, pair)
    dckv_ref[...] = dkv[...].astype(NARROW)
    for k in range(pieces):
        q_refs[k][...] = dq_all[at(order_ref[k], part), :]


def patch_backward(
    x_ref, dx2_ref, x1_ref, nx_ref, n0_ref, pw_ref, mw_ref, dvq_ref, dckv_ref, gain_ref, a_in, a_out,
    kv_weight_ref, weight_ref, grad_ref, norm_ref,
    w_in, w_out, w_q, w_kv, dx1, rounded, dmw, deltas, dpw, sem,
):
    rows, features = x_ref.shape
    loads = copies(
        sem,
        (a_in.at[3, :, pl.ds(0, features)], w_q),
        (a_in.at[2, :, pl.ds(features, 2 * features)], w_kv),
        (a_out.at[0], w_out),
        (a_in.at[0], w_in),
    )
    norm_ref[...] = jnp.zeros_like(norm_ref)

    def kv_weight(j):
        span = at(j, CHUNK)
        kv_weight_ref[:, span] = left_t(nx_ref[...], dckv_ref[:, span]).astype(NARROW)

    loop(2 * features // CHUNK, kv_weight)
    loads[0].wait()
    loads[1].wait()

    def first(i):
        span = at(i, GROUP)
        upstream = right_t(dvq_ref[span, :], w_q[...]) + right_t(dckv_ref[span, :], w_kv[...])
        part, gain, bias = norm_back(x1_ref[span, :], gain_ref[3:4, :], upstream)
        total = dx2_ref[span, :] + part
        dx1[span, :] = total
        rounded[span, :] = total.astype(NARROW)
        norm_ref[0:1, :] += gain
        norm_ref[1:2, :] += bias

    loop(rows // GROUP, first)
    loads[2].wait()
    dmw[...] = right_t(rounded[...], w_out[...]).astype(NARROW)
    weight_ref[:, 3 * features :] = left_t(mw_ref[...], rounded[...]).astype(NARROW)
    deltas[...] = head_rows(dmw[...].astype(SINGLE) * mw_ref[...].astype(SINGLE))
    window = jnp.where(
        iota((GROUP, GROUP), 0) // WIN == iota((GROUP, GROUP), 1) // WIN, 0.0, MASKED
    )

    def group(i):
        span = at(i, GROUP)
        for pair in range(features // PAIR):
            lane = pair * PAIR
            dq, dk, dv = attend_back(
                pw_ref[span, lane : lane + PAIR],
                pw_ref[span, features + lane : features + lane + PAIR],
                pw_ref[span, 2 * features + lane : 2 * features + lane + PAIR],
                dmw[span, lane : lane + PAIR],
                None,
                [deltas[2 * pair + w : 2 * pair + w + 1, span] for w in range(2)],
                lambda scores: scores + window,
            )
            dpw[span, lane : lane + PAIR] = (dq * (1.0 / math.sqrt(HEAD))).astype(NARROW)
            dpw[span, features + lane : features + lane + PAIR] = dk.astype(NARROW)
            dpw[span, 2 * features + lane : 2 * features + lane + PAIR] = dv.astype(NARROW)

    loop(rows // GROUP, group)

    def in_weight(j):
        span = at(j, CHUNK)
        weight_ref[:, span] = left_t(n0_ref[...], dpw[:, span]).astype(NARROW)

    loop(3 * features // CHUNK, in_weight)
    loads[3].wait()

    def last(i):
        span = at(i, GROUP)
        upstream = right_t(dpw[span, :], w_in[...])
        part, gain, bias = norm_back(x_ref[span, :].astype(SINGLE), gain_ref[0:1, :], upstream)
        grad_ref[span, :] = dx1[span, :] + part
        norm_ref[2:3, :] += gain
        norm_ref[3:4, :] += bias

    loop(rows // GROUP, last)


def share_backward(
    pieces, q1_ref, nq_ref, gain_ref, a_in, *rest
):
    q_parts, kv_parts, rest = rest[:pieces], rest[pieces : 2 * pieces], rest[2 * pieces :]
    grad_ref, weight_ref, norm_ref, w_q, w_kv, summed, sem = rest
    features = q1_ref.shape[1]
    loads = copies(
        sem,
        (a_in.at[2, :, pl.ds(0, features)], w_q),
        (a_in.at[3, :, pl.ds(features, 2 * features)], w_kv),
    )
    summed[:, 0:features] = functools.reduce(
        jnp.add, [one[...].astype(SINGLE) for one in q_parts]
    ).astype(NARROW)
    summed[:, features:] = functools.reduce(
        jnp.add, [one[...].astype(SINGLE) for one in kv_parts]
    ).astype(NARROW)

    def weight(j):
        span = at(j, CHUNK)
        weight_ref[:, span] = left_t(nq_ref[...], summed[:, span]).astype(NARROW)

    loop(3 * features // CHUNK, weight)
    for load in loads:
        load.wait()
    upstream = right_t(summed[:, 0:features], w_q[...]) + right_t(summed[:, features:], w_kv[...])
    part, gain, bias = norm_back(q1_ref[...], gain_ref[2:3, :], upstream)
    grad_ref[...] = part.astype(NARROW)
    norm_ref[...] = jnp.zeros_like(norm_ref)
    norm_ref[0:1, :] = gain
    norm_ref[1:2, :] = bias


def causal_backward(
    pieces, share, place_ref, order_ref, q_ref, dq2_ref, n1_ref, pq_ref, mq_ref, log_ref, gain_ref,
    a_in, a_out, *rest
):
    parts, rest = rest[:pieces], rest[pieces:]
    (
        weight_ref, grad_ref, norm_ref,
        w_in, w_out, gathered, dq1, rounded, dmq, deltas, dkv, dpq, sem,
    ) = rest
    rows, features = q_ref.shape
    part = parts[0].shape[0]
    loads = copies(sem, (a_out.at[1], w_out), (a_in.at[1], w_in))
    for k in range(pieces):
        gathered[at(order_ref[k], part), :] = parts[k][...]

    def first(i):
        span = at(i, STRIP)
        total = dq2_ref[span, :] + gathered[span, :].astype(SINGLE)
        dq1[span, :] = total
        rounded[span, :] = total.astype(NARROW)

    loop(rows // STRIP, first)
    loads[0].wait()
    dmq[...] = right_t(rounded[...], w_out[...]).astype(NARROW)
    chosen = chooser(weight_ref.shape[0], features, place_ref[0] * share, share)
    taken = right_t(chosen, mq_ref[...]).astype(NARROW)
    weight_ref[:, 3 * features :] = plain(taken, rounded[...]).astype(NARROW)
    deltas[...] = head_rows(dmq[...].astype(SINGLE) * mq_ref[...].astype(SINGLE))
    edges = [(start, min(start + 256, rows)) for start in range(0, rows, 256)]

    def pair(p):
        for number, (start, end) in reversed(list(enumerate(edges))):
            span = slice(start, end)

            def mask(scores, start=start):
                shape = scores.shape
                return jnp.where(iota(shape, 0) <= iota(shape, 1) + start, scores, MASKED)

            dq, dk, dv = attend_back(
                pq_ref[span, at(p, PAIR)],
                pq_ref[0:end, at(p + features // PAIR, PAIR)],
                pq_ref[0:end, at(p + 2 * features // PAIR, PAIR)],
                dmq[span, at(p, PAIR)],
                row_pair(log_ref, p, span),
                row_pair(deltas, p, span),
                mask,
            )
            dpq[span, at(p, PAIR)] = (dq * (1.0 / math.sqrt(HEAD))).astype(NARROW)
            if end == rows:
                dkv[0:end, 0:PAIR] = dk
                dkv[0:end, PAIR:] = dv
            else:
                dkv[0:end, 0:PAIR] += dk
                dkv[0:end, PAIR:] += dv
        dpq[:, at(p + features // PAIR, PAIR)] = dkv[:, 0:PAIR].astype(NARROW)
        dpq[:, at(p + 2 * features // PAIR, PAIR)] = dkv[:, PAIR:].astype(NARROW)

    loop(features // PAIR, pair)
    taken = right_t(chosen, n1_ref[...]).astype(NARROW)
    weight_ref[:, 0 : 3 * features] = plain(taken, dpq[...]).astype(NARROW)
    loads[1].wait()
    norm_ref[...] = jnp.zeros_like(norm_ref)

    def last(i):
        span = at(i, STRIP)
        upstream = right_t(dpq[span, :], w_in[...])
        piece, gain, bias = norm_back(q_ref[span, :].astype(SINGLE), gain_ref[1:2, :], upstream)
        grad_ref[span, :] = dq1[span, :] + piece
        norm_ref[0:1, :] += gain
        norm_ref[1:2, :] += bias

    loop(rows // STRIP, last)


def bits_of(count):
    return max(count - 1, 0).bit_length()


def swap(tensor, axis, mask):
    return lax.ppermute(tensor, axis, [(i, i ^ mask) for i in range(lax.axis_size(axis))])


def pick(tensor, place, dim):
    return lax.dynamic_index_in_dim(tensor, place, dim, keepdims=False)


def fold(tensor, axis, bit, dim):
    own = (lax.axis_index(axis) >> bit) & 1
    arrived = swap(pick(tensor, 1 - own, dim).astype(NARROW), axis, 1 << bit)
    return pick(tensor, own, dim).astype(SINGLE) + arrived.astype(SINGLE)


def unfold(tensor, axis, bit, dim):
    own = (lax.axis_index(axis) >> bit) & 1
    arrived = swap(tensor, axis, 1 << bit)
    return jnp.where(
        own == 0,
        jnp.stack((tensor, arrived), axis=dim),
        jnp.stack((arrived, tensor), axis=dim),
    )


def scatter_blk(tensor):
    bits = bits_of(lax.axis_size("blk"))
    tensor = tensor.reshape((2,) * bits + tensor.shape[1:])
    for bit in range(bits):
        tensor = fold(tensor, "blk", bit, bits - 1 - bit)
    return tensor


def sum_rep_scatter(tensor, dim):
    bits = bits_of(lax.axis_size("rep"))
    shape = tensor.shape
    tensor = tensor.reshape(
        shape[:dim] + (2,) * bits + (shape[dim] // 2**bits,) + shape[dim + 1 :]
    )
    for bit in range(bits):
        tensor = fold(tensor, "rep", bit, dim)
    return tensor


def gather_rep(tensor, dim):
    bits = bits_of(lax.axis_size("rep"))
    for bit in reversed(range(bits)):
        tensor = unfold(tensor, "rep", bit, dim)
    shape = tensor.shape
    return tensor.reshape(shape[:dim] + (-1,) + shape[dim + bits + 1 :])


def reduce_all(tensor):
    count = lax.axis_size("blk")
    tensor = tensor.reshape(count, tensor.shape[0] // count, tensor.shape[1])
    tensor = sum_rep_scatter(tensor, 1)
    tensor = scatter_blk(tensor).astype(NARROW)
    return gather_rep(tensor, 0)


def reduce_rep(tensor):
    return gather_rep(sum_rep_scatter(tensor, 0).astype(NARROW), 0)


DIRECT = 8


def piece_order():
    count = lax.axis_size("blk")
    numbers = jnp.arange(count, dtype=jnp.int32)
    return numbers ^ lax.axis_index("blk").astype(jnp.int32) if count <= DIRECT else numbers


def exchange(pieces):
    if len(pieces) <= DIRECT:
        return [one if k == 0 else swap(one, "blk", k) for k, one in enumerate(pieces)]
    whole = lax.all_to_all(jnp.stack(pieces), "blk", 0, 0)
    return [whole[k] for k in range(len(pieces))]


def gather(tensor):
    count = lax.axis_size("blk")
    if count <= DIRECT:
        return [tensor if k == 0 else swap(tensor, "blk", k) for k in range(count)]
    whole = lax.all_gather(tensor, "blk")
    return [whole[k] for k in range(count)]


VMEM = pl.BlockSpec(memory_space=pltpu.VMEM)
SMEM = pl.BlockSpec(memory_space=pltpu.SMEM)
ANY = pl.BlockSpec(memory_space=pl.ANY)


def like(*shape, kind=NARROW):
    return jax.ShapeDtypeStruct(shape, kind)


def call(kernel, outs, operands, specs, scratch, flops, grid=None, out_specs=None, semaphores=0):
    scratch = [pltpu.VMEM(shape, kind) for shape, kind in scratch]
    if semaphores:
        scratch.append(pltpu.SemaphoreType.DMA((semaphores,)))
    extra = {} if grid is None else {"grid": grid}
    return pl.pallas_call(
        kernel,
        out_shape=outs,
        in_specs=specs,
        out_specs=[VMEM] * len(outs) if out_specs is None else out_specs,
        scratch_shapes=scratch,
        compiler_params=pltpu.CompilerParams(vmem_limit_bytes=56 * 2**20),
        cost_estimate=pl.CostEstimate(
            flops=int(flops), bytes_accessed=sum(o.size * o.dtype.itemsize for o in operands), transcendentals=0
        ),
        **extra,
    )(*operands)


def body(
    patches,
    queries,
    window_valid,
    answer_length,
    norm_gain,
    norm_bias,
    attn_in,
    attn_out,
    mlp_in,
    mlp_out,
    cot_patches,
    cot_queries,
):
    x, q, cot_x, cot_q = patches[0], queries[0], cot_patches[0], cot_queries[0]
    rows, features = x.shape
    count = q.shape[0]
    hidden = mlp_in.shape[2]
    blocks = lax.axis_size("blk")
    place = lax.axis_index("blk").astype(jnp.int32)
    places = place.reshape(1)
    order = piece_order()
    share = features // blocks
    hidden_share = hidden // blocks
    share_rows = -(-share // 16) * 16
    hidden_rows = -(-hidden_share // 16) * 16
    part = -(-count // (blocks * 16)) * 16
    padded = part * blocks
    wide = 3 * features
    leader = (place == 0).astype(SINGLE)
    valid = jnp.where(jnp.repeat(window_valid[0], WIN) > 0, 0.0, MASKED).astype(SINGLE)

    def own_columns(tensor):
        return lax.dynamic_slice_in_dim(tensor, place * share, share, 1)

    def own_rows(tensor):
        tensor = jnp.pad(tensor, ((0, padded - count), (0, 0)))
        return lax.dynamic_slice_in_dim(tensor, place * part, part, 0)

    square = 2.0 * features * features

    n0, pw, mw, x1, nx, vq, ckv = call(
        window_forward,
        [
            like(rows, features), like(rows, wide), like(rows, features),
            like(rows, features, kind=SINGLE), like(rows, features), like(rows, features),
            like(rows, 2 * features),
        ],
        [x, norm_gain, norm_bias, attn_in, attn_out],
        [VMEM, VMEM, VMEM, ANY, ANY],
        [((features, wide), NARROW), ((features, features), NARROW),
         ((features, features), NARROW), ((features, 2 * features), NARROW)],
        rows * square * 9,
        semaphores=4,
    )
    n1, pq, mq, q1, nq, cq, vkv, log_q = call(
        causal_forward,
        [
            like(count, features), like(count, wide), like(count, features),
            like(count, features, kind=SINGLE), like(count, features), like(count, features),
            like(count, 2 * features), like(16, count, kind=SINGLE),
        ],
        [q, norm_gain, norm_bias, attn_in, attn_out],
        [VMEM, VMEM, VMEM, ANY, ANY],
        [((features, wide), NARROW), ((features, features), NARROW),
         ((features, features), NARROW), ((features, 2 * features), NARROW),
         ((count, PAIR), SINGLE)],
        count * square * 15,
        semaphores=4,
    )
    pieces = call(
        functools.partial(cross_forward, blocks),
        [like(part, features)] * blocks + [like(part, PAIR, kind=SINGLE)] * blocks,
        [order, cq, ckv, valid[None, :]],
        [SMEM, VMEM, VMEM, VMEM],
        [((padded, features), NARROW), ((padded, PAIR), SINGLE)],
        count * square * 6,
    )
    merged = call(
        functools.partial(merge_blocks, blocks),
        [like(part, features), like(part, PAIR, kind=SINGLE)],
        exchange(pieces[:blocks]) + exchange(pieces[blocks:]),
        [VMEM] * (2 * blocks),
        [],
        padded * square,
    )
    co_parts, log_parts = gather(merged[0]), gather(merged[1])
    mv, x2, log_v = call(
        reverse_forward,
        [like(rows, features), like(rows, features, kind=SINGLE), like(16, rows, kind=SINGLE)],
        [answer_length, vq, vkv, x1, attn_out],
        [SMEM, VMEM, VMEM, VMEM, ANY],
        [((features, features), NARROW), ((rows, PAIR), SINGLE)],
        rows * square * 8,
        semaphores=1,
    )
    fixed = lambda *shape: pl.BlockSpec(shape, lambda j: (0,) * len(shape))
    x3, dx2, up_x, down_x, norm_five = call(
        patch_feed_forward,
        [
            like(rows, features), like(rows, features, kind=SINGLE), like(features, hidden),
            like(hidden, features), like(8, features, kind=SINGLE),
        ],
        [x2, cot_x, norm_gain, norm_bias, mlp_in, mlp_out],
        [
            fixed(rows, features), fixed(rows, features), fixed(6, features), fixed(6, features),
            pl.BlockSpec((1, features, CHUNK), lambda j: (0, 0, j)),
            pl.BlockSpec((1, CHUNK, features), lambda j: (0, j, 0)),
        ],
        [((rows, features), NARROW), ((rows, CHUNK), NARROW), ((rows, CHUNK), NARROW),
         ((rows, features), SINGLE), ((rows, features), SINGLE)],
        rows * square * 24,
        grid=(hidden // CHUNK,),
        out_specs=[
            fixed(rows, features), fixed(rows, features),
            pl.BlockSpec((features, CHUNK), lambda j: (0, j)),
            pl.BlockSpec((CHUNK, features), lambda j: (j, 0)),
            fixed(8, features),
        ],
    )
    up_x_total, down_x_total = reduce_all(up_x), reduce_all(down_x)
    dvq, reverse_weight, *kv_pieces = call(
        functools.partial(reverse_backward, blocks),
        [like(rows, features), like(features, 2 * features)] + [like(part, 2 * features)] * blocks,
        [order, answer_length, dx2, mv, vq, vkv, nx, log_v, attn_out],
        [SMEM, SMEM, VMEM, VMEM, VMEM, VMEM, VMEM, VMEM, ANY],
        [((features, features), NARROW), ((rows, features), NARROW), ((rows, features), NARROW),
         ((16, rows), SINGLE), ((padded, 2 * features), SINGLE)],
        rows * square * 16,
        semaphores=1,
    )
    kv_parts = exchange(kv_pieces)
    reverse_total = reduce_all(reverse_weight)
    q3, dq2, up_q, down_q, norm_four, co = call(
        functools.partial(query_feed_forward, blocks, share, hidden_share),
        [
            like(count, features), like(count, features, kind=SINGLE), like(share_rows, hidden),
            like(hidden_rows, features), like(8, features, kind=SINGLE), like(padded, features),
        ],
        [places, order, q1, cot_q, norm_gain, norm_bias, attn_out, mlp_in, mlp_out] + co_parts,
        [
            SMEM, SMEM, fixed(count, features), fixed(count, features), fixed(6, features),
            fixed(6, features), pl.BlockSpec((1, features, features), lambda j: (2, 0, 0)),
            pl.BlockSpec((1, features, CHUNK), lambda j: (1, 0, j)),
            pl.BlockSpec((1, CHUNK, features), lambda j: (1, j, 0)),
        ] + [fixed(part, features)] * blocks,
        [((count, features), SINGLE), ((count, features), NARROW), ((share_rows, count), NARROW),
         ((count, CHUNK), NARROW), ((count, CHUNK), NARROW),
         ((count, features), SINGLE), ((count, features), SINGLE)],
        count * square * 18,
        grid=(hidden // CHUNK,),
        out_specs=[
            fixed(count, features), fixed(count, features),
            pl.BlockSpec((share_rows, CHUNK), lambda j: (0, j)),
            fixed(hidden_rows, features), fixed(8, features), fixed(padded, features),
        ],
    )
    dckv, cross_out_weight, *q_pieces = call(
        functools.partial(cross_backward, blocks, share),
        [like(rows, 2 * features), like(share_rows, features)] + [like(part, features)] * blocks,
        [places, order, dq2, co, cq, ckv, valid[:, None], attn_out] + log_parts,
        [SMEM, SMEM, VMEM, VMEM, VMEM, VMEM, VMEM, ANY] + [VMEM] * blocks,
        [((features, features), NARROW), ((count, features), NARROW), ((count, features), NARROW),
         ((16, count), SINGLE), ((padded, PAIR), SINGLE), ((16, count), SINGLE),
         ((padded, features), NARROW), ((rows, 2 * features), SINGLE)],
        count * square * 12,
        semaphores=1,
    )
    q_parts = exchange(q_pieces)
    up_q_total = reduce_rep(up_q[:share])
    down_q_total = reduce_rep(down_q[:hidden_share])
    kv_weight, window_weight, grad_x, norm_x = call(
        patch_backward,
        [
            like(features, 2 * features), like(features, 4 * features),
            like(rows, features, kind=SINGLE), like(8, features, kind=SINGLE),
        ],
        [x, dx2, x1, nx, n0, pw, mw, dvq, dckv, norm_gain, attn_in, attn_out],
        [VMEM] * 10 + [ANY, ANY],
        [((features, wide), NARROW), ((features, features), NARROW),
         ((features, features), NARROW), ((features, 2 * features), NARROW),
         ((rows, features), SINGLE), ((rows, features), NARROW), ((rows, features), NARROW),
         ((16, rows), SINGLE), ((rows, wide), NARROW)],
        rows * square * 24,
        semaphores=4,
    )
    kv_total, window_total = reduce_all(kv_weight), reduce_all(window_weight)
    dq1_share, share_weight, norm_two = call(
        functools.partial(share_backward, blocks),
        [like(part, features), like(features, wide), like(8, features, kind=SINGLE)],
        [own_rows(q1), own_rows(nq), norm_gain, attn_in] + q_parts + kv_parts,
        [VMEM, VMEM, VMEM, ANY] + [VMEM] * (2 * blocks),
        [((features, features), NARROW), ((features, 2 * features), NARROW),
         ((part, wide), NARROW)],
        part * square * 6,
        semaphores=2,
    )
    share_total = reduce_all(share_weight)
    causal_weight, grad_q, norm_one = call(
        functools.partial(causal_backward, blocks, share),
        [
            like(share_rows, 4 * features), like(count, features, kind=SINGLE),
            like(8, features, kind=SINGLE),
        ],
        [places, order, q, dq2, n1, pq, mq, log_q, norm_gain, attn_in, attn_out]
        + gather(dq1_share),
        [SMEM, SMEM] + [VMEM] * 7 + [ANY, ANY] + [VMEM] * blocks,
        [((features, wide), NARROW), ((features, features), NARROW), ((padded, features), NARROW),
         ((count, features), SINGLE), ((count, features), NARROW), ((count, features), NARROW),
         ((16, count), SINGLE), ((count, 2 * PAIR), SINGLE), ((count, wide), NARROW)],
        count * square * 16,
        semaphores=2,
    )
    query_total = reduce_rep(
        jnp.concatenate((causal_weight[:share], cross_out_weight[:share]), axis=1)
    )
    norms = jnp.stack(
        (
            norm_x[2], norm_one[0] * leader, norm_two[0], norm_x[0], norm_four[0] * leader,
            norm_five[0], norm_x[3], norm_one[1] * leader, norm_two[1], norm_x[1],
            norm_four[1] * leader, norm_five[1],
        )
    )
    norms = own_columns(lax.psum(norms, ("blk", "rep")))
    grad_attn_in = jnp.stack(
        (
            window_total[:, :wide],
            query_total[:, :wide],
            jnp.concatenate((share_total[:, :features], kv_total), axis=1),
            jnp.concatenate((reverse_total[:, :features], share_total[:, features:]), axis=1),
        )
    )
    grad_attn_out = jnp.stack(
        (
            window_total[:, wide:],
            query_total[:, wide : wide + features],
            query_total[:, wide + features :],
            reverse_total[:, features:],
        )
    )
    return (
        x3[None],
        own_columns(q3)[None],
        grad_x[None],
        own_columns(grad_q)[None],
        norms[:6],
        norms[6:],
        grad_attn_in.astype(SINGLE),
        grad_attn_out.astype(SINGLE),
        jnp.stack((up_x_total, up_q_total)).astype(SINGLE),
        jnp.stack((down_x_total, down_q_total)).astype(SINGLE),
    )


def solution(mesh):
    placed = (
        P("rep", "blk", None),
        P("rep", None, None),
        P("rep", "blk"),
        P("rep"),
        P(),
        P(),
        P(),
        P(),
        P(),
        P(),
        P("rep", "blk", None),
        P("rep", None, None),
    )
    return jax.shard_map(
        body,
        mesh=mesh,
        in_specs=placed,
        out_specs=(
            P("rep", "blk", None),
            P("rep", None, "blk"),
            P("rep", "blk", None),
            P("rep", None, "blk"),
            P(None, "blk"),
            P(None, "blk"),
            P(None, "blk", None),
            P(None, "blk", None),
            P(None, "blk", None),
            P(None, "blk", None),
        ),
        check_vma=False,
    )
```

time: 1070 us -> 826 us (0.77)
  matrix products: 379 us -> 0 us
  Pallas kernels: 0 us -> 326 us
  starting transfers between devices: 54.8 us -> 177 us
  other arithmetic: 148 us -> 27.7 us
  local copies, waits for them, and re-layouts: 162 us -> 41.8 us
  waiting for transfers between devices: 240 us -> 203 us
  blocking collectives: 72.5 us -> 37.9 us
    dot_general x65 -> x0, matrix products: 379 us -> none  [the longest x14 91.4 us: matmul(): return jnp.dot(former, latter, preferred_element_type=SINGLE)]
    pallas_call x0 -> x12, Pallas kernels: none -> 326 us  [call(): pl.pallas_call(kernel, out_shape=outs, in_specs=specs, out_specs=[VMEM] *...]
    ppermute x62 -> x103, starting transfers between devices: 54.8 us -> 177 us  [swap(): lax.ppermute(tensor, axis, [(i, i ^ mask) for i in range(lax.axis_size(ax...]
    convert_element_type x15 -> x2, other arithmetic: 49.6 us -> 3.12 us  [the longest x1 1.56 us: body(): jnp.stack((down_x_total, down_q_total)).astype(SINGLE)]
    reduce_sum x22 -> x0, other arithmetic: 44.3 us -> none  [the longest x3 25.4 us: attend_forward(): return (attended, jax.nn.logsumexp(scores, axis=-1))]
    convert_element_type x45 -> x27, local copies, waits for them, and re-layouts: 44.5 us -> 1.43 us  [fold(): arrived = swap(pick(tensor, 1 - own, dim).astype(NARROW), axis, 1 << bit)]
    ppermute x62 -> x103, waiting for transfers between devices: 240 us -> 203 us  [swap(): lax.ppermute(tensor, axis, [(i, i ^ mask) for i in range(lax.axis_size(ax...]
    unnamed x398 -> x136, local copies, waits for them, and re-layouts: 36.5 us -> 4.4 us
  transfers between devices with their start and end apart: 62 -> 103, of which waited for: 33 -> 36; matrix products, arithmetic and copies ran while one was open for 46% -> 7% of each run, Pallas kernels for 0% -> 30%
where the time goes in v2:
time: 826 us; the launch traced here: 816 us
  Pallas kernels  326 us (39%)
  waiting for transfers between devices  203 us (25%)
  starting transfers between devices  177 us (21%)
  local copies, waits for them, and re-layouts  41.8 us (5%)
  blocking collectives  37.9 us (5%)
  other arithmetic  27.7 us (3%)
    pallas_call x12, Pallas kernels, call(): pl.pallas_call(kernel, out_shape=outs, in_specs=specs, out_specs=[VMEM] *...  326 us
    ppermute x103, waiting for transfers between devices, swap(): lax.ppermute(tensor, axis, [(i, i ^ mask) for i in range(lax.axis_size(ax...  203 us
    ppermute x103, starting transfers between devices, swap(): lax.ppermute(tensor, axis, [(i, i ^ mask) for i in range(lax.axis_size(ax...  177 us
    psum x1, blocking collectives, body(): norms = own_columns(lax.psum(norms, ('blk', 'rep')))  37.9 us
  transfers between devices with their start and end apart: 103, of which 36 were waited for; matrix products, arithmetic and copies ran while one was open for 7% of the time, Pallas kernels for 30%

profile of v2, /device:TPU:0, one launch (start us, length us, event | category | flops | bytes accessed | tf_op | source)
XLA Modules:
  0.0 816.1 jit_solution(9036932356654139170)
XLA Ops:
  2.6 24.6 %shard_map.195 = (bf16[512,768]{1,0:T(8,128)(2,1)}, bf16[512,2304]{1,0:T(8,128)(2,1)}, bf16[512,768]{1,0:T(8,128)(2,1)}, f32[512,768]{1,0:T(8,128)}, bf16[512,76...) custom-call(bf16[512,768]{1,0:T(8,128)(2,1)} %bitcast.362, f32[6,768]{1,0:T(8,128)} %gain_ref.13, ...), custom_call_target="tpu_custom_call" | custom-call | flops 5435817984 | bytes 19697664 | tf_op jit(solution)/shard_map/pallas_call | solution.py:921
  27.2 36.7 %shard_map.196 = (bf16[800,768]{1,0:T(8,128)(2,1)}, bf16[800,2304]{1,0:T(8,128)(2,1)}, bf16[800,768]{1,0:T(8,128)(2,1)}, f32[800,768]{1,0:T(8,128)}, bf16[800,76...) custom-call(bf16[800,768]{1,0:T(8,128)(2,1)} %bitcast.359, ...), custom_call_target="tpu_custom_call" | custom-call | flops 14155776000 | bytes 20140032 | tf_op jit(solution)/shard_map/pallas_call | solution.py:921
  64.0 20.9 %shard_map.199 = (bf16[112,768]{1,0:T(8,128)(2,1)}, bf16[112,768]{1,0:T(8,128)(2,1)}, bf16[112,768]{1,0:T(8,128)(2,1)}, bf16[112,768]{1,0:T(8,128)(2,1)}, bf16[1...) custom-call(s32[8]{0:T(128)} %iota_xor_fusion.order_ref, ...), custom_call_target="tpu_custom_call" | custom-call | flops 5662310400 | bytes 2803744 | tf_op jit(solution)/shard_map/pallas_call | solution.py:921
  84.8 3.0 collective-permute-start.7
  89.4 3.0 collective-permute-start.10
  94.3 23.1 %shard_map.197 = (bf16[512,768]{1,0:T(8,128)(2,1)}, f32[512,768]{1,0:T(8,128)}, f32[16,512]{1,0:T(8,128)}) custom-call(s32[1]{0:T(128)S(6)} %copy.98.length_ref, bf16[512,768]{1,0:T(8,128)(2,1)} %get-tuple-element.87.vq_ref, bf16[800,1536]{1,0:T(8,128)(2,1)} %get-tuple-element.88.vkv_ref, f32[512,768]{1,0:T(8,128)} %get-tuple-element.89.x1_ref, ...), custom_call_target="tpu_custom_call" | custom-call | flops 4831838208 | bytes 9535492 | tf_op jit(solution)/shard_map/pallas_call | solution.py:921
  117.4 26.6 %shard_map.198 = (bf16[512,768]{1,0:T(8,128)(2,1)}, f32[512,768]{1,0:T(8,128)}, bf16[768,3072]{1,0:T(8,128)(2,1)}, bf16[3072,768]{1,0:T(8,128)(2,1)}, f32[8,768]{1,0:T(8,128)}) custom-call(f32[512,768]{1,0:T(8,128)} %get-tuple-element.90.x2_ref, bf16[512,768]{1,0:T(8,128)(2,1)} %bitcast.361, f32[6,768]{1,0:T(8,128)} %gain_ref.13, f32[6,768]{1,0:T(8,128)} %bias_ref.7, ...), custom_call_target="tpu_custom_call" | custom-call | flops 14495514624 | bytes 21270528 | tf_op jit(solution)/shard_map/pallas_call | solution.py:921
  144.1 28.3 %shard_map.202 = (bf16[512,768]{1,0:T(8,128)(2,1)}, bf16[768,1536]{1,0:T(8,128)(2,1)}, bf16[112,1536]{1,0:T(8,128)(2,1)}, bf16[112,1536]{1,0:T(8,128)(2,1)}, bf1...) custom-call(s32[8]{0:T(128)} %iota_xor_fusion.order_ref, ...), custom_call_target="tpu_custom_call" | custom-call | flops 9663676416 | bytes 11141156 | tf_op jit(solution)/shard_map/pallas_call | solution.py:921
  172.5 3.7 collective-permute-start.12
  183.4 2.4 collective-permute-start.3
  187.6 3.7 collective-permute-start.5
  191.9 4.2 constant_dynamic-slice_fusion.2
  196.1 10.2 %collective-permute-done.3.refs_4_ = bf16[112,768]{1,0:T(8,128)(2,1)S(1)} collective-permute-done((bf16[112,768]{1,0:T(8,128)(2,1)S(1)}, bf16[112,768]{1,0:T(8,128)(2,1)S(1)}, u32[]{:S(2)}, u32[]{:S(2)}) %collective-permute-start.3) | collective-permute-done | bytes 172064 | tf_op jit(solution)/shard_map/ppermute | solution.py:821
  206.3 3.9 collective-permute-done.4.refs_5_
  211.0 3.1 shard_map.200
  214.1 2.6 collective-permute-start.27
  223.5 3.9 collective-permute-start.18
  227.4 6.7 collective-permute-start.17
  236.4 5.0 collective-permute-start.15
  248.7 5.6 collective-permute-start.25
  257.9 42.3 %shard_map.201 = (bf16[800,768]{1,0:T(8,128)(2,1)}, f32[800,768]{1,0:T(8,128)}, bf16[96,3072]{1,0:T(8,128)(2,1)}, bf16[384,768]{1,0:T(8,128)(2,1)}, f32[8,768]{1,0:T(8,128)}, /*index=5*/bf16[896,768]{1,0:T(8,128)(2,1)}) custom-call(s32[1]{0:T(128)} %bitcast.4.place_ref, s32[8]{0:T(128)} %iota_xor_fusion.order_ref, f32[800,768]{1,0:T(8,128)} %get-tuple-element.92.q1_ref, ...), custom_call_target="tpu_custom_call" | custom-call | flops 16986931200 | bytes 28692516 | tf_op jit(solution)/shard_map/pallas_call | solution.py:921
  303.8 2.8 collective-permute-start.38
  307.3 31.8 %shard_map.203 = (bf16[512,1536]{1,0:T(8,128)(2,1)}, bf16[96,768]{1,0:T(8,128)(2,1)}, bf16[112,768]{1,0:T(8,128)(2,1)}, bf16[112,768]{1,0:T(8,128)(2,1)}, bf16[1...) custom-call(s32[1]{0:T(128)} %bitcast.4.place_ref, ...), custom_call_target="tpu_custom_call" | custom-call | flops 11324620800 | bytes 11814948 | tf_op jit(solution)/shard_map/pallas_call | solution.py:921
  339.1 37.4 %shard_map.204 = (bf16[768,1536]{1,0:T(8,128)(2,1)}, bf16[768,3072]{1,0:T(8,128)(2,1)}, f32[512,768]{1,0:T(8,128)}, f32[8,768]{1,0:T(8,128)}) custom-call(bf16[512,768]{1,0:T(8,128)(2,1)} %bitcast.363, f32[512,768]{1,0:T(8,128)} %get-tuple-element.113.dx2_ref, f32[512,768]{1,0:T(8,128)} %get-tuple-element.89.x1_ref, ...), custom_call_target="tpu_custom_call" | custom-call | flops 14495514624 | bytes 29902848 | tf_op jit(solution)/shard_map/pallas_call | solution.py:921
  376.5 5.8 constant_dynamic-slice_fusion.6
  390.5 2.5 collective-permute-start.30
  393.0 4.2 collective-permute-done.40.rest_14_
  397.2 12.3 %collective-permute-start.31 = (bf16[112,768]{1,0:T(8,128)(2,1)}, bf16[112,768]{1,0:T(8,128)(2,1)}, u32[]{:S(2)}, u32[]{:S(2)}) collective-permute-start(bf16[112,768]{1,0:T(8,128)(2,1)} %get-tuple-element.135), channel_id=1, source_target_pairs={{0,16},{4,20},{8,24},{12,28},{16,0},{20,4},{24,8},{28,12},{1,17},{... | collective-permute-start | bytes 516104 | tf_op jit(solution)/shard_map/ppermute | solution.py:821
  409.5 12.4 %collective-permute-start.32 = (bf16[112,768]{1,0:T(8,128)(2,1)}, bf16[112,768]{1,0:T(8,128)(2,1)}, u32[]{:S(2)}, u32[]{:S(2)}) collective-permute-start(bf16[112,768]{1,0:T(8,128)(2,1)} %get-tuple-element.136), channel_id=1, source_target_pairs={{0,20},{4,16},{8,28},{12,24},{16,4},{20,0},{24,12},{28,8},{1,21},{... | collective-permute-start | bytes 516104 | tf_op jit(solution)/shard_map/ppermute | solution.py:821
  423.1 2.8 collective-permute-start.34
  427.8 3.3 copy.96
  433.3 5.5 collective-permute-done.32.rest_5_
  438.9 6.5 shard_map.205
  445.4 2.5 collective-permute-start.48
  448.0 7.7 collective-permute-start.46
  455.7 2.8 dynamic-slice_bitcast_fusion
  461.3 7.9 collective-permute-start.43
  469.3 5.8 collective-permute-done.46.rest_5_
  477.9 2.8 collective-permute-done.43.rest_2_
  483.8 44.9 %shard_map.206 = (bf16[96,3072]{1,0:T(8,128)(2,1)}, f32[800,768]{1,0:T(8,128)}, f32[8,768]{1,0:T(8,128)}) custom-call(s32[1]{0:T(128)} %bitcast.4.place_ref, s32[8]{0:T(128)} %iota_xor_fusion.order_ref, bf16[800,768]{1,0:T(8,128)(2,1)} %bitcast.360, f32[800,768]{1,0:T(8,128)} %get-tuple-element.121.dq2_ref, bf16[800,768]{1,0:T(8,128)(2,1)} %get-tuple-element.126.n1_ref, ...), custom_call_target="tpu_custom_call" | custom-call | flops 15099494400 | bytes 30150692 | tf_op jit(solution)/shard_map/pallas_call | solution.py:921
  531.5 37.9 %psum.7 = f32[12,768]{1,0:T(8,128)S(1)} all-reduce(f32[12,768]{1,0:T(8,128)S(1)} %stack.349), channel_id=1, replica_groups=mesh['blk'=8,'rep'=4] {'blk','rep'}, use_global_device_ids=true, to_apply=%region_0.1 | all-reduce | flops 9216 | bytes 73728 | tf_op jit(solution)/shard_map/psum | solution.py:1158
  588.1 3.2 collective-permute-done.57
  594.9 4.6 collective-permute-done.58
  603.2 12.3 %collective-permute-done.75 = bf16[8,24,1536]{2,1,0:T(8,128)(2,1)S(1)} collective-permute-done((bf16[8,24,1536]{2,1,0:T(8,128)(2,1)S(1)}, bf16[8,24,1536]{2,1,0:T(8,128)(2,1)S(1)}, u32[]{:S(2)}, u32[]{:S(2)}) %collective-permute-start.75) | collective-permute-done | bytes 589856 | tf_op jit(solution)/shard_map/ppermute | solution.py:821
  619.0 7.2 collective-permute-done.76
  628.1 12.7 %collective-permute-done.68 = bf16[8,24,1536]{2,1,0:T(8,128)(2,1)S(1)} collective-permute-done((bf16[8,24,1536]{2,1,0:T(8,128)(2,1)S(1)}, bf16[8,24,1536]{2,1,0:T(8,128)(2,1)S(1)}, u32[]{:S(2)}, u32[]{:S(2)}) %collective-permute-start.68) | collective-permute-done | bytes 589856 | tf_op jit(solution)/shard_map/ppermute | solution.py:821
  643.3 3.0 collective-permute-done.77
  646.4 2.6 collective-permute-start.78
  649.0 2.7 collective-permute-done.78
  654.9 3.8 collective-permute-done.79
  670.0 3.4 collective-permute-done.71
  674.4 27.6 %collective-permute-done.72 = bf16[24,1536]{1,0:T(8,128)(2,1)S(1)} collective-permute-done((bf16[24,1536]{1,0:T(8,128)(2,1)S(1)}, bf16[24,1536]{1,0:T(8,128)(2,1)S(1)}, u32[]{:S(2)}, u32[]{:S(2)}) %collective-permute-start.72) | collective-permute-done | bytes 73760 | tf_op jit(solution)/shard_map/ppermute | solution.py:821
  708.1 11.0 %collective-permute-done.62 = bf16[2,2,24,2304]{3,2,0,1:T(8,128)(2,1)S(1)} collective-permute-done((bf16[2,2,24,2304]{3,2,0,1:T(8,128)(2,1)S(1)}, bf16[2,2,24,2304]{3,2,0,1:T(8,128)(2,1)S(1)}, u32[]{:S(2)}, u32[]{:S(2)}) %collective-permute-start.62) | collective-permute-done | bytes 442400 | tf_op jit(solution)/shard_map/ppermute | solution.py:821
  722.7 3.6 collective-permute-done.63
  728.6 3.4 collective-permute-done.50
  733.0 23.9 %collective-permute-done.82 = bf16[8,24,3072]{2,1,0:T(8,128)(2,1)S(1)} collective-permute-done((bf16[8,24,3072]{2,1,0:T(8,128)(2,1)S(1)}, bf16[8,24,3072]{2,1,0:T(8,128)(2,1)S(1)}, u32[]{:S(2)}, u32[]{:S(2)}) %collective-permute-start.82) | collective-permute-done | bytes 1179680 | tf_op jit(solution)/shard_map/ppermute | solution.py:821
  759.4 2.6 collective-permute-done.65
  764.3 7.4 collective-permute-done.95
  774.9 6.7 collective-permute-done.96
  782.8 3.9 collective-permute-done.97
  787.8 3.3 collective-permute-done.84
  791.2 2.9 collective-permute-start.85
  794.1 6.6 collective-permute-done.53
  806.6 2.8 collective-permute-done.86
  (424 shorter events, 149.0 us)
Async XLA Ops:
  84.8 87.6 %collective-permute-start.7 = (f32[112,128]{1,0:T(8,128)}, f32[112,128]{1,0:T(8,128)S(1)}, u32[]{:S(2)}, u32[]{:S(2)}) collective-permute-start(f32[112,128]{1,0:T(8,128)} %get-tuple-element.104), channel_id=1, source_target_pairs={{0,4},{4,0},{8,12},{12,8},{16,20},{20,16},{24,28},{28,24},{1,5},{5... | collective-permute-start | bytes 172040 | tf_op jit(solution)/shard_map/ppermute | solution.py:821
  87.8 88.3 %collective-permute-start.8 = (f32[112,128]{1,0:T(8,128)}, f32[112,128]{1,0:T(8,128)S(1)}, u32[]{:S(2)}, u32[]{:S(2)}) collective-permute-start(f32[112,128]{1,0:T(8,128)} %get-tuple-element.105), channel_id=1, source_target_pairs={{0,8},{4,12},{8,0},{12,4},{16,24},{20,28},{24,16},{28,20},{1,9},{5... | collective-permute-start | bytes 172040 | tf_op jit(solution)/shard_map/ppermute | solution.py:821
  89.4 86.8 %collective-permute-start.9 = (f32[112,128]{1,0:T(8,128)}, f32[112,128]{1,0:T(8,128)S(1)}, u32[]{:S(2)}, u32[]{:S(2)}) collective-permute-start(f32[112,128]{1,0:T(8,128)} %get-tuple-element.106), channel_id=1, source_target_pairs={{0,12},{4,8},{8,4},{12,0},{16,28},{20,24},{24,20},{28,16},{1,13},{... | collective-permute-start | bytes 172040 | tf_op jit(solution)/shard_map/ppermute | solution.py:821
  89.4 89.1 %collective-permute-start.10 = (f32[112,128]{1,0:T(8,128)}, f32[112,128]{1,0:T(8,128)S(1)}, u32[]{:S(2)}, u32[]{:S(2)}) collective-permute-start(f32[112,128]{1,0:T(8,128)} %get-tuple-element.107), channel_id=1, source_target_pairs={{0,16},{4,20},{8,24},{12,28},{16,0},{20,4},{24,8},{28,12},{1,17},{... | collective-permute-start | bytes 172040 | tf_op jit(solution)/shard_map/ppermute | solution.py:821
  92.4 89.1 %collective-permute-start.11 = (f32[112,128]{1,0:T(8,128)}, f32[112,128]{1,0:T(8,128)S(1)}, u32[]{:S(2)}, u32[]{:S(2)}) collective-permute-start(f32[112,128]{1,0:T(8,128)} %get-tuple-element.108), channel_id=1, source_target_pairs={{0,20},{4,16},{8,28},{12,24},{16,4},{20,0},{24,12},{28,8},{1,21},{... | collective-permute-start | bytes 172040 | tf_op jit(solution)/shard_map/ppermute | solution.py:821
  181.5 14.6 %collective-permute-start.2 = (bf16[112,768]{1,0:T(8,128)(2,1)S(1)}, bf16[112,768]{1,0:T(8,128)(2,1)S(1)}, u32[]{:S(2)}, u32[]{:S(2)}) collective-permute-start(bf16[112,768]{1,0:T(8,128)(2,1)S(1)} %copy-done.30), channel_id=1, source_target_pairs={{0,12},{4,8},{8,4},{12,0},{16,28},{20,24},{24,20},{28,16},{1,13},{... | collective-permute-start | bytes 516104 | tf_op jit(solution)/shard_map/ppermute | solution.py:821
  183.4 22.9 %collective-permute-start.3 = (bf16[112,768]{1,0:T(8,128)(2,1)S(1)}, bf16[112,768]{1,0:T(8,128)(2,1)S(1)}, u32[]{:S(2)}, u32[]{:S(2)}) collective-permute-start(bf16[112,768]{1,0:T(8,128)(2,1)S(1)} %copy-done.28), channel_id=1, source_target_pairs={{0,16},{4,20},{8,24},{12,28},{16,0},{20,4},{24,8},{28,12},{1,17},{... | collective-permute-start | bytes 516104 | tf_op jit(solution)/shard_map/ppermute | solution.py:821
  185.8 24.3 %collective-permute-start.4 = (bf16[112,768]{1,0:T(8,128)(2,1)S(1)}, bf16[112,768]{1,0:T(8,128)(2,1)S(1)}, u32[]{:S(2)}, u32[]{:S(2)}) collective-permute-start(bf16[112,768]{1,0:T(8,128)(2,1)S(1)} %copy-done.27), channel_id=1, source_target_pairs={{0,20},{4,16},{8,28},{12,24},{16,4},{20,0},{24,12},{28,8},{1,21},{... | collective-permute-start | bytes 516104 | tf_op jit(solution)/shard_map/ppermute | solution.py:821
  187.6 22.6 %collective-permute-start.5 = (bf16[112,768]{1,0:T(8,128)(2,1)S(1)}, bf16[112,768]{1,0:T(8,128)(2,1)S(1)}, u32[]{:S(2)}, u32[]{:S(2)}) collective-permute-start(bf16[112,768]{1,0:T(8,128)(2,1)S(1)} %copy-done.25), channel_id=1, source_target_pairs={{0,24},{4,28},{8,16},{12,20},{16,8},{20,12},{24,0},{28,4},{1,25},{... | collective-permute-start | bytes 516104 | tf_op jit(solution)/shard_map/ppermute | solution.py:821
  191.2 19.0 %collective-permute-start.6 = (bf16[112,768]{1,0:T(8,128)(2,1)S(1)}, bf16[112,768]{1,0:T(8,128)(2,1)S(1)}, u32[]{:S(2)}, u32[]{:S(2)}) collective-permute-start(bf16[112,768]{1,0:T(8,128)(2,1)S(1)} %copy-done.24), channel_id=1, source_target_pairs={{0,28},{4,24},{8,20},{12,16},{16,12},{20,8},{24,4},{28,0},{1,29},{... | collective-permute-start | bytes 516104 | tf_op jit(solution)/shard_map/ppermute | solution.py:821
  216.7 17.5 %collective-permute-start.26 = (f32[112,128]{1,0:T(8,128)}, f32[112,128]{1,0:T(8,128)}, u32[]{:S(2)}, u32[]{:S(2)}) collective-permute-start(f32[112,128]{1,0:T(8,128)} %get-tuple-element.123.rest_0_), channel_id=1, source_target_pairs={{0,24},{4,28},{8,16},{12,20},{16,8},{20,12},{24,0},{28,4},{1,25},{... | collective-permute-start | bytes 172040 | tf_op jit(solution)/shard_map/ppermute | solution.py:821
  218.6 17.8 %collective-permute-start.20 = (bf16[112,768]{1,0:T(8,128)(2,1)}, bf16[112,768]{1,0:T(8,128)(2,1)S(1)}, u32[]{:S(2)}, u32[]{:S(2)}) collective-permute-start(bf16[112,768]{1,0:T(8,128)(2,1)} %get-tuple-element.111.rest_0_), channel_id=1, source_target_pairs={{0,28},{4,24},{8,20},{12,16},{16,12},{20,8},{24,4},{28,0},{1,29},{... | collective-permute-start | bytes 516104 | tf_op jit(solution)/shard_map/ppermute | solution.py:821
  220.6 20.8 %collective-permute-start.19 = (bf16[112,768]{1,0:T(8,128)(2,1)}, bf16[112,768]{1,0:T(8,128)(2,1)S(1)}, u32[]{:S(2)}, u32[]{:S(2)}) collective-permute-start(bf16[112,768]{1,0:T(8,128)(2,1)} %get-tuple-element.111.rest_0_), channel_id=1, source_target_pairs={{0,24},{4,28},{8,16},{12,20},{16,8},{20,12},{24,0},{28,4},{1,25},{... | collective-permute-start | bytes 516104 | tf_op jit(solution)/shard_map/ppermute | solution.py:821
  223.5 25.2 %collective-permute-start.18 = (bf16[112,768]{1,0:T(8,128)(2,1)}, bf16[112,768]{1,0:T(8,128)(2,1)S(1)}, u32[]{:S(2)}, u32[]{:S(2)}) collective-permute-start(bf16[112,768]{1,0:T(8,128)(2,1)} %get-tuple-element.111.rest_0_), channel_id=1, source_target_pairs={{0,20},{4,16},{8,28},{12,24},{16,4},{20,0},{24,12},{28,8},{1,21},{... | collective-permute-start | bytes 516104 | tf_op jit(solution)/shard_map/ppermute | solution.py:821
  227.4 26.9 %collective-permute-start.17 = (bf16[112,768]{1,0:T(8,128)(2,1)}, bf16[112,768]{1,0:T(8,128)(2,1)S(1)}, u32[]{:S(2)}, u32[]{:S(2)}) collective-permute-start(bf16[112,768]{1,0:T(8,128)(2,1)} %get-tuple-element.111.rest_0_), channel_id=1, source_target_pairs={{0,16},{4,20},{8,24},{12,28},{16,0},{20,4},{24,8},{28,12},{1,17},{... | collective-permute-start | bytes 516104 | tf_op jit(solution)/shard_map/ppermute | solution.py:821
  234.2 20.2 %collective-permute-start.16 = (bf16[112,768]{1,0:T(8,128)(2,1)}, bf16[112,768]{1,0:T(8,128)(2,1)S(1)}, u32[]{:S(2)}, u32[]{:S(2)}) collective-permute-start(bf16[112,768]{1,0:T(8,128)(2,1)} %get-tuple-element.111.rest_0_), channel_id=1, source_target_pairs={{0,12},{4,8},{8,4},{12,0},{16,28},{20,24},{24,20},{28,16},{1,13},{... | collective-permute-start | bytes 516104 | tf_op jit(solution)/shard_map/ppermute | solution.py:821
  236.4 19.5 %collective-permute-start.15 = (bf16[112,768]{1,0:T(8,128)(2,1)}, bf16[112,768]{1,0:T(8,128)(2,1)S(1)}, u32[]{:S(2)}, u32[]{:S(2)}) collective-permute-start(bf16[112,768]{1,0:T(8,128)(2,1)} %get-tuple-element.111.rest_0_), channel_id=1, source_target_pairs={{0,8},{4,12},{8,0},{12,4},{16,24},{20,28},{24,16},{28,20},{1,9},{5... | collective-permute-start | bytes 516104 | tf_op jit(solution)/shard_map/ppermute | solution.py:821
  241.4 15.1 %collective-permute-start.14 = (bf16[112,768]{1,0:T(8,128)(2,1)}, bf16[112,768]{1,0:T(8,128)(2,1)}, u32[]{:S(2)}, u32[]{:S(2)}) collective-permute-start(bf16[112,768]{1,0:T(8,128)(2,1)} %get-tuple-element.111.rest_0_), channel_id=1, source_target_pairs={{0,4},{4,0},{8,12},{12,8},{16,20},{20,16},{24,28},{28,24},{1,5},{5... | collective-permute-start | bytes 516104 | tf_op jit(solution)/shard_map/ppermute | solution.py:821
  248.7 51.5 %collective-permute-start.25 = (f32[112,128]{1,0:T(8,128)S(1)}, f32[112,128]{1,0:T(8,128)S(1)}, u32[]{:S(2)}, u32[]{:S(2)}) collective-permute-start(f32[112,128]{1,0:T(8,128)S(1)} %copy-done.51), channel_id=1, source_target_pairs={{0,20},{4,16},{8,28},{12,24},{16,4},{20,0},{24,12},{28,8},{1,21},{... | collective-permute-start | bytes 172040 | tf_op jit(solution)/shard_map/ppermute | solution.py:821
  254.3 46.5 %collective-permute-start.24 = (f32[112,128]{1,0:T(8,128)S(1)}, f32[112,128]{1,0:T(8,128)S(1)}, u32[]{:S(2)}, u32[]{:S(2)}) collective-permute-start(f32[112,128]{1,0:T(8,128)S(1)} %copy-done.51), channel_id=1, source_target_pairs={{0,16},{4,20},{8,24},{12,28},{16,0},{20,4},{24,8},{28,12},{1,17},{... | collective-permute-start | bytes 172040 | tf_op jit(solution)/shard_map/ppermute | solution.py:821
  254.3 48.0 %collective-permute-start.23 = (f32[112,128]{1,0:T(8,128)S(1)}, f32[112,128]{1,0:T(8,128)S(1)}, u32[]{:S(2)}, u32[]{:S(2)}) collective-permute-start(f32[112,128]{1,0:T(8,128)S(1)} %copy-done.51), channel_id=1, source_target_pairs={{0,12},{4,8},{8,4},{12,0},{16,28},{20,24},{24,20},{28,16},{1,13},{... | collective-permute-start | bytes 172040 | tf_op jit(solution)/shard_map/ppermute | solution.py:821
  255.9 47.9 %collective-permute-start.22 = (f32[112,128]{1,0:T(8,128)S(1)}, f32[112,128]{1,0:T(8,128)S(1)}, u32[]{:S(2)}, u32[]{:S(2)}) collective-permute-start(f32[112,128]{1,0:T(8,128)S(1)} %copy-done.51), channel_id=1, source_target_pairs={{0,8},{4,12},{8,0},{12,4},{16,24},{20,28},{24,16},{28,20},{1,9},{5... | collective-permute-start | bytes 172040 | tf_op jit(solution)/shard_map/ppermute | solution.py:821
  256.5 50.2 %collective-permute-start.21 = (f32[112,128]{1,0:T(8,128)S(1)}, f32[112,128]{1,0:T(8,128)S(1)}, u32[]{:S(2)}, u32[]{:S(2)}) collective-permute-start(f32[112,128]{1,0:T(8,128)S(1)} %copy-done.51), channel_id=1, source_target_pairs={{0,4},{4,0},{8,12},{12,8},{16,20},{20,16},{24,28},{28,24},{1,5},{5... | collective-permute-start | bytes 172040 | tf_op jit(solution)/shard_map/ppermute | solution.py:821
  300.3 83.9 %collective-permute-start.35 = (bf16[112,1536]{1,0:T(8,128)(2,1)}, bf16[112,1536]{1,0:T(8,128)(2,1)S(1)}, u32[]{:S(2)}, u32[]{:S(2)}) collective-permute-start(bf16[112,1536]{1,0:T(8,128)(2,1)} %get-tuple-element.140), channel_id=1, source_target_pairs={{0,4},{4,0},{8,12},{12,8},{16,20},{20,16},{24,28},{28,24},{1,5},{5... | collective-permute-start | bytes 1032200 | tf_op jit(solution)/shard_map/ppermute | solution.py:821
  300.9 85.3 %collective-permute-start.36 = (bf16[112,1536]{1,0:T(8,128)(2,1)}, bf16[112,1536]{1,0:T(8,128)(2,1)}, u32[]{:S(2)}, u32[]{:S(2)}) collective-permute-start(bf16[112,1536]{1,0:T(8,128)(2,1)} %get-tuple-element.141), channel_id=1, source_target_pairs={{0,8},{4,12},{8,0},{12,4},{16,24},{20,28},{24,16},{28,20},{1,9},{5... | collective-permute-start | bytes 1032200 | tf_op jit(solution)/shard_map/ppermute | solution.py:821
  302.3 86.2 %collective-permute-start.37 = (bf16[112,1536]{1,0:T(8,128)(2,1)}, bf16[112,1536]{1,0:T(8,128)(2,1)}, u32[]{:S(2)}, u32[]{:S(2)}) collective-permute-start(bf16[112,1536]{1,0:T(8,128)(2,1)} %get-tuple-element.142), channel_id=1, source_target_pairs={{0,12},{4,8},{8,4},{12,0},{16,28},{20,24},{24,20},{28,16},{1,13},{... | collective-permute-start | bytes 1032200 | tf_op jit(solution)/shard_map/ppermute | solution.py:821
  303.8 85.8 %collective-permute-start.38 = (bf16[112,1536]{1,0:T(8,128)(2,1)}, bf16[112,1536]{1,0:T(8,128)(2,1)}, u32[]{:S(2)}, u32[]{:S(2)}) collective-permute-start(bf16[112,1536]{1,0:T(8,128)(2,1)} %get-tuple-element.143), channel_id=1, source_target_pairs={{0,16},{4,20},{8,24},{12,28},{16,0},{20,4},{24,8},{28,12},{1,17},{... | collective-permute-start | bytes 1032200 | tf_op jit(solution)/shard_map/ppermute | solution.py:821
  306.6 83.9 %collective-permute-start.39 = (bf16[112,1536]{1,0:T(8,128)(2,1)}, bf16[112,1536]{1,0:T(8,128)(2,1)}, u32[]{:S(2)}, u32[]{:S(2)}) collective-permute-start(bf16[112,1536]{1,0:T(8,128)(2,1)} %get-tuple-element.144), channel_id=1, source_target_pairs={{0,20},{4,16},{8,28},{12,24},{16,4},{20,0},{24,12},{28,8},{1,21},{... | collective-permute-start | bytes 1032200 | tf_op jit(solution)/shard_map/ppermute | solution.py:821
  386.2 23.3 %collective-permute-start.41 = (bf16[112,1536]{1,0:T(8,128)(2,1)S(1)}, bf16[112,1536]{1,0:T(8,128)(2,1)S(1)}, u32[]{:S(2)}, u32[]{:S(2)}) collective-permute-start(bf16[112,1536]{1,0:T(8,128)(2,1)S(1)} %copy-done.19), channel_id=1, source_target_pairs={{0,28},{4,24},{8,20},{12,16},{16,12},{20,8},{24,4},{28,0},{1,29},{... | collective-permute-start | bytes 1032200 | tf_op jit(solution)/shard_map/ppermute | solution.py:821
  388.6 33.3 %collective-permute-start.28 = (bf16[112,768]{1,0:T(8,128)(2,1)S(1)}, bf16[112,768]{1,0:T(8,128)(2,1)S(1)}, u32[]{:S(2)}, u32[]{:S(2)}) collective-permute-start(bf16[112,768]{1,0:T(8,128)(2,1)S(1)} %copy-done.36), channel_id=1, source_target_pairs={{0,4},{4,0},{8,12},{12,8},{16,20},{20,16},{24,28},{28,24},{1,5},{5... | collective-permute-start | bytes 516104 | tf_op jit(solution)/shard_map/ppermute | solution.py:821
  389.7 33.4 %collective-permute-start.29 = (bf16[112,768]{1,0:T(8,128)(2,1)S(1)}, bf16[112,768]{1,0:T(8,128)(2,1)S(1)}, u32[]{:S(2)}, u32[]{:S(2)}) collective-permute-start(bf16[112,768]{1,0:T(8,128)(2,1)S(1)} %copy-done.35), channel_id=1, source_target_pairs={{0,8},{4,12},{8,0},{12,4},{16,24},{20,28},{24,16},{28,20},{1,9},{5... | collective-permute-start | bytes 516104 | tf_op jit(solution)/shard_map/ppermute | solution.py:821
  390.5 42.2 %collective-permute-start.30 = (bf16[112,768]{1,0:T(8,128)(2,1)}, bf16[112,768]{1,0:T(8,128)(2,1)}, u32[]{:S(2)}, u32[]{:S(2)}) collective-permute-start(bf16[112,768]{1,0:T(8,128)(2,1)} %get-tuple-element.134), channel_id=1, source_target_pairs={{0,12},{4,8},{8,4},{12,0},{16,28},{20,24},{24,20},{28,16},{1,13},{... | collective-permute-start | bytes 516104 | tf_op jit(solution)/shard_map/ppermute | solution.py:821
  397.2 35.6 %collective-permute-start.31 = (bf16[112,768]{1,0:T(8,128)(2,1)}, bf16[112,768]{1,0:T(8,128)(2,1)}, u32[]{:S(2)}, u32[]{:S(2)}) collective-permute-start(bf16[112,768]{1,0:T(8,128)(2,1)} %get-tuple-element.135), channel_id=1, source_target_pairs={{0,16},{4,20},{8,24},{12,28},{16,0},{20,4},{24,8},{28,12},{1,17},{... | collective-permute-start | bytes 516104 | tf_op jit(solution)/shard_map/ppermute | solution.py:821
  409.5 29.4 %collective-permute-start.32 = (bf16[112,768]{1,0:T(8,128)(2,1)}, bf16[112,768]{1,0:T(8,128)(2,1)}, u32[]{:S(2)}, u32[]{:S(2)}) collective-permute-start(bf16[112,768]{1,0:T(8,128)(2,1)} %get-tuple-element.136), channel_id=1, source_target_pairs={{0,20},{4,16},{8,28},{12,24},{16,4},{20,0},{24,12},{28,8},{1,21},{... | collective-permute-start | bytes 516104 | tf_op jit(solution)/shard_map/ppermute | solution.py:821
  421.9 17.0 %collective-permute-start.33 = (bf16[112,768]{1,0:T(8,128)(2,1)}, bf16[112,768]{1,0:T(8,128)(2,1)}, u32[]{:S(2)}, u32[]{:S(2)}) collective-permute-start(bf16[112,768]{1,0:T(8,128)(2,1)} %get-tuple-element.137), channel_id=1, source_target_pairs={{0,24},{4,28},{8,16},{12,20},{16,8},{20,12},{24,0},{28,4},{1,25},{... | collective-permute-start | bytes 516104 | tf_op jit(solution)/shard_map/ppermute | solution.py:821
  423.1 15.8 %collective-permute-start.34 = (bf16[112,768]{1,0:T(8,128)(2,1)}, bf16[112,768]{1,0:T(8,128)(2,1)}, u32[]{:S(2)}, u32[]{:S(2)}) collective-permute-start(bf16[112,768]{1,0:T(8,128)(2,1)} %get-tuple-element.138), channel_id=1, source_target_pairs={{0,28},{4,24},{8,20},{12,16},{16,12},{20,8},{24,4},{28,0},{1,29},{... | collective-permute-start | bytes 516104 | tf_op jit(solution)/shard_map/ppermute | solution.py:821
  432.8 26.8 %collective-permute-start.99 = (bf16[2,96,768]{2,1,0:T(8,128)(2,1)S(1)}, bf16[2,96,768]{2,1,0:T(8,128)(2,1)S(1)}, u32[]{:S(2)}, u32[]{:S(2)}) collective-permute-start(bf16[2,96,768]{2,1,0:T(8,128)(2,1)S(1)} %dynamic-slice_bitcast_fusion.4), channel_id=1, source_target_pairs={{0,1},{1,0},{2,3},{3,2},{4,5},{5,4},{6,7},{7,6},{8,9},{9,8},{10,11... | collective-permute-start | bytes 884744 | tf_op jit(solution)/shard_map/ppermute | solution.py:821
  432.9 26.5 %collective-permute-start.88 = (bf16[2,24,3072]{2,1,0:T(8,128)(2,1)S(1)}, bf16[2,24,3072]{2,1,0:T(8,128)(2,1)S(1)}, u32[]{:S(2)}, u32[]{:S(2)}) collective-permute-start(bf16[2,24,3072]{2,1,0:T(8,128)(2,1)S(1)} %copy-done.14), channel_id=1, source_target_pairs={{0,1},{1,0},{2,3},{3,2},{4,5},{5,4},{6,7},{7,6},{8,9},{9,8},{10,11... | collective-permute-start | bytes 884744 | tf_op jit(solution)/shard_map/ppermute | solution.py:821
  445.4 15.9 %collective-permute-start.48 = (bf16[112,768]{1,0:T(8,128)(2,1)}, bf16[112,768]{1,0:T(8,128)(2,1)S(1)}, u32[]{:S(2)}, u32[]{:S(2)}) collective-permute-start(bf16[112,768]{1,0:T(8,128)(2,1)} %get-tuple-element.147.rest_0_), channel_id=1, source_target_pairs={{0,28},{4,24},{8,20},{12,16},{16,12},{20,8},{24,4},{28,0},{1,29},{... | collective-permute-start | bytes 516104 | tf_op jit(solution)/shard_map/ppermute | solution.py:821
  447.9 21.3 %collective-permute-start.47 = (bf16[112,768]{1,0:T(8,128)(2,1)}, bf16[112,768]{1,0:T(8,128)(2,1)S(1)}, u32[]{:S(2)}, u32[]{:S(2)}) collective-permute-start(bf16[112,768]{1,0:T(8,128)(2,1)} %get-tuple-element.147.rest_0_), channel_id=1, source_target_pairs={{0,24},{4,28},{8,16},{12,20},{16,8},{20,12},{24,0},{28,4},{1,25},{... | collective-permute-start | bytes 516104 | tf_op jit(solution)/shard_map/ppermute | solution.py:821
  448.0 27.2 %collective-permute-start.46 = (bf16[112,768]{1,0:T(8,128)(2,1)}, bf16[112,768]{1,0:T(8,128)(2,1)S(1)}, u32[]{:S(2)}, u32[]{:S(2)}) collective-permute-start(bf16[112,768]{1,0:T(8,128)(2,1)} %get-tuple-element.147.rest_0_), channel_id=1, source_target_pairs={{0,20},{4,16},{8,28},{12,24},{16,4},{20,0},{24,12},{28,8},{1,21},{... | collective-permute-start | bytes 516104 | tf_op jit(solution)/shard_map/ppermute | solution.py:821
  459.3 18.1 %collective-permute-start.45 = (bf16[112,768]{1,0:T(8,128)(2,1)S(1)}, bf16[112,768]{1,0:T(8,128)(2,1)S(1)}, u32[]{:S(2)}, u32[]{:S(2)}) collective-permute-start(bf16[112,768]{1,0:T(8,128)(2,1)S(1)} %copy-done.34), channel_id=1, source_target_pairs={{0,16},{4,20},{8,24},{12,28},{16,0},{20,4},{24,8},{28,12},{1,17},{... | collective-permute-start | bytes 516104 | tf_op jit(solution)/shard_map/ppermute | solution.py:821
  459.5 17.9 %collective-permute-start.44 = (bf16[112,768]{1,0:T(8,128)(2,1)S(1)}, bf16[112,768]{1,0:T(8,128)(2,1)S(1)}, u32[]{:S(2)}, u32[]{:S(2)}) collective-permute-start(bf16[112,768]{1,0:T(8,128)(2,1)S(1)} %copy-done.34), channel_id=1, source_target_pairs={{0,12},{4,8},{8,4},{12,0},{16,28},{20,24},{24,20},{28,16},{1,13},{... | collective-permute-start | bytes 516104 | tf_op jit(solution)/shard_map/ppermute | solution.py:821
  461.3 19.4 %collective-permute-start.43 = (bf16[112,768]{1,0:T(8,128)(2,1)S(1)}, bf16[112,768]{1,0:T(8,128)(2,1)S(1)}, u32[]{:S(2)}, u32[]{:S(2)}) collective-permute-start(bf16[112,768]{1,0:T(8,128)(2,1)S(1)} %copy-done.34), channel_id=1, source_target_pairs={{0,8},{4,12},{8,0},{12,4},{16,24},{20,28},{24,16},{28,20},{1,9},{5... | collective-permute-start | bytes 516104 | tf_op jit(solution)/shard_map/ppermute | solution.py:821
  475.1 109.4 %collective-permute-start.74 = (bf16[8,2,24,1536]{3,2,1,0:T(8,128)(2,1)}, bf16[8,2,24,1536]{3,2,1,0:T(8,128)(2,1)}, u32[]{:S(2)}, u32[]{:S(2)}) collective-permute-start(bf16[8,2,24,1536]{3,2,1,0:T(8,128)(2,1)} %dynamic-slice_bitcast_fusion.1), channel_id=1, source_target_pairs={{0,1},{1,0},{2,3},{3,2},{4,5},{5,4},{6,7},{7,6},{8,9},{9,8},{10,11... | collective-permute-start | bytes 3538952 | tf_op jit(solution)/shard_map/ppermute | solution.py:821
  477.4 182.4 %collective-permute-start.92 = (bf16[8,2,96,768]{3,2,0,1:T(8,128)(2,1)}, bf16[8,2,96,768]{3,2,0,1:T(8,128)(2,1)}, u32[]{:S(2)}, u32[]{:S(2)}) collective-permute-start(bf16[8,2,96,768]{3,2,0,1:T(8,128)(2,1)} %bitcast.273), channel_id=1, source_target_pairs={{0,1},{1,0},{2,3},{3,2},{4,5},{5,4},{6,7},{7,6},{8,9},{9,8},{10,11... | collective-permute-start | bytes 7077896 | tf_op jit(solution)/shard_map/ppermute | solution.py:821
  477.4 122.3 %collective-permute-start.67 = (bf16[8,2,24,1536]{3,2,1,0:T(8,128)(2,1)}, bf16[8,2,24,1536]{3,2,1,0:T(8,128)(2,1)}, u32[]{:S(2)}, u32[]{:S(2)}) collective-permute-start(bf16[8,2,24,1536]{3,2,1,0:T(8,128)(2,1)} %dynamic-slice_bitcast_fusion.2), channel_id=1, source_target_pairs={{0,1},{1,0},{2,3},{3,2},{4,5},{5,4},{6,7},{7,6},{8,9},{9,8},{10,11... | collective-permute-start | bytes 3538952 | tf_op jit(solution)/shard_map/ppermute | solution.py:821
  480.7 90.0 %collective-permute-start.100 = (bf16[96,768]{1,0:T(8,128)(2,1)S(1)}, bf16[96,768]{1,0:T(8,128)(2,1)S(1)}, u32[]{:S(2)}, u32[]{:S(2)}) collective-permute-start(bf16[96,768]{1,0:T(8,128)(2,1)S(1)} %fusion.30), channel_id=1, source_target_pairs={{0,2},{1,3},{2,0},{3,1},{4,6},{5,7},{6,4},{7,5},{8,10},{9,11},{10,... | collective-permute-start | bytes 442376 | tf_op jit(solution)/shard_map/ppermute | solution.py:821
  483.1 90.5 %collective-permute-start.89 = (bf16[24,3072]{1,0:T(8,128)(2,1)S(1)}, bf16[24,3072]{1,0:T(8,128)(2,1)S(1)}, u32[]{:S(2)}, u32[]{:S(2)}) collective-permute-start(bf16[24,3072]{1,0:T(8,128)(2,1)S(1)} %fusion.28), channel_id=1, source_target_pairs={{0,2},{1,3},{2,0},{3,1},{4,6},{5,7},{6,4},{7,5},{8,10},{9,11},{10,... | collective-permute-start | bytes 442376 | tf_op jit(solution)/shard_map/ppermute | solution.py:821
  578.2 123.9 %collective-permute-start.49 = (bf16[8,2,24,3072]{3,2,0,1:T(8,128)(2,1)}, bf16[8,2,24,3072]{3,2,0,1:T(8,128)(2,1)S(1)}, u32[]{:S(2)}, u32[]{:S(2)}) collective-permute-start(bf16[8,2,24,3072]{3,2,0,1:T(8,128)(2,1)} %bitcast.308), channel_id=1, source_target_pairs={{0,1},{1,0},{2,3},{3,2},{4,5},{5,4},{6,7},{7,6},{8,9},{9,8},{10,11... | collective-permute-start | bytes 7077896 | tf_op jit(solution)/shard_map/ppermute | solution.py:821
  594.7 109.3 %collective-permute-start.81 = (bf16[8,2,24,3072]{3,2,0,1:T(8,128)(2,1)S(1)}, bf16[8,2,24,3072]{3,2,0,1:T(8,128)(2,1)S(1)}, u32[]{:S(2)}, u32[]{:S(2)}) collective-permute-start(bf16[8,2,24,3072]{3,2,0,1:T(8,128)(2,1)S(1)} %bitcast.307), channel_id=1, source_target_pairs={{0,1},{1,0},{2,3},{3,2},{4,5},{5,4},{6,7},{7,6},{8,9},{9,8},{10,11... | collective-permute-start | bytes 7077896 | tf_op jit(solution)/shard_map/ppermute | solution.py:821
  599.6 53.9 %collective-permute-start.60 = (bf16[8,2,24,2304]{3,2,1,0:T(8,128)(2,1)S(1)}, bf16[8,2,24,2304]{3,2,1,0:T(8,128)(2,1)S(1)}, u32[]{:S(2)}, u32[]{:S(2)}) collective-permute-start(bf16[8,2,24,2304]{3,2,1,0:T(8,128)(2,1)S(1)} %copy-done.8), channel_id=1, source_target_pairs={{0,1},{1,0},{2,3},{3,2},{4,5},{5,4},{6,7},{7,6},{8,9},{9,8},{10,11... | collective-permute-start | bytes 5308424 | tf_op jit(solution)/shard_map/ppermute | solution.py:821
  599.7 15.8 %collective-permute-start.75 = (bf16[8,24,1536]{2,1,0:T(8,128)(2,1)S(1)}, bf16[8,24,1536]{2,1,0:T(8,128)(2,1)S(1)}, u32[]{:S(2)}, u32[]{:S(2)}) collective-permute-start(bf16[8,24,1536]{2,1,0:T(8,128)(2,1)S(1)} %fusion.6), channel_id=1, source_target_pairs={{0,2},{1,3},{2,0},{3,1},{4,6},{5,7},{6,4},{7,5},{8,10},{9,11},{10,... | collective-permute-start | bytes 1769480 | tf_op jit(solution)/shard_map/ppermute | solution.py:821
  626.2 14.5 %collective-permute-start.68 = (bf16[8,24,1536]{2,1,0:T(8,128)(2,1)S(1)}, bf16[8,24,1536]{2,1,0:T(8,128)(2,1)S(1)}, u32[]{:S(2)}, u32[]{:S(2)}) collective-permute-start(bf16[8,24,1536]{2,1,0:T(8,128)(2,1)S(1)} %fusion.5), channel_id=1, source_target_pairs={{0,2},{1,3},{2,0},{3,1},{4,6},{5,7},{6,4},{7,5},{8,10},{9,11},{10,... | collective-permute-start | bytes 1769480 | tf_op jit(solution)/shard_map/ppermute | solution.py:821
  658.7 47.9 %collective-permute-start.61 = (bf16[8,24,2304]{2,1,0:T(8,128)(2,1)S(1)}, bf16[8,24,2304]{2,1,0:T(8,128)(2,1)S(1)}, u32[]{:S(2)}, u32[]{:S(2)}) collective-permute-start(bf16[8,24,2304]{2,1,0:T(8,128)(2,1)S(1)} %fusion.3), channel_id=1, source_target_pairs={{0,2},{1,3},{2,0},{3,1},{4,6},{5,7},{6,4},{7,5},{8,10},{9,11},{10,... | collective-permute-start | bytes 2654216 | tf_op jit(solution)/shard_map/ppermute | solution.py:821
  666.4 54.8 %collective-permute-start.93 = (bf16[8,96,768]{2,1,0:T(8,128)(2,1)S(1)}, bf16[8,96,768]{2,1,0:T(8,128)(2,1)S(1)}, u32[]{:S(2)}, u32[]{:S(2)}) collective-permute-start(bf16[8,96,768]{2,1,0:T(8,128)(2,1)S(1)} %fusion.2), channel_id=1, source_target_pairs={{0,2},{1,3},{2,0},{3,1},{4,6},{5,7},{6,4},{7,5},{8,10},{9,11},{10,... | collective-permute-start | bytes 3538952 | tf_op jit(solution)/shard_map/ppermute | solution.py:821
  673.4 28.6 %collective-permute-start.72 = (bf16[24,1536]{1,0:T(8,128)(2,1)S(1)}, bf16[24,1536]{1,0:T(8,128)(2,1)S(1)}, u32[]{:S(2)}, u32[]{:S(2)}) collective-permute-start(bf16[24,1536]{1,0:T(8,128)(2,1)S(1)} %fusion.32), channel_id=1, source_target_pairs={{0,2},{1,3},{2,0},{3,1},{4,6},{5,7},{6,4},{7,5},{8,10},{9,11},{10,... | collective-permute-start | bytes 221192 | tf_op jit(solution)/shard_map/ppermute | solution.py:821
  703.1 28.8 %collective-permute-start.50 = (bf16[8,24,3072]{2,1,0:T(8,128)(2,1)S(1)}, bf16[8,24,3072]{2,1,0:T(8,128)(2,1)S(1)}, u32[]{:S(2)}, u32[]{:S(2)}) collective-permute-start(bf16[8,24,3072]{2,1,0:T(8,128)(2,1)S(1)} %fusion), channel_id=1, source_target_pairs={{0,2},{1,3},{2,0},{3,1},{4,6},{5,7},{6,4},{7,5},{8,10},{9,11},{10,... | collective-permute-start | bytes 3538952 | tf_op jit(solution)/shard_map/ppermute | solution.py:821
  705.7 51.2 %collective-permute-start.82 = (bf16[8,24,3072]{2,1,0:T(8,128)(2,1)S(1)}, bf16[8,24,3072]{2,1,0:T(8,128)(2,1)S(1)}, u32[]{:S(2)}, u32[]{:S(2)}) collective-permute-start(bf16[8,24,3072]{2,1,0:T(8,128)(2,1)S(1)} %fusion.1), channel_id=1, source_target_pairs={{0,2},{1,3},{2,0},{3,1},{4,6},{5,7},{6,4},{7,5},{8,10},{9,11},{10,... | collective-permute-start | bytes 3538952 | tf_op jit(solution)/shard_map/ppermute | solution.py:821
  721.6 40.5 %collective-permute-start.94 = (bf16[2,2,96,768]{3,2,1,0:T(8,128)(2,1)S(1)}, bf16[2,2,96,768]{3,2,1,0:T(8,128)(2,1)S(1)}, u32[]{:S(2)}, u32[]{:S(2)}) collective-permute-start(bf16[2,2,96,768]{3,2,1,0:T(8,128)(2,1)S(1)} %fusion.7), channel_id=1, source_target_pairs={{0,4},{4,0},{8,12},{12,8},{16,20},{20,16},{24,28},{28,24},{1,5},{5... | collective-permute-start | bytes 1769480 | tf_op jit(solution)/shard_map/ppermute | solution.py:821
  726.3 30.8 %collective-permute-start.64 = (bf16[24,2304]{1,0:T(8,128)(2,1)S(1)}, bf16[24,2304]{1,0:T(8,128)(2,1)S(1)}, u32[]{:S(2)}, u32[]{:S(2)}) collective-permute-start(bf16[24,2304]{1,0:T(8,128)(2,1)S(1)} %fusion.33), channel_id=1, source_target_pairs={{0,16},{4,20},{8,24},{12,28},{16,0},{20,4},{24,8},{28,12},{1,17},{... | collective-permute-start | bytes 331784 | tf_op jit(solution)/shard_map/ppermute | solution.py:821
  732.3 41.9 %collective-permute-start.51 = (bf16[2,2,24,3072]{3,2,1,0:T(8,128)(2,1)S(1)}, bf16[2,2,24,3072]{3,2,1,0:T(8,128)(2,1)S(1)}, u32[]{:S(2)}, u32[]{:S(2)}) collective-permute-start(bf16[2,2,24,3072]{3,2,1,0:T(8,128)(2,1)S(1)} %fusion.4), channel_id=1, source_target_pairs={{0,4},{4,0},{8,12},{12,8},{16,20},{20,16},{24,28},{28,24},{1,5},{5... | collective-permute-start | bytes 1769480 | tf_op jit(solution)/shard_map/ppermute | solution.py:821
  758.1 16.6 %collective-permute-start.83 = (bf16[2,2,24,3072]{3,2,0,1:T(8,128)(2,1)S(1)}, bf16[2,2,24,3072]{3,2,0,1:T(8,128)(2,1)S(1)}, u32[]{:S(2)}, u32[]{:S(2)}) collective-permute-start(bf16[2,2,24,3072]{3,2,0,1:T(8,128)(2,1)S(1)} %fusion.8), channel_id=1, source_target_pairs={{0,4},{4,0},{8,12},{12,8},{16,20},{20,16},{24,28},{28,24},{1,5},{5... | collective-permute-start | bytes 1769480 | tf_op jit(solution)/shard_map/ppermute | solution.py:821
  786.8 18.0 %collective-permute-start.98 = (bf16[2,96,768]{2,1,0:T(8,128)(2,1)S(1)}, bf16[2,96,768]{2,1,0:T(8,128)(2,1)S(1)}, u32[]{:S(2)}, u32[]{:S(2)}) collective-permute-start(bf16[2,96,768]{2,1,0:T(8,128)(2,1)S(1)} %maximum_select_fusion.18), channel_id=1, source_target_pairs={{0,1},{1,0},{2,3},{3,2},{4,5},{5,4},{6,7},{7,6},{8,9},{9,8},{10,11... | collective-permute-start | bytes 884744 | tf_op jit(solution)/shard_map/ppermute | solution.py:821
  (107 other events, 1100.0 us)

commit v3 on v2

--- a/solution.py
+++ b/solution.py
@@ -187,8 +187,24 @@
     return made
 
 
-def keep(scores):
-    return scores
+DIRECT = 8
+
+
+def place_of(axis="blk"):
+    return lax.axis_index(axis)
+
+
+def flipped(index, mask, count):
+    total, weight = 0, 1
+    while weight < count:
+        bit = (index // weight) % 2
+        total = total + weight * ((1 - bit) if mask & weight else bit)
+        weight *= 2
+    return total
+
+
+def piece_at(number, count):
+    return flipped(place_of(), number, count) if count <= DIRECT else number
 
 
 def window_forward(
@@ -326,7 +342,7 @@
     loop(2 * features // CHUNK, third)
 
 
-def cross_forward(pieces, order_ref, cq_ref, ckv_ref, valid_ref, *rest):
+def cross_forward(pieces, cq_ref, ckv_ref, valid_ref, *rest):
     out_refs, log_refs, (whole, logs) = rest[:pieces], rest[pieces : 2 * pieces], rest[2 * pieces :]
     rows, features = cq_ref.shape
     part = out_refs[0].shape[0]
@@ -349,8 +365,8 @@
 
     loop(features // PAIR, pair)
     for k in range(pieces):
-        out_refs[k][...] = whole[at(order_ref[k], part), :]
-        log_refs[k][...] = logs[at(order_ref[k], part), :]
+        out_refs[k][...] = whole[at(piece_at(k, pieces), part), :]
+        log_refs[k][...] = logs[at(piece_at(k, pieces), part), :]
 
 
 def merge_blocks(pieces, *refs):
@@ -463,7 +479,7 @@
 
 
 def query_feed_forward(
-    pieces, share, hidden_share, place_ref, order_ref, q1_ref, cot_ref, gain_ref, bias_ref,
+    pieces, share, hidden_share, q1_ref, cot_ref, gain_ref, bias_ref,
     w_out, up_ref, down_ref, *rest,
 ):
     parts, rest = rest[:pieces], rest[pieces:]
@@ -479,7 +495,7 @@
     @pl.when(step == 0)
     def begin():
         for k in range(pieces):
-            co_ref[at(order_ref[k], part), :] = parts[k][...]
+            co_ref[at(piece_at(k, pieces), part), :] = parts[k][...]
 
         def first(i):
             span = at(i, STRIP)
@@ -491,14 +507,14 @@
 
         loop(rows // STRIP, first)
         chosen[...] = right_t(
-            chooser(chosen.shape[0], features, place_ref[0] * share, share), normed[...]
+            chooser(chosen.shape[0], features, place_of() * share, share), normed[...]
         ).astype(NARROW)
 
     feed_forward_step(
         STRIP, normed, up_ref.at[0], down_ref.at[0], cot_ref, hidden, slope, out, grad
     )
     up_grad_ref[...] = plain(chosen[...], slope[...]).astype(NARROW)
-    begins = place_ref[0] * hidden_share
+    begins = place_of() * hidden_share
 
     @pl.when(begins // width == step)
     def own_hidden():
@@ -524,7 +540,7 @@
 
 
 def reverse_backward(
-    pieces, order_ref, length_ref, dx2_ref, mv_ref, vq_ref, vkv_ref, nx_ref, log_ref, a_out,
+    pieces, length_ref, dx2_ref, mv_ref, vq_ref, vkv_ref, nx_ref, log_ref, a_out,
     *rest,
 ):
     dvq_ref, weight_ref, rest = rest[0], rest[1], rest[2:]
@@ -569,11 +585,11 @@
     loop(features // PAIR, pair)
     weight_ref[:, 0:features] = left_t(nx_ref[...], dvq_ref[...]).astype(NARROW)
     for k in range(pieces):
-        kv_refs[k][...] = dkv[at(order_ref[k], part), :].astype(NARROW)
+        kv_refs[k][...] = dkv[at(piece_at(k, pieces), part), :].astype(NARROW)
 
 
 def cross_backward(
-    pieces, share, place_ref, order_ref, dq2_ref, co_ref, cq_ref, ckv_ref, valid_ref, a_out, *rest
+    pieces, share, dq2_ref, co_ref, cq_ref, ckv_ref, valid_ref, a_out, *rest
 ):
     log_parts, rest = rest[:pieces], rest[pieces:]
     dckv_ref, weight_ref, rest = rest[0], rest[1], rest[2:]
@@ -585,13 +601,13 @@
     part = log_parts[0].shape[0]
     (load,) = copies(sem, (a_out.at[2], w_out))
     for k in range(pieces):
-        logs[at(order_ref[k], part), :] = log_parts[k][...]
+        logs[at(piece_at(k, pieces), part), :] = log_parts[k][...]
     turned[...] = turn(logs[0:rows, :])
     rounded[...] = dq2_ref[...].astype(NARROW)
     load.wait()
     dco[...] = right_t(rounded[...], w_out[...]).astype(NARROW)
     taken = right_t(
-        chooser(weight_ref.shape[0], features, place_ref[0] * share, share), co_ref[0:rows, :]
+        chooser(weight_ref.shape[0], features, place_of() * share, share), co_ref[0:rows, :]
     ).astype(NARROW)
     weight_ref[...] = plain(taken, rounded[...]).astype(NARROW)
     deltas[...] = head_rows(dco[...].astype(SINGLE) * co_ref[0:rows, :].astype(SINGLE))
@@ -624,21 +640,19 @@
     loop(features // PAIR, pair)
     dckv_ref[...] = dkv[...].astype(NARROW)
     for k in range(pieces):
-        q_refs[k][...] = dq_all[at(order_ref[k], part), :]
-
-
-def patch_backward(
-    x_ref, dx2_ref, x1_ref, nx_ref, n0_ref, pw_ref, mw_ref, dvq_ref, dckv_ref, gain_ref, a_in, a_out,
-    kv_weight_ref, weight_ref, grad_ref, norm_ref,
-    w_in, w_out, w_q, w_kv, dx1, rounded, dmw, deltas, dpw, sem,
+        q_refs[k][...] = dq_all[at(piece_at(k, pieces), part), :]
+
+
+def patch_cross_backward(
+    dx2_ref, x1_ref, nx_ref, dvq_ref, dckv_ref, gain_ref, a_in,
+    kv_weight_ref, dx1_ref, norm_ref,
+    w_q, w_kv, sem,
 ):
-    rows, features = x_ref.shape
+    rows, features = dx2_ref.shape
     loads = copies(
         sem,
         (a_in.at[3, :, pl.ds(0, features)], w_q),
         (a_in.at[2, :, pl.ds(features, 2 * features)], w_kv),
-        (a_out.at[0], w_out),
-        (a_in.at[0], w_in),
     )
     norm_ref[...] = jnp.zeros_like(norm_ref)
 
@@ -654,14 +668,23 @@
         span = at(i, GROUP)
         upstream = right_t(dvq_ref[span, :], w_q[...]) + right_t(dckv_ref[span, :], w_kv[...])
         part, gain, bias = norm_back(x1_ref[span, :], gain_ref[3:4, :], upstream)
-        total = dx2_ref[span, :] + part
-        dx1[span, :] = total
-        rounded[span, :] = total.astype(NARROW)
+        dx1_ref[span, :] = dx2_ref[span, :] + part
         norm_ref[0:1, :] += gain
         norm_ref[1:2, :] += bias
 
     loop(rows // GROUP, first)
-    loads[2].wait()
+
+
+def window_backward(
+    x_ref, dx1_ref, n0_ref, pw_ref, mw_ref, gain_ref, a_in, a_out,
+    weight_ref, grad_ref, norm_ref,
+    w_in, w_out, rounded, dmw, deltas, dpw, sem,
+):
+    rows, features = x_ref.shape
+    loads = copies(sem, (a_out.at[0], w_out), (a_in.at[0], w_in))
+    norm_ref[...] = jnp.zeros_like(norm_ref)
+    rounded[...] = dx1_ref[...].astype(NARROW)
+    loads[0].wait()
     dmw[...] = right_t(rounded[...], w_out[...]).astype(NARROW)
     weight_ref[:, 3 * features :] = left_t(mw_ref[...], rounded[...]).astype(NARROW)
     deltas[...] = head_rows(dmw[...].astype(SINGLE) * mw_ref[...].astype(SINGLE))
@@ -693,15 +716,15 @@
         weight_ref[:, span] = left_t(n0_ref[...], dpw[:, span]).astype(NARROW)
 
     loop(3 * features // CHUNK, in_weight)
-    loads[3].wait()
+    loads[1].wait()
 
     def last(i):
         span = at(i, GROUP)
         upstream = right_t(dpw[span, :], w_in[...])
         part, gain, bias = norm_back(x_ref[span, :].astype(SINGLE), gain_ref[0:1, :], upstream)
-        grad_ref[span, :] = dx1[span, :] + part
-        norm_ref[2:3, :] += gain
-        norm_ref[3:4, :] += bias
+        grad_ref[span, :] = dx1_ref[span, :] + part
+        norm_ref[0:1, :] += gain
+        norm_ref[1:2, :] += bias
 
     loop(rows // GROUP, last)
 
@@ -740,7 +763,7 @@
 
 
 def causal_backward(
-    pieces, share, place_ref, order_ref, q_ref, dq2_ref, n1_ref, pq_ref, mq_ref, log_ref, gain_ref,
+    pieces, share, q_ref, dq2_ref, n1_ref, pq_ref, mq_ref, log_ref, cross_ref, gain_ref,
     a_in, a_out, *rest
 ):
     parts, rest = rest[:pieces], rest[pieces:]
@@ -752,7 +775,7 @@
     part = parts[0].shape[0]
     loads = copies(sem, (a_out.at[1], w_out), (a_in.at[1], w_in))
     for k in range(pieces):
-        gathered[at(order_ref[k], part), :] = parts[k][...]
+        gathered[at(piece_at(k, pieces), part), :] = parts[k][...]
 
     def first(i):
         span = at(i, STRIP)
@@ -763,9 +786,11 @@
     loop(rows // STRIP, first)
     loads[0].wait()
     dmq[...] = right_t(rounded[...], w_out[...]).astype(NARROW)
-    chosen = chooser(weight_ref.shape[0], features, place_ref[0] * share, share)
+    chosen = chooser(weight_ref.shape[0], features, place_of() * share, share)
     taken = right_t(chosen, mq_ref[...]).astype(NARROW)
-    weight_ref[:, 3 * features :] = plain(taken, rounded[...]).astype(NARROW)
+    weight_ref[:, 3 * features : 4 * features] = plain(taken, rounded[...]).astype(NARROW)
+    weight_ref[:, 4 * features : 5 * features] = cross_ref[...]
+    weight_ref[:, 5 * features :] = jnp.zeros_like(weight_ref[:, 5 * features :])
     deltas[...] = head_rows(dmq[...].astype(SINGLE) * mq_ref[...].astype(SINGLE))
     edges = [(start, min(start + 256, rows)) for start in range(0, rows, 256)]
 
@@ -880,28 +905,124 @@
     return gather_rep(sum_rep_scatter(tensor, 0).astype(NARROW), 0)
 
 
-DIRECT = 8
-
-
-def piece_order():
-    count = lax.axis_size("blk")
-    numbers = jnp.arange(count, dtype=jnp.int32)
-    return numbers ^ lax.axis_index("blk").astype(jnp.int32) if count <= DIRECT else numbers
-
-
 def exchange(pieces):
-    if len(pieces) <= DIRECT:
-        return [one if k == 0 else swap(one, "blk", k) for k, one in enumerate(pieces)]
     whole = lax.all_to_all(jnp.stack(pieces), "blk", 0, 0)
     return [whole[k] for k in range(len(pieces))]
 
 
 def gather(tensor):
     count = lax.axis_size("blk")
-    if count <= DIRECT:
-        return [tensor if k == 0 else swap(tensor, "blk", k) for k in range(count)]
     whole = lax.all_gather(tensor, "blk")
     return [whole[k] for k in range(count)]
+
+
+def whole(ref):
+    return ref
+
+
+class Move:
+    def __init__(self, source, shape, axis, flip, take=whole):
+        self.source, self.shape, self.axis, self.flip, self.take = source, shape, axis, flip, take
+
+
+class Reduction:
+    def __init__(self, tensor):
+        blocks = lax.axis_size("blk")
+        height = tensor.shape[0] // blocks
+        self.tensor = tensor.reshape(blocks, 2, height // 2, tensor.shape[1])
+
+    def moves(self, stage):
+        tensor = self.tensor
+        shape = tensor.shape
+        if stage == "core":
+            return [
+                Move(tensor, shape[:1] + shape[2:], "rep", 1,
+                     lambda ref: ref.at[:, 1 - place_of("rep") % 2])
+            ]
+        if stage == "x":
+            width = shape[-1] // 2
+
+            def columns(ref):
+                span = pl.ds(pl.multiple_of((1 - place_of("rep") // 2) * width, width), width)
+                return ref.at[(slice(None),) * (len(shape) - 1) + (span,)]
+
+            return [Move(tensor, shape[:-1] + (width,), "rep", 2, columns)]
+        if stage == "y":
+            tensor = self.tensor = tensor.reshape((shape[0] // 2, 2) + shape[1:])
+            return [
+                Move(tensor, tensor.shape[:1] + shape[1:], "blk", 1,
+                     lambda ref: ref.at[:, 1 - place_of() % 2])
+            ]
+        if stage == "z":
+            length = shape[0]
+            return [
+                Move(tensor, shape[1:], "blk", 2 * k,
+                     lambda ref, k=k: ref.at[flipped(place_of() // 2, k, length)])
+                for k in range(1, length)
+            ]
+        return [Move(tensor, shape, "rep", 2 if stage == "back_x" else 1)]
+
+    def absorb(self, stage, arrived):
+        tensor = self.tensor
+        rep, blk = lax.axis_index("rep"), lax.axis_index("blk")
+        if stage == "core":
+            own = pick(tensor, rep % 2, 1)
+        elif stage == "x":
+            width = tensor.shape[-1] // 2
+            own = lax.dynamic_slice_in_dim(tensor, (rep // 2) * width, width, tensor.ndim - 1)
+        elif stage == "y":
+            own = pick(tensor, blk % 2, 1)
+        elif stage == "z":
+            own = pick(tensor, blk // 2, 0)
+        else:
+            bit, dim = (rep // 2, tensor.ndim - 1) if stage == "back_x" else (rep % 2, 0)
+            self.tensor = jnp.where(
+                bit == 0,
+                jnp.concatenate((tensor, arrived[0]), axis=dim),
+                jnp.concatenate((arrived[0], tensor), axis=dim),
+            )
+            return
+        total = own.astype(SINGLE)
+        for one in arrived:
+            total = total + one.astype(SINGLE)
+        self.tensor = total.astype(NARROW)
+
+
+class RepSum:
+    def __init__(self, tensor, dim):
+        self.tensor, self.dim = tensor, dim
+
+    def moves(self, stage):
+        shape = list(self.tensor.shape)
+        if stage == "out":
+            size = shape[self.dim] = shape[self.dim] // 4
+
+            def quarter(ref, k):
+                span = pl.ds(pl.multiple_of(flipped(place_of("rep"), k, 4) * size, size), size)
+                return ref.at[span, :] if self.dim == 0 else ref.at[:, span]
+
+            return [
+                Move(self.tensor, tuple(shape), "rep", k, lambda ref, k=k: quarter(ref, k))
+                for k in range(1, 4)
+            ]
+        return [Move(self.tensor, tuple(shape), "rep", k) for k in range(1, 4)]
+
+    def absorb(self, stage, arrived):
+        rep = lax.axis_index("rep")
+        if stage == "out":
+            size = self.tensor.shape[self.dim] // 4
+            total = lax.dynamic_slice_in_dim(self.tensor, rep * size, size, self.dim).astype(SINGLE)
+            for one in arrived:
+                total = total + one.astype(SINGLE)
+            self.tensor = total.astype(NARROW)
+            return
+        held = [self.tensor] + list(arrived)
+        for weight in (1, 2):
+            flip = (rep // weight) % 2 == 1
+            held = [
+                jnp.where(flip, held[k ^ weight], held[k]) for k in range(4)
+            ]
+        self.tensor = jnp.concatenate(held, axis=self.dim)
 
 
 VMEM = pl.BlockSpec(memory_space=pltpu.VMEM)
@@ -913,23 +1034,156 @@
     return jax.ShapeDtypeStruct(shape, kind)
 
 
-def call(kernel, outs, operands, specs, scratch, flops, grid=None, out_specs=None, semaphores=0):
+def call(
+    kernel, outs, operands, specs, scratch, flops, grid=None, out_specs=None, semaphores=0,
+    moves=(), ident=None,
+):
     scratch = [pltpu.VMEM(shape, kind) for shape, kind in scratch]
     if semaphores:
         scratch.append(pltpu.SemaphoreType.DMA((semaphores,)))
+    out_specs = [VMEM] * len(outs) if out_specs is None else out_specs
     extra = {} if grid is None else {"grid": grid}
-    return pl.pallas_call(
-        kernel,
-        out_shape=outs,
-        in_specs=specs,
-        out_specs=[VMEM] * len(outs) if out_specs is None else out_specs,
+    params = {}
+    sources = []
+    for move in moves:
+        if not any(move.source is one for one in sources):
+            sources.append(move.source)
+    number = [next(k for k, one in enumerate(sources) if one is move.source) for move in moves]
+    fixed_in, fixed_out = len(operands), len(outs)
+    partners = sorted({(move.axis, move.flip) for move in moves})
+    body_kernel = kernel
+    if moves:
+        params = {"collective_id": ident, "has_side_effects": True}
+        scratch += [pltpu.SemaphoreType.DMA((len(moves),))] * 2
+
+        def body_kernel(*refs):
+            ins, refs = refs[:fixed_in], refs[fixed_in:]
+            sent, refs = refs[: len(sources)], refs[len(sources) :]
+            results, refs = refs[:fixed_out], refs[fixed_out:]
+            landed, refs = refs[: len(moves)], refs[len(moves) :]
+            rest, (send_sem, recv_sem) = refs[:-2], refs[-2:]
+
+            def target(axis, flip):
+                return {axis: flipped(lax.axis_index(axis), flip, lax.axis_size(axis))}
+
+            def made(k):
+                move = moves[k]
+                return pltpu.make_async_remote_copy(
+                    src_ref=move.take(sent[number[k]]),
+                    dst_ref=landed[k],
+                    send_sem=send_sem.at[k],
+                    recv_sem=recv_sem.at[k],
+                    device_id=target(move.axis, move.flip),
+                    device_id_type=pl.DeviceIdType.MESH,
+                )
+
+            def begin():
+                barrier = pltpu.get_barrier_semaphore()
+                for axis, flip in partners:
+                    pl.semaphore_signal(
+                        barrier, inc=1, device_id=target(axis, flip),
+                        device_id_type=pl.DeviceIdType.MESH,
+                    )
+                pl.semaphore_wait(barrier, len(partners))
+                for k in range(len(moves)):
+                    made(k).start()
+
+            def finish():
+                for k in range(len(moves)):
+                    made(k).wait()
+
+            if grid is None:
+                begin()
+                kernel(*ins, *results, *rest)
+                finish()
+            else:
+                pl.when(pl.program_id(0) == 0)(begin)
+                kernel(*ins, *results, *rest)
+                pl.when(pl.program_id(0) == pl.num_programs(0) - 1)(finish)
+
+    result = pl.pallas_call(
+        body_kernel,
+        out_shape=list(outs) + [like(*m.shape, kind=m.source.dtype) for m in moves],
+        in_specs=list(specs) + [ANY] * len(sources),
+        out_specs=list(out_specs) + [ANY] * len(moves),
         scratch_shapes=scratch,
-        compiler_params=pltpu.CompilerParams(vmem_limit_bytes=56 * 2**20),
+        compiler_params=pltpu.CompilerParams(vmem_limit_bytes=56 * 2**20, **params),
         cost_estimate=pl.CostEstimate(
-            flops=int(flops), bytes_accessed=sum(o.size * o.dtype.itemsize for o in operands), transcendentals=0
+            flops=int(flops),
+            bytes_accessed=sum(o.size * o.dtype.itemsize for o in operands),
+            transcendentals=0,
         ),
         **extra,
-    )(*operands)
+    )(*operands, *sources)
+    return list(result[:fixed_out]), list(result[fixed_out:])
+
+
+def nothing():
+    return None
+
+
+class Courier:
+    def __init__(self, active):
+        self.active, self.waiting, self.ident = active, [], 0
+
+    def load(self, *jobs):
+        self.waiting += jobs
+
+    def run(self, kernel, outs, operands, specs, scratch, flops, **extra):
+        jobs, self.waiting = self.waiting, []
+        moves, ends = [], []
+        for job, stage in jobs:
+            moves += job.moves(stage)
+            ends.append(len(moves))
+        if moves:
+            self.ident += 1
+        results, arrived = call(
+            kernel, outs, operands, specs, scratch, flops, moves=tuple(moves), ident=self.ident, **extra
+        )
+        start = 0
+        for (job, stage), end in zip(jobs, ends):
+            job.absorb(stage, arrived[start:end])
+            start = end
+        return results
+
+
+class Exchange:
+    def __init__(self, pieces):
+        self.pieces = pieces
+
+    def moves(self, stage):
+        return [Move(one, one.shape, "blk", k) for k, one in enumerate(self.pieces) if k]
+
+    def absorb(self, stage, arrived):
+        self.result = self.pieces[:1] + list(arrived)
+
+
+class Gather:
+    def __init__(self, tensor):
+        self.tensor = tensor
+
+    def moves(self, stage):
+        return [
+            Move(self.tensor, self.tensor.shape, "blk", k) for k in range(1, lax.axis_size("blk"))
+        ]
+
+    def absorb(self, stage, arrived):
+        self.result = [self.tensor] + list(arrived)
+
+
+class Norms:
+    def __init__(self, tensor):
+        self.tensor = tensor
+
+    def moves(self, stage):
+        axis = "rep" if stage == "out" else "blk"
+        return [
+            Move(self.tensor, self.tensor.shape, axis, k) for k in range(1, lax.axis_size(axis))
+        ]
+
+    def absorb(self, stage, arrived):
+        for one in arrived:
+            self.tensor = self.tensor + one
 
 
 def body(
@@ -952,8 +1206,6 @@
     hidden = mlp_in.shape[2]
     blocks = lax.axis_size("blk")
     place = lax.axis_index("blk").astype(jnp.int32)
-    places = place.reshape(1)
-    order = piece_order()
     share = features // blocks
     hidden_share = hidden // blocks
     share_rows = -(-share // 16) * 16
@@ -961,8 +1213,12 @@
     part = -(-count // (blocks * 16)) * 16
     padded = part * blocks
     wide = 3 * features
+    last = wide + features + features
+    causal_columns = -(-last // 512) * 512
     leader = (place == 0).astype(SINGLE)
     valid = jnp.where(jnp.repeat(window_valid[0], WIN) > 0, 0.0, MASKED).astype(SINGLE)
+    carried = blocks == DIRECT and lax.axis_size("rep") == 4 and share % 32 == 0
+    courier = Courier(carried)
 
     def own_columns(tensor):
         return lax.dynamic_slice_in_dim(tensor, place * share, share, 1)
@@ -972,8 +1228,9 @@
         return lax.dynamic_slice_in_dim(tensor, place * part, part, 0)
 
     square = 2.0 * features * features
-
-    n0, pw, mw, x1, nx, vq, ckv = call(
+    run = courier.run
+
+    n0, pw, mw, x1, nx, vq, ckv = run(
         window_forward,
         [
             like(rows, features), like(rows, wide), like(rows, features),
@@ -987,7 +1244,7 @@
         rows * square * 9,
         semaphores=4,
     )
-    n1, pq, mq, q1, nq, cq, vkv, log_q = call(
+    n1, pq, mq, q1, nq, cq, vkv, log_q = run(
         causal_forward,
         [
             like(count, features), like(count, wide), like(count, features),
@@ -1002,24 +1259,18 @@
         count * square * 15,
         semaphores=4,
     )
-    pieces = call(
+    pieces = run(
         functools.partial(cross_forward, blocks),
         [like(part, features)] * blocks + [like(part, PAIR, kind=SINGLE)] * blocks,
-        [order, cq, ckv, valid[None, :]],
-        [SMEM, VMEM, VMEM, VMEM],
+        [cq, ckv, valid[None, :]],
+        [VMEM, VMEM, VMEM],
         [((padded, features), NARROW), ((padded, PAIR), SINGLE)],
         count * square * 6,
     )
-    merged = call(
-        functools.partial(merge_blocks, blocks),
-        [like(part, features), like(part, PAIR, kind=SINGLE)],
-        exchange(pieces[:blocks]) + exchange(pieces[blocks:]),
-        [VMEM] * (2 * blocks),
-        [],
-        padded * square,
-    )
-    co_parts, log_parts = gather(merged[0]), gather(merged[1])
-    mv, x2, log_v = call(
+    outs, logs = Exchange(pieces[:blocks]), Exchange(pieces[blocks:])
+    if carried:
+        courier.load((outs, ""), (logs, ""))
+    mv, x2, log_v = run(
         reverse_forward,
         [like(rows, features), like(rows, features, kind=SINGLE), like(16, rows, kind=SINGLE)],
         [answer_length, vq, vkv, x1, attn_out],
@@ -1028,8 +1279,23 @@
         rows * square * 8,
         semaphores=1,
     )
+    if not carried:
+        outs.result, logs.result = exchange(outs.pieces), exchange(logs.pieces)
+    merged = run(
+        functools.partial(merge_blocks, blocks),
+        [like(part, features), like(part, PAIR, kind=SINGLE)],
+        outs.result + logs.result,
+        [VMEM] * (2 * blocks),
+        [],
+        padded * square,
+    )
+    co_parts, log_parts = Gather(merged[0]), Gather(merged[1])
+    if carried:
+        courier.load((co_parts, ""), (log_parts, ""))
+    else:
+        co_parts.result, log_parts.result = gather(merged[0]), gather(merged[1])
     fixed = lambda *shape: pl.BlockSpec(shape, lambda j: (0,) * len(shape))
-    x3, dx2, up_x, down_x, norm_five = call(
+    x3, dx2, up_x, down_x, norm_five = run(
         patch_feed_forward,
         [
             like(rows, features), like(rows, features, kind=SINGLE), like(features, hidden),
@@ -1052,28 +1318,34 @@
             fixed(8, features),
         ],
     )
-    up_x_total, down_x_total = reduce_all(up_x), reduce_all(down_x)
-    dvq, reverse_weight, *kv_pieces = call(
+    if carried:
+        up_x, down_x = Reduction(up_x), Reduction(down_x)
+        courier.load((up_x, "core"), (down_x, "core"))
+    dvq, reverse_weight, *kv_pieces = run(
         functools.partial(reverse_backward, blocks),
         [like(rows, features), like(features, 2 * features)] + [like(part, 2 * features)] * blocks,
-        [order, answer_length, dx2, mv, vq, vkv, nx, log_v, attn_out],
-        [SMEM, SMEM, VMEM, VMEM, VMEM, VMEM, VMEM, VMEM, ANY],
+        [answer_length, dx2, mv, vq, vkv, nx, log_v, attn_out],
+        [SMEM, VMEM, VMEM, VMEM, VMEM, VMEM, VMEM, ANY],
         [((features, features), NARROW), ((rows, features), NARROW), ((rows, features), NARROW),
          ((16, rows), SINGLE), ((padded, 2 * features), SINGLE)],
         rows * square * 16,
         semaphores=1,
     )
-    kv_parts = exchange(kv_pieces)
-    reverse_total = reduce_all(reverse_weight)
-    q3, dq2, up_q, down_q, norm_four, co = call(
+    kv_parts = Exchange(kv_pieces)
+    if carried:
+        reverse_weight = Reduction(reverse_weight)
+        courier.load((up_x, "x"), (down_x, "x"), (reverse_weight, "core"), (kv_parts, ""))
+    else:
+        kv_parts.result = exchange(kv_pieces)
+    q3, dq2, up_q, down_q, norm_four, co = run(
         functools.partial(query_feed_forward, blocks, share, hidden_share),
         [
             like(count, features), like(count, features, kind=SINGLE), like(share_rows, hidden),
             like(hidden_rows, features), like(8, features, kind=SINGLE), like(padded, features),
         ],
-        [places, order, q1, cot_q, norm_gain, norm_bias, attn_out, mlp_in, mlp_out] + co_parts,
+        [q1, cot_q, norm_gain, norm_bias, attn_out, mlp_in, mlp_out] + co_parts.result,
         [
-            SMEM, SMEM, fixed(count, features), fixed(count, features), fixed(6, features),
+            fixed(count, features), fixed(count, features), fixed(6, features),
             fixed(6, features), pl.BlockSpec((1, features, features), lambda j: (2, 0, 0)),
             pl.BlockSpec((1, features, CHUNK), lambda j: (1, 0, j)),
             pl.BlockSpec((1, CHUNK, features), lambda j: (1, j, 0)),
@@ -1089,87 +1361,146 @@
             fixed(hidden_rows, features), fixed(8, features), fixed(padded, features),
         ],
     )
-    dckv, cross_out_weight, *q_pieces = call(
+    if carried:
+        up_q, down_q = RepSum(up_q, 1), RepSum(down_q, 0)
+        courier.load(
+            (up_x, "y"), (down_x, "y"), (reverse_weight, "x"), (up_q, "out"), (down_q, "out")
+        )
+    dckv, cross_out_weight, *q_pieces = run(
         functools.partial(cross_backward, blocks, share),
         [like(rows, 2 * features), like(share_rows, features)] + [like(part, features)] * blocks,
-        [places, order, dq2, co, cq, ckv, valid[:, None], attn_out] + log_parts,
-        [SMEM, SMEM, VMEM, VMEM, VMEM, VMEM, VMEM, ANY] + [VMEM] * blocks,
+        [dq2, co, cq, ckv, valid[:, None], attn_out] + log_parts.result,
+        [VMEM, VMEM, VMEM, VMEM, VMEM, ANY] + [VMEM] * blocks,
         [((features, features), NARROW), ((count, features), NARROW), ((count, features), NARROW),
          ((16, count), SINGLE), ((padded, PAIR), SINGLE), ((16, count), SINGLE),
          ((padded, features), NARROW), ((rows, 2 * features), SINGLE)],
         count * square * 12,
         semaphores=1,
     )
-    q_parts = exchange(q_pieces)
-    up_q_total = reduce_rep(up_q[:share])
-    down_q_total = reduce_rep(down_q[:hidden_share])
-    kv_weight, window_weight, grad_x, norm_x = call(
-        patch_backward,
+    q_parts = Exchange(q_pieces)
+    if carried:
+        courier.load((q_parts, ""), (reverse_weight, "y"), (up_q, "back"), (down_q, "back"))
+    else:
+        q_parts.result = exchange(q_pieces)
+    kv_weight, dx1, norm_three = run(
+        patch_cross_backward,
         [
-            like(features, 2 * features), like(features, 4 * features),
-            like(rows, features, kind=SINGLE), like(8, features, kind=SINGLE),
+            like(features, 2 * features), like(rows, features, kind=SINGLE),
+            like(8, features, kind=SINGLE),
         ],
-        [x, dx2, x1, nx, n0, pw, mw, dvq, dckv, norm_gain, attn_in, attn_out],
-        [VMEM] * 10 + [ANY, ANY],
-        [((features, wide), NARROW), ((features, features), NARROW),
-         ((features, features), NARROW), ((features, 2 * features), NARROW),
-         ((rows, features), SINGLE), ((rows, features), NARROW), ((rows, features), NARROW),
-         ((16, rows), SINGLE), ((rows, wide), NARROW)],
-        rows * square * 24,
-        semaphores=4,
-    )
-    kv_total, window_total = reduce_all(kv_weight), reduce_all(window_weight)
-    dq1_share, share_weight, norm_two = call(
+        [dx2, x1, nx, dvq, dckv, norm_gain, attn_in],
+        [VMEM] * 6 + [ANY],
+        [((features, features), NARROW), ((features, 2 * features), NARROW)],
+        rows * square * 12,
+        semaphores=2,
+    )
+    dq1_share, share_weight, norm_two = run(
         functools.partial(share_backward, blocks),
         [like(part, features), like(features, wide), like(8, features, kind=SINGLE)],
-        [own_rows(q1), own_rows(nq), norm_gain, attn_in] + q_parts + kv_parts,
+        [own_rows(q1), own_rows(nq), norm_gain, attn_in] + q_parts.result + kv_parts.result,
         [VMEM, VMEM, VMEM, ANY] + [VMEM] * (2 * blocks),
         [((features, features), NARROW), ((features, 2 * features), NARROW),
          ((part, wide), NARROW)],
         part * square * 6,
         semaphores=2,
     )
-    share_total = reduce_all(share_weight)
-    causal_weight, grad_q, norm_one = call(
+    dq1_parts = Gather(dq1_share)
+    if carried:
+        kv_weight, share_weight = Reduction(kv_weight), Reduction(share_weight)
+        courier.load(
+            (dq1_parts, ""), (up_x, "z"), (down_x, "z"), (reverse_weight, "z"),
+            (kv_weight, "core"), (share_weight, "core"),
+        )
+    else:
+        dq1_parts.result = gather(dq1_share)
+    window_weight, grad_x, norm_zero = run(
+        window_backward,
+        [
+            like(features, 4 * features), like(rows, features, kind=SINGLE),
+            like(8, features, kind=SINGLE),
+        ],
+        [x, dx1, n0, pw, mw, norm_gain, attn_in, attn_out],
+        [VMEM] * 6 + [ANY, ANY],
+        [((features, wide), NARROW), ((features, features), NARROW),
+         ((rows, features), NARROW), ((rows, features), NARROW),
+         ((16, rows), SINGLE), ((rows, wide), NARROW)],
+        rows * square * 16,
+        semaphores=2,
+    )
+    if carried:
+        window_weight = Reduction(window_weight)
+        courier.load(
+            (window_weight, "core"), (kv_weight, "x"), (share_weight, "y"),
+            (up_x, "back_x"), (down_x, "back_x"), (reverse_weight, "back_x"),
+        )
+    causal_weight, grad_q, norm_one = run(
         functools.partial(causal_backward, blocks, share),
         [
-            like(share_rows, 4 * features), like(count, features, kind=SINGLE),
+            like(share_rows, causal_columns), like(count, features, kind=SINGLE),
             like(8, features, kind=SINGLE),
         ],
-        [places, order, q, dq2, n1, pq, mq, log_q, norm_gain, attn_in, attn_out]
-        + gather(dq1_share),
-        [SMEM, SMEM] + [VMEM] * 7 + [ANY, ANY] + [VMEM] * blocks,
+        [q, dq2, n1, pq, mq, log_q, cross_out_weight, norm_gain, attn_in, attn_out]
+        + dq1_parts.result,
+        [VMEM] * 8 + [ANY, ANY] + [VMEM] * blocks,
         [((features, wide), NARROW), ((features, features), NARROW), ((padded, features), NARROW),
          ((count, features), SINGLE), ((count, features), NARROW), ((count, features), NARROW),
          ((16, count), SINGLE), ((count, 2 * PAIR), SINGLE), ((count, wide), NARROW)],
         count * square * 16,
         semaphores=2,
     )
-    query_total = reduce_rep(
-        jnp.concatenate((causal_weight[:share], cross_out_weight[:share]), axis=1)
-    )
     norms = jnp.stack(
         (
-            norm_x[2], norm_one[0] * leader, norm_two[0], norm_x[0], norm_four[0] * leader,
-            norm_five[0], norm_x[3], norm_one[1] * leader, norm_two[1], norm_x[1],
+            norm_zero[0], norm_one[0] * leader, norm_two[0], norm_three[0], norm_four[0] * leader,
+            norm_five[0], norm_zero[1], norm_one[1] * leader, norm_two[1], norm_three[1],
             norm_four[1] * leader, norm_five[1],
         )
     )
-    norms = own_columns(lax.psum(norms, ("blk", "rep")))
+    if carried:
+        norms = Norms(jnp.pad(norms, ((0, 4), (0, 0))))
+        causal_weight = RepSum(causal_weight, 1)
+        arrive = lambda *jobs: (courier.load(*jobs), run(nothing, [], [], [], [], 0))
+        arrive(
+            (window_weight, "x"), (share_weight, "x"), (kv_weight, "y"), (norms, "out"),
+            (causal_weight, "out"), (up_x, "back_core"), (down_x, "back_core"),
+            (reverse_weight, "back_core"),
+        )
+        arrive(
+            (window_weight, "y"), (share_weight, "z"), (kv_weight, "z"), (norms, "back"),
+            (causal_weight, "back"),
+        )
+        arrive((window_weight, "z"), (share_weight, "back_x"), (kv_weight, "back_x"))
+        arrive((window_weight, "back_x"), (share_weight, "back_core"), (kv_weight, "back_core"))
+        arrive((window_weight, "back_core"))
+        up_x, down_x, reverse_weight, window_weight, kv_weight, share_weight, causal_weight = (
+            one.tensor
+            for one in (
+                up_x, down_x, reverse_weight, window_weight, kv_weight, share_weight, causal_weight
+            )
+        )
+        up_q, down_q, norms = up_q.tensor, down_q.tensor, norms.tensor[:12]
+    else:
+        up_x, down_x, reverse_weight, window_weight, kv_weight, share_weight = (
+            reduce_all(one)
+            for one in (up_x, down_x, reverse_weight, window_weight, kv_weight, share_weight)
+        )
+        up_q, down_q = reduce_rep(up_q[:share]), reduce_rep(down_q[:hidden_share])
+        causal_weight = reduce_rep(causal_weight[:share])
+        norms = lax.psum(norms, ("blk", "rep"))
+    norms = own_columns(norms)
     grad_attn_in = jnp.stack(
         (
-            window_total[:, :wide],
-            query_total[:, :wide],
-            jnp.concatenate((share_total[:, :features], kv_total), axis=1),
-            jnp.concatenate((reverse_total[:, :features], share_total[:, features:]), axis=1),
+            window_weight[:, :wide],
+            causal_weight[:, :wide],
+            jnp.concatenate((share_weight[:, :features], kv_weight), axis=1),
+            jnp.concatenate((reverse_weight[:, :features], share_weight[:, features:]), axis=1),
         )
     )
     grad_attn_out = jnp.stack(
         (
-            window_total[:, wide:],
-            query_total[:, wide : wide + features],
-            query_total[:, wide + features :],
-            reverse_total[:, features:],
+            window_weight[:, wide:],
+            causal_weight[:, wide : wide + features],
+            causal_weight[:, wide + features : last],
+            reverse_weight[:, features:],
         )
     )
     return (
@@ -1181,8 +1512,8 @@
         norms[6:],
         grad_attn_in.astype(SINGLE),
         grad_attn_out.astype(SINGLE),
-        jnp.stack((up_x_total, up_q_total)).astype(SINGLE),
-        jnp.stack((down_x_total, down_q_total)).astype(SINGLE),
+        jnp.stack((up_x, up_q)).astype(SINGLE),
+        jnp.stack((down_x, down_q)).astype(SINGLE),
     )
 
 

time: 826 us -> 683 us (0.83)
  Pallas kernels: 326 us -> 577 us
  waiting for transfers between devices: 203 us -> 0 us
  starting transfers between devices: 177 us -> 0 us
  other arithmetic: 27.7 us -> 75.2 us
  blocking collectives: 37.9 us -> 0 us
  local copies, waits for them, and re-layouts: 41.8 us -> 18.6 us
    pallas_call x12 -> x18, Pallas kernels: 326 us -> 577 us  [call(): pl.pallas_call(body_kernel, out_shape=list(outs) + [like(*m.shape, kind=m...]
    ppermute x103 -> x0, waiting for transfers between devices: 203 us -> none  [swap(): lax.ppermute(tensor, axis, [(i, i ^ mask) for i in range(lax.axis_size(ax...]
    ppermute x103 -> x0, starting transfers between devices: 177 us -> none  [swap(): lax.ppermute(tensor, axis, [(i, i ^ mask) for i in range(lax.axis_size(ax...]
    convert_element_type x11 -> x28, other arithmetic: 4.72 us -> 56.5 us  [the longest x26 53.3 us: absorb(): self.tensor = total.astype(NARROW)]
    psum x1 -> x0, blocking collectives: 37.9 us -> none  [body(): norms = own_columns(lax.psum(norms, ('blk', 'rep')))]
    dynamic_slice x5 -> x0, local copies, waits for them, and re-layouts: 16.5 us -> none  [pick(): return lax.dynamic_index_in_dim(tensor, place, dim, keepdims=False)]
    add x27 -> x3, other arithmetic: 9.86 us -> 1.53 us  [absorb(): self.tensor = self.tensor + one]
  transfers between devices with their start and end apart: 103 -> 0, of which waited for: 36 -> 0; matrix products, arithmetic and copies ran while one was open for 7% -> 0% of each run, Pallas kernels for 30% -> 0%
where the time goes in v3:
time: 683 us; the launch traced here: 674 us
  Pallas kernels  577 us (84%)
  other arithmetic  75.2 us (11%)
  local copies, waits for them, and re-layouts  18.6 us (3%)
    pallas_call x18, Pallas kernels, call(): pl.pallas_call(body_kernel, out_shape=list(outs) + [like(*m.shape, kind=m...  577 us
    convert_element_type x26, other arithmetic, absorb(): self.tensor = total.astype(NARROW)  53.3 us

profile of v3, /device:TPU:0, one launch (start us, length us, event | category | flops | bytes accessed | tf_op | source)
XLA Modules:
  0.0 673.5 jit_solution(7053335875881920503)
XLA Ops:
  2.8 0.9 select_n.458.refs_4_
  3.7 24.7 %shard_map.195 = (bf16[512,768]{1,0:T(8,128)(2,1)}, bf16[512,2304]{1,0:T(8,128)(2,1)}, bf16[512,768]{1,0:T(8,128)(2,1)}, f32[512,768]{1,0:T(8,128)}, bf16[512,76...) custom-call(bf16[512,768]{1,0:T(8,128)(2,1)} %bitcast.174, f32[6,768]{1,0:T(8,128)} %refs_7_.5, ...), custom_call_target="tpu_custom_call" | custom-call | flops 5435817984 | bytes 19697664 | tf_op jit(solution)/shard_map/pallas_call | solution.py:1104
  28.4 36.7 %shard_map.196 = (bf16[800,768]{1,0:T(8,128)(2,1)}, bf16[800,2304]{1,0:T(8,128)(2,1)}, bf16[800,768]{1,0:T(8,128)(2,1)}, f32[800,768]{1,0:T(8,128)}, bf16[800,76...) custom-call(bf16[800,768]{1,0:T(8,128)(2,1)} %bitcast.171, ...), custom_call_target="tpu_custom_call" | custom-call | flops 14155776000 | bytes 20140032 | tf_op jit(solution)/shard_map/pallas_call | solution.py:1104
  65.1 1.6 pad_dynamic-slice_fusion.1.nq_ref
  66.7 1.7 pad_dynamic-slice_fusion.q1_ref
  68.5 20.9 %shard_map.197 = (bf16[112,768]{1,0:T(8,128)(2,1)}, bf16[112,768]{1,0:T(8,128)(2,1)}, bf16[112,768]{1,0:T(8,128)(2,1)}, bf16[112,768]{1,0:T(8,128)(2,1)}, bf16[1...) custom-call(bf16[800,768]{1,0:T(8,128)(2,1)} %get-tuple-element.216., ...), custom_call_target="tpu_custom_call" | custom-call | flops 5662310400 | bytes 2803712 | tf_op jit(solution)/shard_map/pallas_call | solution.py:1104
  89.3 49.5 %shard_map.198 = (bf16[512,768]{1,0:T(8,128)(2,1)}, f32[512,768]{1,0:T(8,128)}, f32[16,512]{1,0:T(8,128)}, bf16[112,768]{1,0:T(8,128)(2,1)}, bf16[112,768]{1,0:T...) custom-call(s32[1]{0:T(128)S(6)} %copy.60.refs_0_, ...), custom_call_target="tpu_custom_call" | custom-call | flops 4831838208 | bytes 9535492 | tf_op jit(solution)/shard_map/pallas_call | solution.py:1104
  138.8 3.1 shard_map.199
  142.0 47.1 %shard_map.200 = (bf16[512,768]{1,0:T(8,128)(2,1)}, f32[512,768]{1,0:T(8,128)}, bf16[768,3072]{1,0:T(8,128)(2,1)}, bf16[3072,768]{1,0:T(8,128)(2,1)}, f32[8,768]...) custom-call(f32[512,768]{1,0:T(8,128)} %get-tuple-element.232.refs_0, ...), custom_call_target="tpu_custom_call" | custom-call | flops 14495514624 | bytes 21270528 | tf_op jit(solution)/shard_map/pallas_call | solution.py:1104
  189.1 29.3 %shard_map.201 = (bf16[512,768]{1,0:T(8,128)(2,1)}, bf16[768,1536]{1,0:T(8,128)(2,1)}, bf16[112,1536]{1,0:T(8,128)(2,1)}, bf16[112,1536]{1,0:T(8,128)(2,1)}, bf1...) custom-call(s32[1]{0:T(128)S(6)} %copy.60.refs_0_, ...), custom_call_target="tpu_custom_call" | custom-call | flops 9663676416 | bytes 11141124 | tf_op jit(solution)/shard_map/pallas_call | solution.py:1104
  218.4 3.8 fusion.1.refs_16_
  223.0 2.4 fusion.2.refs_15_
  225.3 62.9 %shard_map.202 = (bf16[800,768]{1,0:T(8,128)(2,1)}, f32[800,768]{1,0:T(8,128)}, bf16[96,3072]{1,0:T(8,128)(2,1)}, bf16[384,768]{1,0:T(8,128)(2,1)}, f32[8,768]{1...) custom-call(f32[800,768]{1,0:T(8,128)} %get-tuple-element.252.refs_0, ...), custom_call_target="tpu_custom_call" | custom-call | flops 16986931200 | bytes 28692480 | tf_op jit(solution)/shard_map/pallas_call | solution.py:1104
  289.1 2.7 add_convert_fusion.1
  291.8 3.4 fusion.5
  295.2 1.1 constant_dynamic-slice_fusion.8
  297.2 33.3 %shard_map.203 = (bf16[512,1536]{1,0:T(8,128)(2,1)}, bf16[96,768]{1,0:T(8,128)(2,1)}, bf16[112,768]{1,0:T(8,128)(2,1)}, bf16[112,768]{1,0:T(8,128)(2,1)}, bf16[1...) custom-call(f32[800,768]{1,0:T(8,128)} %get-tuple-element.278.refs_0, ...), custom_call_target="tpu_custom_call" | custom-call | flops 11324620800 | bytes 11814912 | tf_op jit(solution)/shard_map/pallas_call | solution.py:1104
  330.6 2.2 fusion.8.refs_10_
  332.8 1.0 fusion.9.refs_9_
  333.8 1.6 add_convert_fusion.7.refs_16_
  335.4 1.7 add_convert_fusion.8.refs_15_
  337.1 1.0 add_convert_fusion.4
  338.0 41.0 %shard_map.204 = (bf16[768,1536]{1,0:T(8,128)(2,1)}, f32[512,768]{1,0:T(8,128)}, f32[8,768]{1,0:T(8,128)}, bf16[112,768]{1,0:T(8,128)(2,1)}, bf16[112,768]{1,0:T...) custom-call(f32[512,768]{1,0:T(8,128)} %get-tuple-element.261.refs_1, ...), custom_call_target="tpu_custom_call" | custom-call | flops 7247757312 | bytes 20465664 | tf_op jit(solution)/shard_map/pallas_call | solution.py:1104
  379.1 1.8 fusion.11.refs_11_
  381.6 6.6 shard_map.205
  389.5 76.0 %shard_map.206 = (bf16[768,3072]{1,0:T(8,128)(2,1)}, f32[512,768]{1,0:T(8,128)}, f32[8,768]{1,0:T(8,128)}, bf16[112,768]{1,0:T(8,128)(2,1)}, bf16[112,768]{1,0:T...) custom-call(bf16[512,768]{1,0:T(8,128)(2,1)} %bitcast.175, ...), custom_call_target="tpu_custom_call" | custom-call | flops 9663676416 | bytes 25184256 | tf_op jit(solution)/shard_map/pallas_call | solution.py:1104
  465.5 1.8 fusion.31.refs_23_
  467.3 1.9 fusion.18.refs_22_
  469.2 1.8 fusion.21.refs_21_
  471.0 1.7 fusion.3
  472.7 1.0 copy-done.34
  473.7 1.3 fusion.4.refs_19_
  475.0 47.0 %shard_map.207 = (bf16[96,4096]{1,0:T(8,128)(2,1)}, f32[800,768]{1,0:T(8,128)}, f32[8,768]{1,0:T(8,128)}, bf16[8,48,3072]{2,1,0:T(8,128)(2,1)}, bf16[8,48,768]{2...) custom-call(bf16[800,768]{1,0:T(8,128)(2,1)} %bitcast.172, ...), custom_call_target="tpu_custom_call" | custom-call | flops 15099494400 | bytes 30298112 | tf_op jit(solution)/shard_map/pallas_call | solution.py:1104
  522.1 2.1 add_convert_fusion.3
  524.2 2.4 fusion.6.refs_1_
  526.7 4.0 fusion.refs_0_
  530.7 1.4 constant_dynamic-slice_fusion.7
  532.1 0.9 copy.42
  537.7 48.3 %shard_map.208 = (bf16[8,48,1536]{2,1,0:T(8,128)(2,1)}, bf16[4,48,1152]{2,1,0:T(8,128)(2,1)}, bf16[4,48,768]{2,1,0:T(8,128)(2,1)}, f32[16,768]{1,0:T(8,128)}, f3...) custom-call(bf16[8,48,3072]{2,1,0:T(8,128)(2,1)} %fusion.refs_0_, ...), custom_call_target="tpu_custom_call" | custom-call | tf_op jit(solution)/shard_map/pallas_call | solution.py:1104
  586.1 2.2 add_convert_fusion.6.refs_4_
  588.2 1.7 fusion.10.refs_2_
  590.0 0.9 add_convert_fusion.5.refs_1_
  590.9 2.7 add_convert_fusion
  595.0 1.6 maximum_convert_fusion.2
  596.6 1.6 maximum_convert_fusion.1
  598.1 28.1 %shard_map.209 = (bf16[4,48,1536]{2,1,0:T(8,128)(2,1)}, bf16[48,1152]{1,0:T(8,128)(2,1)}, bf16[48,1152]{1,0:T(8,128)(2,1)}, bf16[48,1152]{1,0:T(8,128)(2,1)}, bf...) custom-call(bf16[4,2,48,1536]{3,2,1,0:T(8,128)(2,1)} %bitcast.129, ...), custom_call_target="tpu_custom_call" | custom-call | tf_op jit(solution)/shard_map/pallas_call | solution.py:1104
  626.3 1.7 fusion.28.refs_2_
  627.9 1.8 fusion.24.refs_1_
  629.7 2.1 fusion.7.refs_0_
  631.8 0.9 fusion.32
  633.3 14.9 %shard_map.210 = (bf16[48,1536]{1,0:T(8,128)(2,1)}, bf16[48,1536]{1,0:T(8,128)(2,1)}, bf16[48,1536]{1,0:T(8,128)(2,1)}, bf16[48,1152]{1,0:T(8,128)(2,1)}, bf16[48,768]{1,0:T(8,128)(2,1)}) custom-call(bf16[4,48,1536]{2,1,0:T(8,128)(2,1)} %fusion.7.refs_0_, bf16[48,1152]{1,0:T(8,128)(2,1)} %fusion.24.refs_1_, bf16[48,768]{1,0:T(8,128)(2,1)} %fusion.28.refs_2_), custom_call_target="tpu_custom_call" | custom-call | tf_op jit(solution)/shard_map/pallas_call | solution.py:1104
  648.2 1.9 fusion.15.refs_0_
  650.1 1.7 maximum_select_fusion.11.refs_2_
  651.7 1.7 maximum_select_fusion.9.refs_1_
  653.5 5.8 shard_map.211
  659.2 1.9 maximum_select_fusion.6.refs_0_
  661.1 1.1 maximum_select_fusion.7
  662.2 1.1 maximum_select_fusion.3
  663.5 2.0 shard_map.212
  665.5 1.2 maximum_select_fusion
  667.0 1.1 maximum_convert_fusion.3
  668.1 2.1 maximum_convert_fusion
  670.2 0.9 copy.61
  671.9 1.1 copy.62
  (171 shorter events, 13.8 us)
Async XLA Ops:
  189.0 29.3 %slice-start = ((s8[4718592]{0:T(1024)(128)(4,1)}), s8[4194304]{0:T(1024)(128)(4,1)S(1)}, s32[]{:S(2)}) async-start(s8[4718592]{0:T(1024)(128)(4,1)} %bitcast.149), calls=%async_computation | async-start | bytes 8388608
  189.0 29.3 %slice-start.1 = ((s8[4718592]{0:T(1024)(128)(4,1)}), s8[524288]{0:T(1024)(128)(4,1)S(1)}, s32[]{:S(2)}) async-start(s8[4718592]{0:T(1024)(128)(4,1)} %bitcast.149), calls=%async_computation.1 | async-start | bytes 1048576
  218.4 3.8 copy-start.15
  218.4 4.6 copy-start.23
  225.3 63.7 %copy-start.3 = (bf16[8,192,768]{2,1,0:T(8,128)(2,1)S(1)}, bf16[8,192,768]{2,1,0:T(8,128)(2,1)}, u32[]{:S(2)}) copy-start(bf16[8,192,768]{2,1,0:T(8,128)(2,1)} %fusion.1.refs_16_) | copy-start | bytes 7077892
  225.3 66.5 %copy-start.37 = (bf16[768,1536]{1,0:T(8,128)(2,1)S(1)}, bf16[768,1536]{1,0:T(8,128)(2,1)}, u32[]{:S(2)}) copy-start(bf16[768,1536]{1,0:T(8,128)(2,1)} %get-tuple-element.268) | copy-start | bytes 7077892
  289.1 2.8 copy-start.4
  289.1 2.8 copy-start.25
  297.2 33.4 %copy-start.8 = (bf16[8,192,384]{2,1,0:T(8,128)(2,1)S(1)}, bf16[8,192,384]{2,1,0:T(8,128)(2,1)}, u32[]{:S(2)}) copy-start(bf16[8,192,384]{2,1,0:T(8,128)(2,1)} %add_convert_fusion.1) | copy-start | bytes 3538948
  330.5 2.2 copy-start.11
  330.5 2.2 copy-start.36
  330.5 3.2 copy-start.49
  330.6 3.2 copy-start.50
  330.6 3.2 copy-start.51
  332.8 2.7 copy-start.46
  332.8 2.7 copy-start.47
  332.8 2.7 copy-start.48
  332.8 4.3 copy-start.10
  332.8 4.3 copy-start.35
  338.0 41.0 %copy-start.20 = (bf16[8,48,768]{2,1,0:T(8,128)(2,1)S(1)}, bf16[8,48,768]{2,1,0:T(8,128)(2,1)}, u32[]{:S(2)}) copy-start(bf16[8,48,768]{2,1,0:T(8,128)(2,1)} %add_convert_fusion.4) | copy-start | bytes 1769476
  381.6 7.5 %copy-start.32 = (bf16[96,768]{1,0:T(8,128)(2,1)S(1)}, bf16[96,768]{1,0:T(8,128)(2,1)}, u32[]{:S(2)}) copy-start(bf16[96,768]{1,0:T(8,128)(2,1)} %add_convert_fusion.8.refs_15_) | copy-start | bytes 442372
  381.6 7.5 %copy-start.57 = (bf16[96,768]{1,0:T(8,128)(2,1)S(1)}, bf16[96,768]{1,0:T(8,128)(2,1)}, u32[]{:S(2)}) copy-start(bf16[96,768]{1,0:T(8,128)(2,1)} %get-tuple-element.411) | copy-start | bytes 442372
  381.6 7.5 %copy-start.58 = (bf16[96,768]{1,0:T(8,128)(2,1)S(1)}, bf16[96,768]{1,0:T(8,128)(2,1)}, u32[]{:S(2)}) copy-start(bf16[96,768]{1,0:T(8,128)(2,1)} %get-tuple-element.410) | copy-start | bytes 442372
  381.6 7.5 %copy-start.59 = (bf16[96,768]{1,0:T(8,128)(2,1)S(1)}, bf16[96,768]{1,0:T(8,128)(2,1)}, u32[]{:S(2)}) copy-start(bf16[96,768]{1,0:T(8,128)(2,1)} %get-tuple-element.409) | copy-start | bytes 442372
  388.3 1.1 copy-start.53
  388.3 1.1 copy-start.54
  389.5 81.5 %copy-start.27 = (bf16[768,2304]{1,0:T(8,128)(2,1)S(1)}, bf16[768,2304]{1,0:T(8,128)(2,1)}, u32[]{:S(2)}) copy-start(bf16[768,2304]{1,0:T(8,128)(2,1)} %get-tuple-element.333) | copy-start | bytes 10616836
  465.5 5.5 copy-start.18
  471.0 1.7 copy-start.24
  471.0 2.7 copy-start.34
  475.0 47.0 %copy-start.9 = (bf16[8,48,1536]{2,1,0:T(8,128)(2,1)S(1)}, bf16[8,48,1536]{2,1,0:T(8,128)(2,1)}, u32[]{:S(2)}) copy-start(bf16[8,48,1536]{2,1,0:T(8,128)(2,1)} %fusion.4.refs_19_) | copy-start | bytes 3538948
  522.0 2.2 copy-start.5
  524.2 2.5 copy-start.14
  530.7 4.7 copy-start.42
  530.7 4.7 copy-start.61
  530.7 5.4 copy-start.33
  530.7 5.4 copy-start.56
  530.7 6.2 copy-start.31
  530.7 6.2 copy-start.55
  537.7 50.5 %copy-start.6 = (bf16[8,48,768]{2,1,0:T(8,128)(2,1)S(1)}, bf16[8,48,768]{2,1,0:T(8,128)(2,1)}, u32[]{:S(2)}) copy-start(bf16[8,48,768]{2,1,0:T(8,128)(2,1)} %add_convert_fusion.3) | copy-start | bytes 1769476
  537.7 52.3 %copy-start.2 = (bf16[4,48,2304]{2,1,0:T(8,128)(2,1)S(1)}, bf16[4,48,2304]{2,1,0:T(8,128)(2,1)}, u32[]{:S(2)}) copy-start(bf16[4,48,2304]{2,1,0:T(8,128)(2,1)} %fusion.6.refs_1_) | copy-start | bytes 2654212
  586.0 3.9 copy-start.38
  586.1 4.8 copy-start
  590.9 2.7 copy-start.63
  590.9 2.7 copy-start.64
  590.9 2.7 copy-start.65
  590.9 3.4 copy-start.22
  590.9 3.4 copy-start.60
  593.6 1.2 copy-start.13
  593.6 1.2 copy-start.40
  598.1 31.6 %copy-start.1 = (bf16[8,48,1536]{2,1,0:T(8,128)(2,1)S(1)}, bf16[8,48,1536]{2,1,0:T(8,128)(2,1)}, u32[]{:S(2)}) copy-start(bf16[8,48,1536]{2,1,0:T(8,128)(2,1)} %add_convert_fusion) | copy-start | bytes 3538948
  626.2 5.6 copy-start.39
  626.2 5.5 copy-start.62
  629.7 20.3 %copy-start.29 = (bf16[48,768]{1,0:T(8,128)(2,1)S(1)}, bf16[48,768]{1,0:T(8,128)(2,1)}, u32[]{:S(2)}) copy-start(bf16[48,768]{1,0:T(8,128)(2,1)} %fusion.28.refs_2_) | copy-start | bytes 221188
  629.7 22.0 %copy-start.26 = (bf16[48,1152]{1,0:T(8,128)(2,1)S(1)}, bf16[48,1152]{1,0:T(8,128)(2,1)}, u32[]{:S(2)}) copy-start(bf16[48,1152]{1,0:T(8,128)(2,1)} %fusion.24.refs_1_) | copy-start | bytes 331780
  651.7 9.4 %copy-start.21 = (bf16[48,1536]{1,0:T(8,128)(2,1)S(1)}, bf16[48,1536]{1,0:T(8,128)(2,1)}, u32[]{:S(2)}) copy-start(bf16[48,1536]{1,0:T(8,128)(2,1)} %maximum_select_fusion.11.refs_2_) | copy-start | bytes 442372
  653.4 8.7 %copy-start.16 = (bf16[48,2304]{1,0:T(8,128)(2,1)S(1)}, bf16[48,2304]{1,0:T(8,128)(2,1)}, u32[]{:S(2)}) copy-start(bf16[48,2304]{1,0:T(8,128)(2,1)} %maximum_select_fusion.9.refs_1_) | copy-start | bytes 663556
  663.3 2.2 copy-start.7
  663.5 3.3 copy-start.17
  663.5 3.3 copy-start.43
  663.5 3.3 copy-start.44
  663.5 3.3 copy-start.45
  668.1 2.1 copy-start.28
  670.2 1.7 copy-start.19
  (4 other events, 4.1 us)

commit v4 on v3

--- a/solution.py
+++ b/solution.py
@@ -16,9 +16,11 @@
 SINGLE = jnp.float32
 EXACT = lax.Precision.HIGHEST
 GROUP = 128
+WINDOWS = 256
 PAIR = 128
 HEAD = 64
 STRIP = 160
+LONG = 400
 CHUNK = 768
 
 
@@ -109,39 +111,54 @@
     return iota((1, PAIR), 1) < HEAD
 
 
+def both(tensor, value=1.0):
+    return jnp.concatenate((tensor * half(0, value), tensor * half(1, value)), axis=0)
+
+
 def attend(queries, keys, values, mask):
-    outs, logs = [], []
+    rows = queries.shape[0]
+    scores = right_t(both(queries, 1.0 / math.sqrt(HEAD)), keys)
+    weights, totals, logs = [], [], []
     for which in range(2):
-        scores = mask(right_t(queries * half(which, 1.0 / math.sqrt(HEAD)), keys))
-        peak = jnp.max(scores, axis=-1, keepdims=True)
-        weights = jnp.exp(scores - peak)
-        total = jnp.sum(weights, axis=-1, keepdims=True)
-        outs.append(plain(weights.astype(NARROW), values) * (1.0 / total))
+        part = mask(scores[which * rows : (which + 1) * rows])
+        peak = jnp.max(part, axis=-1, keepdims=True)
+        part = jnp.exp(part - peak)
+        total = jnp.sum(part, axis=-1, keepdims=True)
+        weights.append(part.astype(NARROW))
+        totals.append(1.0 / total)
         logs.append(peak + jnp.log(total))
-    return jnp.where(lower_lanes(), outs[0], outs[1]), logs
+    out = plain(jnp.concatenate(weights, axis=0), values)
+    return jnp.where(lower_lanes(), out[:rows] * totals[0], out[rows:] * totals[1]), logs
 
 
 def attend_back(queries, keys, values, upstream, logs, deltas, mask):
     scaled = queries * jnp.asarray(1.0 / math.sqrt(HEAD), NARROW)
-    grads = []
+    count = keys.shape[0]
+    keys = both(keys)
+    turned_keys = keys.T
+    scores = right_t(keys, scaled)
+    inner = right_t(both(values), upstream)
+    weights, slopes = [], []
     for which in range(2):
-        lanes = half(which)
-        scores = mask(right_t(keys * lanes, scaled))
+        span = slice(which * count, (which + 1) * count)
+        part = mask(scores[span])
         if logs is None:
-            weights = jnp.exp(scores - jnp.max(scores, axis=0, keepdims=True))
-            weights = weights * (1.0 / jnp.sum(weights, axis=0, keepdims=True))
+            part = jnp.exp(part - jnp.max(part, axis=0, keepdims=True))
+            part = part * (1.0 / jnp.sum(part, axis=0, keepdims=True))
         else:
-            weights = jnp.exp(scores - logs[which])
-        inner = right_t(values * lanes, upstream)
-        slope = (weights * (inner - deltas[which])).astype(NARROW)
-        grads.append(
-            (
-                left_t(slope, keys),
-                plain(slope, scaled),
-                plain(weights.astype(NARROW), upstream),
-            )
-        )
-    return tuple(jnp.where(lower_lanes(), one, two) for one, two in zip(*grads))
+            part = jnp.exp(part - logs[which])
+        weights.append(part.astype(NARROW))
+        slopes.append((part * (inner[span] - deltas[which])).astype(NARROW))
+    slope = jnp.concatenate(slopes, axis=0)
+    query_grad = plain(turned_keys, slope).T
+    key_grad = plain(slope, scaled)
+    value_grad = plain(jnp.concatenate(weights, axis=0), upstream)
+    lanes = lower_lanes()
+    return (
+        query_grad,
+        jnp.where(lanes, key_grad[:count], key_grad[count:]),
+        jnp.where(lanes, value_grad[:count], value_grad[count:]),
+    )
 
 
 def head_rows(tensor):
@@ -173,8 +190,25 @@
     return jnp.where(hit, 1.0, 0.0).astype(NARROW)
 
 
+def spans(rows, size):
+    edges = [(start, min(start + size, rows)) for start in range(0, rows, size)]
+    if len(edges) > 1 and edges[-1][1] - edges[-1][0] < PAIR:
+        edges[-2:] = [(edges[-2][0], rows)]
+    return edges
+
+
 def mark(log_ref, rows, head, value):
     log_ref[rows, :] = jnp.where(iota((1, PAIR), 1) == head, value, log_ref[rows, :])
+
+
+def store_rows(ref, columns, value):
+    ref[(slice(None),) * (len(ref.shape) - 1) + (columns,)] = value.astype(ref.dtype).reshape(
+        ref.shape[:-1] + value.shape[1:]
+    )
+
+
+def nothing(*unused):
+    return None
 
 
 def copies(semaphores, *pairs):
@@ -236,11 +270,11 @@
 
     loop(3 * features // CHUNK, project)
     window = jnp.where(
-        iota((GROUP, GROUP), 0) // WIN == iota((GROUP, GROUP), 1) // WIN, 0.0, MASKED
+        iota((WINDOWS, WINDOWS), 0) // WIN == iota((WINDOWS, WINDOWS), 1) // WIN, 0.0, MASKED
     )
 
     def group(i):
-        span = at(i, GROUP)
+        span = at(i, WINDOWS)
         for pair in range(features // PAIR):
             lane = pair * PAIR
             out, unused = attend(
@@ -251,7 +285,7 @@
             )
             mw_ref[span, lane : lane + PAIR] = out.astype(NARROW)
 
-    loop(rows // GROUP, group)
+    loop(rows // WINDOWS, group)
     loads[1].wait()
 
     def second(i):
@@ -303,8 +337,8 @@
     logs[...] = jnp.zeros_like(logs)
 
     def pair(p):
-        for strip in range(rows // STRIP):
-            start, end = strip * STRIP, (strip + 1) * STRIP
+        for start in range(0, rows, LONG):
+            end = min(start + LONG, rows)
 
             def mask(scores, start=start):
                 shape = scores.shape
@@ -342,17 +376,17 @@
     loop(2 * features // CHUNK, third)
 
 
-def cross_forward(pieces, cq_ref, ckv_ref, valid_ref, *rest):
-    out_refs, log_refs, (whole, logs) = rest[:pieces], rest[pieces : 2 * pieces], rest[2 * pieces :]
+def cross_forward(pieces, cq_ref, ckv_ref, valid_ref, whole, *rest):
+    log_refs, (logs,) = rest[:pieces], rest[pieces:]
     rows, features = cq_ref.shape
-    part = out_refs[0].shape[0]
+    part = log_refs[0].shape[1]
     logs[...] = jnp.zeros_like(logs)
     if whole.shape[0] > rows:
         whole[rows:, :] = jnp.zeros((whole.shape[0] - rows, features), NARROW)
 
     def pair(p):
-        for strip in range(rows // STRIP):
-            span = slice(strip * STRIP, (strip + 1) * STRIP)
+        for start in range(0, rows, LONG):
+            span = slice(start, min(start + LONG, rows))
             out, sums = attend(
                 cq_ref[span, at(p, PAIR)],
                 ckv_ref[:, at(p, PAIR)],
@@ -365,14 +399,19 @@
 
     loop(features // PAIR, pair)
     for k in range(pieces):
-        out_refs[k][...] = whole[at(piece_at(k, pieces), part), :]
-        log_refs[k][...] = logs[at(piece_at(k, pieces), part), :]
-
-
-def merge_blocks(pieces, *refs):
-    outs, logs = refs[:pieces], refs[pieces : 2 * pieces]
-    co_ref, log_ref = refs[2 * pieces :]
-    features = co_ref.shape[1]
+        log_refs[k][...] = turn(logs[at(piece_at(k, pieces), part), :])
+
+
+def untwist(rows):
+    same = jnp.where(iota((16, PAIR), 0) == iota((16, PAIR), 1), 1.0, 0.0)
+    return dot(rows, same.astype(SINGLE), 0, 0, EXACT)
+
+
+def merge_blocks(pieces, own_ref, *refs):
+    logs, refs = refs[:pieces], refs[pieces:]
+    halves, (co_ref, log_ref) = (refs[: pieces - 1], refs[pieces - 1 : -2]), refs[-2:]
+    part, features = co_ref.shape
+    width = features // 2
     peak = functools.reduce(jnp.maximum, [one[...] for one in logs])
     total = peak + jnp.log(functools.reduce(jnp.add, [jnp.exp(one[...] - peak) for one in logs]))
     log_ref[...] = total
@@ -381,10 +420,14 @@
     ).astype(NARROW)
     result = jnp.zeros(co_ref.shape, SINGLE)
     for k in range(pieces):
-        weight = jnp.exp(logs[k][...] - total)
+        weight = untwist(jnp.exp(logs[k][...] - total))
         high = weight.astype(NARROW)
         low = (weight - high.astype(SINGLE)).astype(NARROW)
-        result = result + (plain(high, spread) + plain(low, spread)) * outs[k][...].astype(SINGLE)
+        if k == 0:
+            block = own_ref[at(place_of(), part), :]
+        else:
+            block = jnp.concatenate((halves[0][k - 1][...], halves[1][k - 1][...]), axis=1)
+        result = result + (plain(high, spread) + plain(low, spread)) * block.astype(SINGLE)
     co_ref[...] = result.astype(NARROW)
 
 
@@ -400,8 +443,8 @@
     bias = jnp.where(iota((1, keys), 1) < length_ref[0], 0.0, MASKED)
 
     def pair(p):
-        for strip in range(rows // GROUP):
-            span = slice(strip * GROUP, (strip + 1) * GROUP)
+        for start in range(0, rows, WINDOWS):
+            span = slice(start, start + WINDOWS)
             out, sums = attend(
                 vq_ref[span, at(p, PAIR)],
                 vkv_ref[:, at(p, PAIR)],
@@ -458,7 +501,7 @@
         loop(rows // GROUP, first)
 
     feed_forward_step(
-        256, normed, up_ref.at[0], down_ref.at[0], cot_ref, hidden, slope, out, grad
+        512, normed, up_ref.at[0], down_ref.at[0], cot_ref, hidden, slope, out, grad
     )
     up_grad_ref[...] = left_t(normed[...], slope[...]).astype(NARROW)
     down_grad_ref[...] = left_t(hidden[...], cot_ref[...]).astype(NARROW)
@@ -511,7 +554,7 @@
         ).astype(NARROW)
 
     feed_forward_step(
-        STRIP, normed, up_ref.at[0], down_ref.at[0], cot_ref, hidden, slope, out, grad
+        LONG, normed, up_ref.at[0], down_ref.at[0], cot_ref, hidden, slope, out, grad
     )
     up_grad_ref[...] = plain(chosen[...], slope[...]).astype(NARROW)
     begins = place_of() * hidden_share
@@ -541,18 +584,21 @@
 
 def reverse_backward(
     pieces, length_ref, dx2_ref, mv_ref, vq_ref, vkv_ref, nx_ref, log_ref, a_out,
-    *rest,
+    *rest, launch=nothing,
 ):
     dvq_ref, weight_ref, rest = rest[0], rest[1], rest[2:]
-    kv_refs, (w_out, rounded, dmv, deltas, dkv, sem) = rest[:pieces], rest[pieces:]
+    k_refs, v_refs, rest = rest[:pieces], rest[pieces : 2 * pieces], rest[2 * pieces :]
+    w_out, rounded, dmv, deltas, dkv, sem = rest
     rows, features = vq_ref.shape
     keys = vkv_ref.shape[0]
-    part = kv_refs[0].shape[0]
+    part = k_refs[0].shape[0]
     (load,) = copies(sem, (a_out.at[3], w_out))
     rounded[...] = dx2_ref[...].astype(NARROW)
     load.wait()
     dmv[...] = right_t(rounded[...], w_out[...]).astype(NARROW)
-    weight_ref[:, features:] = left_t(mv_ref[...], rounded[...]).astype(NARROW)
+    store_rows(
+        weight_ref, slice(features, 2 * features), left_t(mv_ref[...], rounded[...])
+    )
     deltas[...] = head_rows(dmv[...].astype(SINGLE) * mv_ref[...].astype(SINGLE))
     if dkv.shape[0] > keys:
         dkv[keys:, :] = jnp.zeros((dkv.shape[0] - keys, 2 * features), SINGLE)
@@ -583,9 +629,12 @@
                 dkv[0:keys, at(p + features // PAIR, PAIR)] += dv
 
     loop(features // PAIR, pair)
-    weight_ref[:, 0:features] = left_t(nx_ref[...], dvq_ref[...]).astype(NARROW)
+    store_rows(weight_ref, slice(0, features), left_t(nx_ref[...], dvq_ref[...]))
+    launch(1)
     for k in range(pieces):
-        kv_refs[k][...] = dkv[at(piece_at(k, pieces), part), :].astype(NARROW)
+        span = at(piece_at(k, pieces), part)
+        k_refs[k][...] = dkv[span, 0:features].astype(NARROW)
+        v_refs[k][...] = dkv[span, features:].astype(NARROW)
 
 
 def cross_backward(
@@ -598,10 +647,10 @@
         rest[pieces:],
     )
     rows, features = cq_ref.shape
-    part = log_parts[0].shape[0]
+    part = log_parts[0].shape[1]
     (load,) = copies(sem, (a_out.at[2], w_out))
     for k in range(pieces):
-        logs[at(piece_at(k, pieces), part), :] = log_parts[k][...]
+        logs[at(piece_at(k, pieces), part), :] = untwist(log_parts[k][...])
     turned[...] = turn(logs[0:rows, :])
     rounded[...] = dq2_ref[...].astype(NARROW)
     load.wait()
@@ -613,9 +662,7 @@
     deltas[...] = head_rows(dco[...].astype(SINGLE) * co_ref[0:rows, :].astype(SINGLE))
     if dq_all.shape[0] > rows:
         dq_all[rows:, :] = jnp.zeros((dq_all.shape[0] - rows, features), NARROW)
-    edges = [(start, min(start + 256, rows)) for start in range(0, rows, 256)]
-    if len(edges) > 1 and edges[-1][1] - edges[-1][0] < 128:
-        edges[-2:] = [(edges[-2][0], rows)]
+    edges = spans(rows, 512)
 
     def pair(p):
         for number, (start, end) in enumerate(edges):
@@ -643,24 +690,25 @@
         q_refs[k][...] = dq_all[at(piece_at(k, pieces), part), :]
 
 
-def patch_cross_backward(
-    dx2_ref, x1_ref, nx_ref, dvq_ref, dckv_ref, gain_ref, a_in,
-    kv_weight_ref, dx1_ref, norm_ref,
-    w_q, w_kv, sem,
+def patch_backward(
+    x_ref, dx2_ref, x1_ref, nx_ref, n0_ref, pw_ref, mw_ref, dvq_ref, dckv_ref, gain_ref, a_in, a_out,
+    kv_weight_ref, weight_ref, grad_ref, norm_ref,
+    w_in, w_out, w_q, w_kv, dx1, rounded, dmw, deltas, dpw, sem,
+    launch=nothing,
 ):
-    rows, features = dx2_ref.shape
+    rows, features = x_ref.shape
     loads = copies(
         sem,
         (a_in.at[3, :, pl.ds(0, features)], w_q),
         (a_in.at[2, :, pl.ds(features, 2 * features)], w_kv),
+        (a_out.at[0], w_out),
+        (a_in.at[0], w_in),
     )
     norm_ref[...] = jnp.zeros_like(norm_ref)
-
-    def kv_weight(j):
-        span = at(j, CHUNK)
-        kv_weight_ref[:, span] = left_t(nx_ref[...], dckv_ref[:, span]).astype(NARROW)
-
-    loop(2 * features // CHUNK, kv_weight)
+    for start in range(0, 2 * features, CHUNK):
+        span = slice(start, start + CHUNK)
+        store_rows(kv_weight_ref, span, left_t(nx_ref[...], dckv_ref[:, span]))
+    launch(0)
     loads[0].wait()
     loads[1].wait()
 
@@ -668,32 +716,25 @@
         span = at(i, GROUP)
         upstream = right_t(dvq_ref[span, :], w_q[...]) + right_t(dckv_ref[span, :], w_kv[...])
         part, gain, bias = norm_back(x1_ref[span, :], gain_ref[3:4, :], upstream)
-        dx1_ref[span, :] = dx2_ref[span, :] + part
+        total = dx2_ref[span, :] + part
+        dx1[span, :] = total
+        rounded[span, :] = total.astype(NARROW)
         norm_ref[0:1, :] += gain
         norm_ref[1:2, :] += bias
 
     loop(rows // GROUP, first)
-
-
-def window_backward(
-    x_ref, dx1_ref, n0_ref, pw_ref, mw_ref, gain_ref, a_in, a_out,
-    weight_ref, grad_ref, norm_ref,
-    w_in, w_out, rounded, dmw, deltas, dpw, sem,
-):
-    rows, features = x_ref.shape
-    loads = copies(sem, (a_out.at[0], w_out), (a_in.at[0], w_in))
-    norm_ref[...] = jnp.zeros_like(norm_ref)
-    rounded[...] = dx1_ref[...].astype(NARROW)
-    loads[0].wait()
+    loads[2].wait()
     dmw[...] = right_t(rounded[...], w_out[...]).astype(NARROW)
-    weight_ref[:, 3 * features :] = left_t(mw_ref[...], rounded[...]).astype(NARROW)
+    store_rows(
+        weight_ref, slice(3 * features, 4 * features), left_t(mw_ref[...], rounded[...])
+    )
     deltas[...] = head_rows(dmw[...].astype(SINGLE) * mw_ref[...].astype(SINGLE))
     window = jnp.where(
-        iota((GROUP, GROUP), 0) // WIN == iota((GROUP, GROUP), 1) // WIN, 0.0, MASKED
+        iota((WINDOWS, WINDOWS), 0) // WIN == iota((WINDOWS, WINDOWS), 1) // WIN, 0.0, MASKED
     )
 
     def group(i):
-        span = at(i, GROUP)
+        span = at(i, WINDOWS)
         for pair in range(features // PAIR):
             lane = pair * PAIR
             dq, dk, dv = attend_back(
@@ -709,30 +750,29 @@
             dpw[span, features + lane : features + lane + PAIR] = dk.astype(NARROW)
             dpw[span, 2 * features + lane : 2 * features + lane + PAIR] = dv.astype(NARROW)
 
-    loop(rows // GROUP, group)
-
-    def in_weight(j):
-        span = at(j, CHUNK)
-        weight_ref[:, span] = left_t(n0_ref[...], dpw[:, span]).astype(NARROW)
-
-    loop(3 * features // CHUNK, in_weight)
-    loads[1].wait()
+    loop(rows // WINDOWS, group)
+    for start in range(0, 3 * features, CHUNK):
+        span = slice(start, start + CHUNK)
+        store_rows(weight_ref, span, left_t(n0_ref[...], dpw[:, span]))
+    launch(1)
+    loads[3].wait()
 
     def last(i):
         span = at(i, GROUP)
         upstream = right_t(dpw[span, :], w_in[...])
         part, gain, bias = norm_back(x_ref[span, :].astype(SINGLE), gain_ref[0:1, :], upstream)
-        grad_ref[span, :] = dx1_ref[span, :] + part
-        norm_ref[0:1, :] += gain
-        norm_ref[1:2, :] += bias
+        grad_ref[span, :] = dx1[span, :] + part
+        norm_ref[2:3, :] += gain
+        norm_ref[3:4, :] += bias
 
     loop(rows // GROUP, last)
 
 
 def share_backward(
-    pieces, q1_ref, nq_ref, gain_ref, a_in, *rest
+    pieces, q1_ref, nq_ref, gain_ref, a_in, *rest, launch=nothing
 ):
-    q_parts, kv_parts, rest = rest[:pieces], rest[pieces : 2 * pieces], rest[2 * pieces :]
+    parts = [rest[k * pieces : (k + 1) * pieces] for k in range(3)]
+    rest = rest[3 * pieces :]
     grad_ref, weight_ref, norm_ref, w_q, w_kv, summed, sem = rest
     features = q1_ref.shape[1]
     loads = copies(
@@ -740,18 +780,12 @@
         (a_in.at[2, :, pl.ds(0, features)], w_q),
         (a_in.at[3, :, pl.ds(features, 2 * features)], w_kv),
     )
-    summed[:, 0:features] = functools.reduce(
-        jnp.add, [one[...].astype(SINGLE) for one in q_parts]
-    ).astype(NARROW)
-    summed[:, features:] = functools.reduce(
-        jnp.add, [one[...].astype(SINGLE) for one in kv_parts]
-    ).astype(NARROW)
-
-    def weight(j):
-        span = at(j, CHUNK)
-        weight_ref[:, span] = left_t(nq_ref[...], summed[:, span]).astype(NARROW)
-
-    loop(3 * features // CHUNK, weight)
+    for k in range(3):
+        span = slice(k * features, (k + 1) * features)
+        total = functools.reduce(jnp.add, [one[...].astype(SINGLE) for one in parts[k]])
+        summed[:, span] = total.astype(NARROW)
+        store_rows(weight_ref, span, left_t(nq_ref[...], summed[:, span]))
+    launch(1)
     for load in loads:
         load.wait()
     upstream = right_t(summed[:, 0:features], w_q[...]) + right_t(summed[:, features:], w_kv[...])
@@ -792,7 +826,7 @@
     weight_ref[:, 4 * features : 5 * features] = cross_ref[...]
     weight_ref[:, 5 * features :] = jnp.zeros_like(weight_ref[:, 5 * features :])
     deltas[...] = head_rows(dmq[...].astype(SINGLE) * mq_ref[...].astype(SINGLE))
-    edges = [(start, min(start + 256, rows)) for start in range(0, rows, 256)]
+    edges = spans(rows, 256)
 
     def pair(p):
         for number, (start, end) in reversed(list(enumerate(edges))):
@@ -921,15 +955,26 @@
 
 
 class Move:
+    late = None
+
     def __init__(self, source, shape, axis, flip, take=whole):
         self.source, self.shape, self.axis, self.flip, self.take = source, shape, axis, flip, take
 
 
+def in_order(held, rep):
+    for weight in (1, 2):
+        flip = (rep // weight) % 2 == 1
+        held = [jnp.where(flip, held[k ^ weight], held[k]) for k in range(4)]
+    return held
+
+
 class Reduction:
     def __init__(self, tensor):
-        blocks = lax.axis_size("blk")
-        height = tensor.shape[0] // blocks
-        self.tensor = tensor.reshape(blocks, 2, height // 2, tensor.shape[1])
+        if len(tensor.shape) == 2:
+            blocks = lax.axis_size("blk")
+            height = tensor.shape[0] // blocks
+            tensor = tensor.reshape(blocks, 2, height // 2, tensor.shape[1])
+        self.tensor = tensor
 
     def moves(self, stage):
         tensor = self.tensor
@@ -960,7 +1005,7 @@
                      lambda ref, k=k: ref.at[flipped(place_of() // 2, k, length)])
                 for k in range(1, length)
             ]
-        return [Move(tensor, shape, "rep", 2 if stage == "back_x" else 1)]
+        return [Move(tensor, shape, "rep", k) for k in range(1, 4)]
 
     def absorb(self, stage, arrived):
         tensor = self.tensor
@@ -975,11 +1020,9 @@
         elif stage == "z":
             own = pick(tensor, blk // 2, 0)
         else:
-            bit, dim = (rep // 2, tensor.ndim - 1) if stage == "back_x" else (rep % 2, 0)
-            self.tensor = jnp.where(
-                bit == 0,
-                jnp.concatenate((tensor, arrived[0]), axis=dim),
-                jnp.concatenate((arrived[0], tensor), axis=dim),
+            held = in_order([tensor] + list(arrived), rep)
+            self.tensor = jnp.concatenate(
+                [jnp.concatenate((held[k], held[k + 2]), axis=1) for k in range(2)], axis=0
             )
             return
         total = own.astype(SINGLE)
@@ -1016,12 +1059,7 @@
                 total = total + one.astype(SINGLE)
             self.tensor = total.astype(NARROW)
             return
-        held = [self.tensor] + list(arrived)
-        for weight in (1, 2):
-            flip = (rep // weight) % 2 == 1
-            held = [
-                jnp.where(flip, held[k ^ weight], held[k]) for k in range(4)
-            ]
+        held = in_order([self.tensor] + list(arrived), rep)
         self.tensor = jnp.concatenate(held, axis=self.dim)
 
 
@@ -1046,9 +1084,11 @@
     params = {}
     sources = []
     for move in moves:
-        if not any(move.source is one for one in sources):
+        if move.late is None and not any(move.source is one for one in sources):
             sources.append(move.source)
-    number = [next(k for k, one in enumerate(sources) if one is move.source) for move in moves]
+    number = [
+        next((k for k, one in enumerate(sources) if one is move.source), None) for move in moves
+    ]
     fixed_in, fixed_out = len(operands), len(outs)
     partners = sorted({(move.axis, move.flip) for move in moves})
     body_kernel = kernel
@@ -1068,8 +1108,9 @@
 
             def made(k):
                 move = moves[k]
+                late = move.late is not None
                 return pltpu.make_async_remote_copy(
-                    src_ref=move.take(sent[number[k]]),
+                    src_ref=move.take(results[move.late] if late else sent[number[k]]),
                     dst_ref=landed[k],
                     send_sem=send_sem.at[k],
                     recv_sem=recv_sem.at[k],
@@ -1085,8 +1126,12 @@
                         device_id_type=pl.DeviceIdType.MESH,
                     )
                 pl.semaphore_wait(barrier, len(partners))
+                launch(None)
+
+            def launch(which):
                 for k in range(len(moves)):
-                    made(k).start()
+                    if moves[k].late == which:
+                        made(k).start()
 
             def finish():
                 for k in range(len(moves)):
@@ -1094,7 +1139,10 @@
 
             if grid is None:
                 begin()
-                kernel(*ins, *results, *rest)
+                if any(move.late is not None for move in moves):
+                    kernel(*ins, *results, *rest, launch=launch)
+                else:
+                    kernel(*ins, *results, *rest)
                 finish()
             else:
                 pl.when(pl.program_id(0) == 0)(begin)
@@ -1118,10 +1166,6 @@
     return list(result[:fixed_out]), list(result[fixed_out:])
 
 
-def nothing():
-    return None
-
-
 class Courier:
     def __init__(self, active):
         self.active, self.waiting, self.ident = active, [], 0
@@ -1132,8 +1176,11 @@
     def run(self, kernel, outs, operands, specs, scratch, flops, **extra):
         jobs, self.waiting = self.waiting, []
         moves, ends = [], []
-        for job, stage in jobs:
-            moves += job.moves(stage)
+        for job, stage, *late in jobs:
+            added = job.moves(stage)
+            for move in added:
+                move.late = late[0] if late else None
+            moves += added
             ends.append(len(moves))
         if moves:
             self.ident += 1
@@ -1141,7 +1188,9 @@
             kernel, outs, operands, specs, scratch, flops, moves=tuple(moves), ident=self.ident, **extra
         )
         start = 0
-        for (job, stage), end in zip(jobs, ends):
+        for (job, stage, *late), end in zip(jobs, ends):
+            if late:
+                job.tensor = results[late[0]]
             job.absorb(stage, arrived[start:end])
             start = end
         return results
@@ -1156,6 +1205,23 @@
 
     def absorb(self, stage, arrived):
         self.result = self.pieces[:1] + list(arrived)
+
+
+class Pieces:
+    def __init__(self, tensor, part, start, width):
+        self.tensor, self.part, self.start, self.width = tensor, part, start, width
+
+    def moves(self, stage):
+        part, span = self.part, slice(self.start, self.start + self.width)
+        count = lax.axis_size("blk")
+        return [
+            Move(self.tensor, (part, self.width), "blk", k,
+                 lambda ref, k=k: ref.at[at(flipped(place_of(), k, count), part), span])
+            for k in range(1, count)
+        ]
+
+    def absorb(self, stage, arrived):
+        self.result = list(arrived)
 
 
 class Gather:
@@ -1259,17 +1325,18 @@
         count * square * 15,
         semaphores=4,
     )
-    pieces = run(
+    outs, *log_pieces = run(
         functools.partial(cross_forward, blocks),
-        [like(part, features)] * blocks + [like(part, PAIR, kind=SINGLE)] * blocks,
+        [like(padded, features)] + [like(16, part, kind=SINGLE)] * blocks,
         [cq, ckv, valid[None, :]],
         [VMEM, VMEM, VMEM],
-        [((padded, features), NARROW), ((padded, PAIR), SINGLE)],
+        [((padded, PAIR), SINGLE)],
         count * square * 6,
     )
-    outs, logs = Exchange(pieces[:blocks]), Exchange(pieces[blocks:])
+    logs = Exchange(log_pieces)
+    halves = [Pieces(outs, part, k * features // 2, features // 2) for k in range(2)]
     if carried:
-        courier.load((outs, ""), (logs, ""))
+        courier.load((logs, ""), (halves[0], ""))
     mv, x2, log_v = run(
         reverse_forward,
         [like(rows, features), like(rows, features, kind=SINGLE), like(16, rows, kind=SINGLE)],
@@ -1279,21 +1346,8 @@
         rows * square * 8,
         semaphores=1,
     )
-    if not carried:
-        outs.result, logs.result = exchange(outs.pieces), exchange(logs.pieces)
-    merged = run(
-        functools.partial(merge_blocks, blocks),
-        [like(part, features), like(part, PAIR, kind=SINGLE)],
-        outs.result + logs.result,
-        [VMEM] * (2 * blocks),
-        [],
-        padded * square,
-    )
-    co_parts, log_parts = Gather(merged[0]), Gather(merged[1])
     if carried:
-        courier.load((co_parts, ""), (log_parts, ""))
-    else:
-        co_parts.result, log_parts.result = gather(merged[0]), gather(merged[1])
+        courier.load((halves[1], ""))
     fixed = lambda *shape: pl.BlockSpec(shape, lambda j: (0,) * len(shape))
     x3, dx2, up_x, down_x, norm_five = run(
         patch_feed_forward,
@@ -1319,11 +1373,34 @@
         ],
     )
     if carried:
+        merged = run(
+            functools.partial(merge_blocks, blocks),
+            [like(part, features), like(16, part, kind=SINGLE)],
+            [outs] + logs.result + halves[0].result + halves[1].result,
+            [VMEM] * (3 * blocks - 1),
+            [],
+            padded * square,
+        )
+        co_parts, log_parts = Gather(merged[0]), Gather(merged[1])
         up_x, down_x = Reduction(up_x), Reduction(down_x)
-        courier.load((up_x, "core"), (down_x, "core"))
-    dvq, reverse_weight, *kv_pieces = run(
+        reverse_weight = Reduction(like(blocks, 2, share // 2, 2 * features))
+        courier.load(
+            (co_parts, ""), (log_parts, ""), (up_x, "core"), (down_x, "core"),
+            (reverse_weight, "core", 1),
+        )
+    else:
+        whole_logs = jnp.stack(exchange(log_pieces))
+        merged_log = jax.nn.logsumexp(whole_logs, axis=0)
+        weights = jnp.transpose(jnp.exp(whole_logs - merged_log)[:, :HEADS], (0, 2, 1))
+        shares = lax.all_to_all(outs.reshape(blocks, part, features), "blk", 0, 0)
+        merged_out = jnp.sum(jnp.repeat(weights, HEAD, axis=2) * shares.astype(SINGLE), axis=0)
+        co_parts, log_parts = Gather(None), Gather(None)
+        co_parts.result, log_parts.result = gather(merged_out.astype(NARROW)), gather(merged_log)
+    folded = (blocks, 2, share // 2) if carried else (features,)
+    dvq, reverse_grad, *kv_pieces = run(
         functools.partial(reverse_backward, blocks),
-        [like(rows, features), like(features, 2 * features)] + [like(part, 2 * features)] * blocks,
+        [like(rows, features), like(*folded, 2 * features)]
+        + [like(part, features)] * (2 * blocks),
         [answer_length, dx2, mv, vq, vkv, nx, log_v, attn_out],
         [SMEM, VMEM, VMEM, VMEM, VMEM, VMEM, VMEM, ANY],
         [((features, features), NARROW), ((rows, features), NARROW), ((rows, features), NARROW),
@@ -1331,12 +1408,11 @@
         rows * square * 16,
         semaphores=1,
     )
-    kv_parts = Exchange(kv_pieces)
+    k_parts, v_parts = Exchange(kv_pieces[:blocks]), Exchange(kv_pieces[blocks:])
     if carried:
-        reverse_weight = Reduction(reverse_weight)
-        courier.load((up_x, "x"), (down_x, "x"), (reverse_weight, "core"), (kv_parts, ""))
+        courier.load((up_x, "x"), (k_parts, ""))
     else:
-        kv_parts.result = exchange(kv_pieces)
+        k_parts.result, v_parts.result = exchange(k_parts.pieces), exchange(v_parts.pieces)
     q3, dq2, up_q, down_q, norm_four, co = run(
         functools.partial(query_feed_forward, blocks, share, hidden_share),
         [
@@ -1363,9 +1439,7 @@
     )
     if carried:
         up_q, down_q = RepSum(up_q, 1), RepSum(down_q, 0)
-        courier.load(
-            (up_x, "y"), (down_x, "y"), (reverse_weight, "x"), (up_q, "out"), (down_q, "out")
-        )
+        courier.load((down_x, "x"), (v_parts, ""), (up_x, "y"))
     dckv, cross_out_weight, *q_pieces = run(
         functools.partial(cross_backward, blocks, share),
         [like(rows, 2 * features), like(share_rows, features)] + [like(part, features)] * blocks,
@@ -1379,60 +1453,57 @@
     )
     q_parts = Exchange(q_pieces)
     if carried:
-        courier.load((q_parts, ""), (reverse_weight, "y"), (up_q, "back"), (down_q, "back"))
+        kv_weight = Reduction(like(blocks, 2, share // 2, 2 * features))
+        window_weight = Reduction(like(blocks, 2, share // 2, 4 * features))
+        courier.load(
+            (q_parts, ""), (down_x, "y"), (reverse_weight, "x"), (up_q, "out"), (down_q, "out"),
+            (kv_weight, "core", 0), (window_weight, "core", 1),
+        )
     else:
         q_parts.result = exchange(q_pieces)
-    kv_weight, dx1, norm_three = run(
-        patch_cross_backward,
+    kv_grad, window_grad, grad_x, norm_x = run(
+        patch_backward,
         [
-            like(features, 2 * features), like(rows, features, kind=SINGLE),
-            like(8, features, kind=SINGLE),
+            like(*folded, 2 * features), like(*folded, 4 * features),
+            like(rows, features, kind=SINGLE), like(8, features, kind=SINGLE),
         ],
-        [dx2, x1, nx, dvq, dckv, norm_gain, attn_in],
-        [VMEM] * 6 + [ANY],
-        [((features, features), NARROW), ((features, 2 * features), NARROW)],
-        rows * square * 12,
-        semaphores=2,
-    )
-    dq1_share, share_weight, norm_two = run(
+        [x, dx2, x1, nx, n0, pw, mw, dvq, dckv, norm_gain, attn_in, attn_out],
+        [VMEM] * 10 + [ANY, ANY],
+        [((features, wide), NARROW), ((features, features), NARROW),
+         ((features, features), NARROW), ((features, 2 * features), NARROW),
+         ((rows, features), SINGLE), ((rows, features), NARROW), ((rows, features), NARROW),
+         ((16, rows), SINGLE), ((rows, wide), NARROW)],
+        rows * square * 24,
+        semaphores=4,
+    )
+    if carried:
+        share_weight = Reduction(like(blocks, 2, share // 2, wide))
+        courier.load((share_weight, "core", 1))
+    dq1_share, share_grad, norm_two = run(
         functools.partial(share_backward, blocks),
-        [like(part, features), like(features, wide), like(8, features, kind=SINGLE)],
-        [own_rows(q1), own_rows(nq), norm_gain, attn_in] + q_parts.result + kv_parts.result,
-        [VMEM, VMEM, VMEM, ANY] + [VMEM] * (2 * blocks),
+        [like(part, features), like(*folded, wide), like(8, features, kind=SINGLE)],
+        [own_rows(q1), own_rows(nq), norm_gain, attn_in]
+        + q_parts.result + k_parts.result + v_parts.result,
+        [VMEM, VMEM, VMEM, ANY] + [VMEM] * (3 * blocks),
         [((features, features), NARROW), ((features, 2 * features), NARROW),
          ((part, wide), NARROW)],
         part * square * 6,
         semaphores=2,
     )
     dq1_parts = Gather(dq1_share)
+
+    def arrive(*jobs):
+        courier.load(*jobs)
+        run(nothing, [], [], [], [], 0)
+
     if carried:
-        kv_weight, share_weight = Reduction(kv_weight), Reduction(share_weight)
+        arrive((dq1_parts, ""), (window_weight, "x"), (reverse_weight, "y"))
         courier.load(
-            (dq1_parts, ""), (up_x, "z"), (down_x, "z"), (reverse_weight, "z"),
-            (kv_weight, "core"), (share_weight, "core"),
+            (up_x, "z"), (down_x, "z"), (reverse_weight, "z"), (window_weight, "y"),
+            (share_weight, "y"), (kv_weight, "x"), (up_q, "back"), (down_q, "back"),
         )
     else:
         dq1_parts.result = gather(dq1_share)
-    window_weight, grad_x, norm_zero = run(
-        window_backward,
-        [
-            like(features, 4 * features), like(rows, features, kind=SINGLE),
-            like(8, features, kind=SINGLE),
-        ],
-        [x, dx1, n0, pw, mw, norm_gain, attn_in, attn_out],
-        [VMEM] * 6 + [ANY, ANY],
-        [((features, wide), NARROW), ((features, features), NARROW),
-         ((rows, features), NARROW), ((rows, features), NARROW),
-         ((16, rows), SINGLE), ((rows, wide), NARROW)],
-        rows * square * 16,
-        semaphores=2,
-    )
-    if carried:
-        window_weight = Reduction(window_weight)
-        courier.load(
-            (window_weight, "core"), (kv_weight, "x"), (share_weight, "y"),
-            (up_x, "back_x"), (down_x, "back_x"), (reverse_weight, "back_x"),
-        )
     causal_weight, grad_q, norm_one = run(
         functools.partial(causal_backward, blocks, share),
         [
@@ -1450,27 +1521,23 @@
     )
     norms = jnp.stack(
         (
-            norm_zero[0], norm_one[0] * leader, norm_two[0], norm_three[0], norm_four[0] * leader,
-            norm_five[0], norm_zero[1], norm_one[1] * leader, norm_two[1], norm_three[1],
+            norm_x[2], norm_one[0] * leader, norm_two[0], norm_x[0], norm_four[0] * leader,
+            norm_five[0], norm_x[3], norm_one[1] * leader, norm_two[1], norm_x[1],
             norm_four[1] * leader, norm_five[1],
         )
     )
     if carried:
         norms = Norms(jnp.pad(norms, ((0, 4), (0, 0))))
         causal_weight = RepSum(causal_weight, 1)
-        arrive = lambda *jobs: (courier.load(*jobs), run(nothing, [], [], [], [], 0))
         arrive(
-            (window_weight, "x"), (share_weight, "x"), (kv_weight, "y"), (norms, "out"),
-            (causal_weight, "out"), (up_x, "back_core"), (down_x, "back_core"),
-            (reverse_weight, "back_core"),
+            (share_weight, "x"), (causal_weight, "out"), (norms, "out"), (kv_weight, "y"),
+            (window_weight, "z"),
         )
         arrive(
-            (window_weight, "y"), (share_weight, "z"), (kv_weight, "z"), (norms, "back"),
-            (causal_weight, "back"),
+            (share_weight, "z"), (kv_weight, "z"), (causal_weight, "back"), (norms, "back"),
+            (up_x, "back"), (down_x, "back"), (reverse_weight, "back"), (window_weight, "back"),
         )
-        arrive((window_weight, "z"), (share_weight, "back_x"), (kv_weight, "back_x"))
-        arrive((window_weight, "back_x"), (share_weight, "back_core"), (kv_weight, "back_core"))
-        arrive((window_weight, "back_core"))
+        arrive((share_weight, "back"), (kv_weight, "back"))
         up_x, down_x, reverse_weight, window_weight, kv_weight, share_weight, causal_weight = (
             one.tensor
             for one in (
@@ -1481,7 +1548,7 @@
     else:
         up_x, down_x, reverse_weight, window_weight, kv_weight, share_weight = (
             reduce_all(one)
-            for one in (up_x, down_x, reverse_weight, window_weight, kv_weight, share_weight)
+            for one in (up_x, down_x, reverse_grad, window_grad, kv_grad, share_grad)
         )
         up_q, down_q = reduce_rep(up_q[:share]), reduce_rep(down_q[:hidden_share])
         causal_weight = reduce_rep(causal_weight[:share])

time: 683 us -> 524 us (0.77)
  Pallas kernels: 577 us -> 429 us
  other arithmetic: 75.2 us -> 68.1 us
    pallas_call x18 -> x16, Pallas kernels: 577 us -> 429 us  [call(): pl.pallas_call(body_kernel, out_shape=list(outs) + [like(*m.shape, kind=m...]
    select_n x15 -> x9, other arithmetic: 11.5 us -> 3.49 us  [in_order(): held = [jnp.where(flip, held[k ^ weight], held[k]) for k in range(4)]]
where the time goes in v4:
time: 524 us; the launch traced here: 515 us
  Pallas kernels  429 us (82%)
  other arithmetic  68.1 us (13%)
  local copies, waits for them, and re-layouts  15.5 us (3%)
    pallas_call x16, Pallas kernels, call(): pl.pallas_call(body_kernel, out_shape=list(outs) + [like(*m.shape, kind=m...  429 us
    convert_element_type x26, other arithmetic, absorb(): self.tensor = total.astype(NARROW)  53.2 us

profile of v4, /device:TPU:0, one launch (start us, length us, event | category | flops | bytes accessed | tf_op | source)
XLA Modules:
  0.0 514.8 jit_solution(18407054089179358536)
XLA Ops:
  2.8 0.9 select_n.631.refs_4_
  3.7 15.2 %shard_map.195 = (bf16[512,768]{1,0:T(8,128)(2,1)}, bf16[512,2304]{1,0:T(8,128)(2,1)}, bf16[512,768]{1,0:T(8,128)(2,1)}, f32[512,768]{1,0:T(8,128)}, bf16[512,76...) custom-call(bf16[512,768]{1,0:T(8,128)(2,1)} %bitcast.154, f32[6,768]{1,0:T(8,128)} %refs_7_.3, ...), custom_call_target="tpu_custom_call" | custom-call | flops 5435817984 | bytes 19697664 | tf_op jit(solution)/shard_map/pallas_call | solution.py:1152
  18.9 30.0 %shard_map.196 = (bf16[800,768]{1,0:T(8,128)(2,1)}, bf16[800,2304]{1,0:T(8,128)(2,1)}, bf16[800,768]{1,0:T(8,128)(2,1)}, f32[800,768]{1,0:T(8,128)}, bf16[800,76...) custom-call(bf16[800,768]{1,0:T(8,128)(2,1)} %bitcast.151, ...), custom_call_target="tpu_custom_call" | custom-call | flops 14155776000 | bytes 20140032 | tf_op jit(solution)/shard_map/pallas_call | solution.py:1152
  48.9 1.6 pad_dynamic-slice_fusion.1.refs_1_
  50.5 1.7 pad_dynamic-slice_fusion.refs_0_
  52.2 12.6 %shard_map.197 = (bf16[896,768]{1,0:T(8,128)(2,1)}, f32[16,112]{1,0:T(8,128)}, f32[16,112]{1,0:T(8,128)}, f32[16,112]{1,0:T(8,128)}, f32[16,112]{1,0:T(8,128)}, ...) custom-call(bf16[800,768]{1,0:T(8,128)(2,1)} %get-tuple-element.236.cq_ref.refs_2_, ...), custom_call_target="tpu_custom_call" | custom-call | flops 5662310400 | bytes 2803712 | tf_op jit(solution)/shard_map/pallas_call | solution.py:1152
  64.8 24.6 %shard_map.198 = (bf16[512,768]{1,0:T(8,128)(2,1)}, f32[512,768]{1,0:T(8,128)}, f32[16,512]{1,0:T(8,128)}, f32[16,112]{1,0:T(8,128)}, f32[16,112]{1,0:T(8,128)},...) custom-call(s32[1]{0:T(128)S(6)} %copy.67.refs_0_, ...), custom_call_target="tpu_custom_call" | custom-call | flops 4831838208 | bytes 9535492 | tf_op jit(solution)/shard_map/pallas_call | solution.py:1152
  89.4 30.8 %shard_map.199 = (bf16[512,768]{1,0:T(8,128)(2,1)}, f32[512,768]{1,0:T(8,128)}, bf16[768,3072]{1,0:T(8,128)(2,1)}, bf16[3072,768]{1,0:T(8,128)(2,1)}, f32[8,768]...) custom-call(f32[512,768]{1,0:T(8,128)} %get-tuple-element.246.refs_0, ...), custom_call_target="tpu_custom_call" | custom-call | flops 14495514624 | bytes 21270528 | tf_op jit(solution)/shard_map/pallas_call | solution.py:1152
  120.2 4.8 shard_map.200
  125.0 39.9 %shard_map.201 = (bf16[512,768]{1,0:T(8,128)(2,1)}, bf16[8,2,48,1536]{3,2,1,0:T(8,128)(2,1)}, bf16[112,768]{1,0:T(8,128)(2,1)}, bf16[112,768]{1,0:T(8,128)(2,1)}...) custom-call(s32[1]{0:T(128)S(6)} %copy.67.refs_0_, ...), custom_call_target="tpu_custom_call" | custom-call | flops 9663676416 | bytes 11141124 | tf_op jit(solution)/shard_map/pallas_call | solution.py:1152
  164.9 4.5 fusion.1.refs_14_
  169.5 2.4 fusion.2.refs_15_
  171.8 1.4 fusion.5.refs_20_
  173.2 39.4 %shard_map.202 = (bf16[800,768]{1,0:T(8,128)(2,1)}, f32[800,768]{1,0:T(8,128)}, bf16[96,3072]{1,0:T(8,128)(2,1)}, bf16[384,768]{1,0:T(8,128)(2,1)}, f32[8,768]{1...) custom-call(f32[800,768]{1,0:T(8,128)} %get-tuple-element.248.refs_0, ...), custom_call_target="tpu_custom_call" | custom-call | flops 16986931200 | bytes 28692480 | tf_op jit(solution)/shard_map/pallas_call | solution.py:1152
  212.6 0.8 slice_multiply_fusion
  213.4 2.6 add_convert_fusion.2
  216.1 1.1 constant_dynamic-slice_fusion.8
  217.2 0.8 copy.35
  218.0 33.3 %shard_map.203 = (bf16[512,1536]{1,0:T(8,128)(2,1)}, bf16[96,768]{1,0:T(8,128)(2,1)}, bf16[112,768]{1,0:T(8,128)(2,1)}, bf16[112,768]{1,0:T(8,128)(2,1)}, bf16[1...) custom-call(f32[800,768]{1,0:T(8,128)} %get-tuple-element.299.refs_0, ...), custom_call_target="tpu_custom_call" | custom-call | flops 11324620800 | bytes 11413504 | tf_op jit(solution)/shard_map/pallas_call | solution.py:1152
  251.3 2.1 fusion.9.refs_18_
  253.4 1.3 add_convert_fusion.1
  254.8 39.3 %shard_map.204 = (bf16[8,2,48,1536]{3,2,1,0:T(8,128)(2,1)}, bf16[8,2,48,3072]{3,2,1,0:T(8,128)(2,1)}, f32[512,768]{1,0:T(8,128)}, f32[8,768]{1,0:T(8,128)}, bf16...) custom-call(bf16[512,768]{1,0:T(8,128)(2,1)} %bitcast.155, ...), custom_call_target="tpu_custom_call" | custom-call | flops 14495514624 | bytes 29902848 | tf_op jit(solution)/shard_map/pallas_call | solution.py:1152
  294.1 2.4 add_convert_fusion.7
  296.4 2.1 fusion.8.refs_19_
  298.6 1.0 add_convert_fusion.4
  299.5 2.8 fusion.4.refs_23_
  302.3 9.6 %shard_map.205 = (bf16[112,768]{1,0:T(8,128)(2,1)}, bf16[8,2,48,2304]{3,2,1,0:T(8,128)(2,1)}, f32[8,768]{1,0:T(8,128)}, bf16[8,48,2304]{2,1,0:T(8,128)(2,1)}) custom-call(f32[112,768]{1,0:T(8,128)} %pad_dynamic-slice_fusion.refs_0_, bf16[112,768]{1,0:T(8,128)(2,1)} %pad_dynamic-slice_fusion.1.refs_1_, f32[6,768]{1,0:T(8,128)} %refs_7_.3, ...), custom_call_target="tpu_custom_call" | custom-call | flops 792723456 | bytes 18819072 | tf_op jit(solution)/shard_map/pallas_call | solution.py:1152
  311.9 0.8 fusion.54
  312.7 3.8 fusion.3
  316.5 2.4 fusion.refs_1_
  318.9 34.4 %shard_map.206 = (bf16[112,768]{1,0:T(8,128)(2,1)}, bf16[112,768]{1,0:T(8,128)(2,1)}, bf16[112,768]{1,0:T(8,128)(2,1)}, bf16[112,768]{1,0:T(8,128)(2,1)}, bf16[1...) custom-call(bf16[112,768]{1,0:T(8,128)(2,1)} %get-tuple-element.361., ...), custom_call_target="tpu_custom_call" | custom-call | tf_op jit(solution)/shard_map/pallas_call | solution.py:1152
  353.3 2.7 add_convert_fusion
  356.0 0.8 fusion.17.refs_20_
  356.8 45.6 %shard_map.207 = (bf16[96,4096]{1,0:T(8,128)(2,1)}, f32[800,768]{1,0:T(8,128)}, f32[8,768]{1,0:T(8,128)}, bf16[48,1536]{1,0:T(8,128)(2,1)}, bf16[48,1536]{1,0:T(...) custom-call(bf16[800,768]{1,0:T(8,128)(2,1)} %bitcast.152, ...), custom_call_target="tpu_custom_call" | custom-call | flops 15099494400 | bytes 30298112 | tf_op jit(solution)/shard_map/pallas_call | solution.py:1152
  402.5 1.8 fusion.45.refs_6_
  404.2 2.0 fusion.32.refs_5_
  406.2 1.9 fusion.35.refs_4_
  408.1 2.2 fusion.7.refs_4_
  410.2 2.0 add_convert_fusion.3
  412.3 1.1 fusion.6.refs_0_
  413.4 1.3 constant_dynamic-slice_fusion.7
  414.8 0.9 copy.45
  415.7 0.8 slice_multiply_fusion.1
  417.5 23.4 %shard_map.208 = (bf16[4,48,1152]{2,1,0:T(8,128)(2,1)}, bf16[96,1024]{1,0:T(8,128)(2,1)}, bf16[96,1024]{1,0:T(8,128)(2,1)}, bf16[96,1024]{1,0:T(8,128)(2,1)}, f3...) custom-call(bf16[4,48,2304]{2,1,0:T(8,128)(2,1)} %fusion.6.refs_0_, ...), custom_call_target="tpu_custom_call" | custom-call | tf_op jit(solution)/shard_map/pallas_call | solution.py:1152
  440.9 2.0 fusion.29.refs_7_
  442.9 2.0 add_convert_fusion.6.refs_2_
  445.0 1.7 fusion.16.refs_1_
  446.7 0.9 add_convert_fusion.5.refs_0_
  448.2 35.1 %shard_map.209 = (bf16[48,1152]{1,0:T(8,128)(2,1)}, bf16[48,1152]{1,0:T(8,128)(2,1)}, bf16[48,1152]{1,0:T(8,128)(2,1)}, bf16[48,768]{1,0:T(8,128)(2,1)}, bf16[48...) custom-call(bf16[4,48,1152]{2,1,0:T(8,128)(2,1)} %add_convert_fusion, ...), custom_call_target="tpu_custom_call" | custom-call | tf_op jit(solution)/shard_map/pallas_call | solution.py:1152
  483.4 1.7 fusion.42.refs_1_
  485.1 1.8 fusion.38.refs_0_
  486.9 0.8 add.335
  487.7 0.9 fusion.46
  489.2 1.0 broadcast_select_fusion.66
  491.8 10.9 %shard_map.210 = (bf16[48,1152]{1,0:T(8,128)(2,1)}, bf16[48,1152]{1,0:T(8,128)(2,1)}, bf16[48,1152]{1,0:T(8,128)(2,1)}, bf16[48,768]{1,0:T(8,128)(2,1)}, bf16[48...) custom-call(bf16[48,1152]{1,0:T(8,128)(2,1)} %fusion.38.refs_0_, bf16[48,768]{1,0:T(8,128)(2,1)} %fusion.42.refs_1_), custom_call_target="tpu_custom_call" | custom-call | tf_op jit(solution)/shard_map/pallas_call | solution.py:1152
  502.8 1.1 broadcast_select_fusion.52
  503.9 1.0 broadcast_select_fusion.70
  505.2 1.1 maximum_convert_fusion.3
  506.3 1.6 maximum_convert_fusion.2
  507.9 1.6 maximum_convert_fusion.1
  509.4 2.1 maximum_convert_fusion
  511.5 0.9 copy.68
  512.4 0.8 copy-done.15
  513.2 1.1 copy.69
  (147 shorter events, 5.5 us)
Async XLA Ops:
  125.0 44.4 %slice-start.2 = ((s8[4718592]{0:T(1024)(128)(4,1)}), s8[4194304]{0:T(1024)(128)(4,1)S(1)}, s32[]{:S(2)}) async-start(s8[4718592]{0:T(1024)(128)(4,1)} %bitcast.135), calls=%async_computation.2 | async-start | bytes 8388608
  125.0 44.4 %slice-start.3 = ((s8[4718592]{0:T(1024)(128)(4,1)}), s8[524288]{0:T(1024)(128)(4,1)S(1)}, s32[]{:S(2)}) async-start(s8[4718592]{0:T(1024)(128)(4,1)} %bitcast.135), calls=%async_computation.3 | async-start | bytes 1048576
  164.9 4.6 copy-start.13
  169.4 2.4 copy-start.20
  169.4 2.4 copy-start.29
  173.2 40.2 %copy-start.3 = (bf16[8,48,3072]{2,1,0:T(8,128)(2,1)S(1)}, bf16[8,48,3072]{2,1,0:T(8,128)(2,1)}, u32[]{:S(2)}) copy-start(bf16[8,48,3072]{2,1,0:T(8,128)(2,1)} %fusion.2.refs_15_) | copy-start | bytes 7077892
  218.0 33.3 %copy-start.11 = (bf16[8,48,1536]{2,1,0:T(8,128)(2,1)S(1)}, bf16[8,48,1536]{2,1,0:T(8,128)(2,1)}, u32[]{:S(2)}) copy-start(bf16[8,48,1536]{2,1,0:T(8,128)(2,1)} %add_convert_fusion.2) | copy-start | bytes 3538948
  218.0 35.4 %copy-start.2 = (bf16[8,192,768]{2,1,0:T(8,128)(2,1)S(1)}, bf16[8,192,768]{2,1,0:T(8,128)(2,1)}, u32[]{:S(2)}) copy-start(bf16[8,192,768]{2,1,0:T(8,128)(2,1)} %fusion.1.refs_14_) | copy-start | bytes 7077892
  251.3 2.1 copy-start.21
  294.0 2.4 copy-start.10
  294.0 4.5 copy-start.7
  294.1 4.5 copy-start.30
  296.4 3.1 copy-start.19
  299.5 17.0 %slice-start = ((s8[4718592]{0:T(1024)(128)(4,1)}), s8[4194304]{0:T(1024)(128)(4,1)S(1)}, s32[]{:S(2)}) async-start(s8[4718592]{0:T(1024)(128)(4,1)} %bitcast.132), calls=%async_computation | async-start | bytes 8388608
  302.3 9.6 %copy-start.55 = (f32[8,768]{1,0:T(8,128)S(1)}, f32[8,768]{1,0:T(8,128)}, u32[]{:S(2)}) copy-start(f32[8,768]{1,0:T(8,128)} %get-tuple-element.387) | copy-start | bytes 73732
  302.3 14.2 %slice-start.1 = ((s8[4718592]{0:T(1024)(128)(4,1)}), s8[524288]{0:T(1024)(128)(4,1)S(1)}, s32[]{:S(2)}) async-start(s8[4718592]{0:T(1024)(128)(4,1)} %bitcast.132), calls=%async_computation.1 | async-start | bytes 1048576
  312.7 3.8 copy-start.12
  318.9 34.4 %copy-start = (bf16[8,48,3072]{2,1,0:T(8,128)(2,1)S(1)}, bf16[8,48,3072]{2,1,0:T(8,128)(2,1)}, u32[]{:S(2)}) copy-start(bf16[8,48,3072]{2,1,0:T(8,128)(2,1)} %fusion.refs_1_) | copy-start | bytes 7077892
  353.3 2.7 copy-start.6
  353.3 2.7 copy-start.33
  402.4 5.6 %copy-start.9 = (bf16[8,48,1536]{2,1,0:T(8,128)(2,1)S(1)}, bf16[8,48,1536]{2,1,0:T(8,128)(2,1)}, u32[]{:S(2)}) copy-start(bf16[8,48,1536]{2,1,0:T(8,128)(2,1)} %add_convert_fusion) | copy-start | bytes 3538948
  404.2 6.0 %copy-start.8 = (bf16[8,48,1536]{2,1,0:T(8,128)(2,1)S(1)}, bf16[8,48,1536]{2,1,0:T(8,128)(2,1)}, u32[]{:S(2)}) copy-start(bf16[8,48,1536]{2,1,0:T(8,128)(2,1)} %fusion.4.refs_23_) | copy-start | bytes 3538948
  408.0 4.2 copy-start.4
  408.1 4.2 copy-start.23
  412.3 5.0 copy-start.28
  412.3 5.0 copy-start.46
  412.3 5.0 copy-start.47
  412.3 4.9 copy-start.48
  414.7 2.6 copy-start.27
  414.7 2.6 copy-start.40
  414.7 2.6 copy-start.41
  414.7 2.6 copy-start.42
  440.9 4.1 copy-start.5
  440.9 5.8 %copy-start.1 = (bf16[4,48,2304]{2,1,0:T(8,128)(2,1)S(1)}, bf16[4,48,2304]{2,1,0:T(8,128)(2,1)}, u32[]{:S(2)}) copy-start(bf16[4,48,2304]{2,1,0:T(8,128)(2,1)} %fusion.6.refs_0_) | copy-start | bytes 2654212
  440.9 5.8 %copy-start.32 = (bf16[4,48,1152]{2,1,0:T(8,128)(2,1)S(1)}, bf16[4,48,1152]{2,1,0:T(8,128)(2,1)}, u32[]{:S(2)}) copy-start(bf16[4,48,1152]{2,1,0:T(8,128)(2,1)} %get-tuple-element.399) | copy-start | bytes 1327108
  442.9 4.7 copy-start.52
  442.9 4.7 copy-start.53
  442.9 4.7 copy-start.54
  447.6 41.6 %copy-start.25 = (bf16[48,768]{1,0:T(8,128)(2,1)S(1)}, bf16[48,768]{1,0:T(8,128)(2,1)}, u32[]{:S(2)}) copy-start(bf16[48,768]{1,0:T(8,128)(2,1)} %fusion.45.refs_6_) | copy-start | bytes 221188
  448.2 38.6 %copy-start.31 = (f32[16,768]{1,0:T(8,128)S(1)}, f32[16,768]{1,0:T(8,128)}, u32[]{:S(2)}) copy-start(f32[16,768]{1,0:T(8,128)} %add_add_fusion.refs_3_) | copy-start | bytes 147460
  483.3 6.9 %copy-start.18 = (bf16[48,1536]{1,0:T(8,128)(2,1)S(1)}, bf16[48,1536]{1,0:T(8,128)(2,1)}, u32[]{:S(2)}) copy-start(bf16[48,1536]{1,0:T(8,128)(2,1)} %fusion.29.refs_7_) | copy-start | bytes 442372
  483.3 6.9 %copy-start.49 = (bf16[48,1536]{1,0:T(8,128)(2,1)S(1)}, bf16[48,1536]{1,0:T(8,128)(2,1)}, u32[]{:S(2)}) copy-start(bf16[48,1536]{1,0:T(8,128)(2,1)} %get-tuple-element.425) | copy-start | bytes 442372
  483.3 6.9 %copy-start.50 = (bf16[48,1536]{1,0:T(8,128)(2,1)S(1)}, bf16[48,1536]{1,0:T(8,128)(2,1)}, u32[]{:S(2)}) copy-start(bf16[48,1536]{1,0:T(8,128)(2,1)} %get-tuple-element.424) | copy-start | bytes 442372
  483.4 6.9 %copy-start.51 = (bf16[48,1536]{1,0:T(8,128)(2,1)S(1)}, bf16[48,1536]{1,0:T(8,128)(2,1)}, u32[]{:S(2)}) copy-start(bf16[48,1536]{1,0:T(8,128)(2,1)} %get-tuple-element.423) | copy-start | bytes 442372
  490.3 0.9 copy-start.17
  490.3 1.0 copy-start.43
  490.3 1.0 copy-start.44
  490.3 1.1 copy-start.45
  490.4 1.1 copy-start.16
  490.4 1.1 copy-start.37
  490.5 1.2 copy-start.38
  490.5 1.2 copy-start.39
  491.7 11.0 %copy-start.22 = (bf16[48,1152]{1,0:T(8,128)(2,1)S(1)}, bf16[48,1152]{1,0:T(8,128)(2,1)}, u32[]{:S(2)}) copy-start(bf16[48,1152]{1,0:T(8,128)(2,1)} %fusion.38.refs_0_) | copy-start | bytes 331780
  491.7 12.2 %copy-start.26 = (bf16[48,768]{1,0:T(8,128)(2,1)S(1)}, bf16[48,768]{1,0:T(8,128)(2,1)}, u32[]{:S(2)}) copy-start(bf16[48,768]{1,0:T(8,128)(2,1)} %fusion.42.refs_1_) | copy-start | bytes 221188
  502.7 2.3 copy-start.14
  502.7 2.3 copy-start.34
  502.7 2.3 copy-start.35
  502.8 2.3 copy-start.36
  509.4 2.1 copy-start.24
  511.5 1.7 copy-start.15

commit v5 on v4

--- a/solution.py
+++ b/solution.py
@@ -365,13 +365,16 @@
         nq_ref[span, :] = norm(total, gain_ref[2:3, :], bias_ref[2:3, :]).astype(NARROW)
 
     loop(rows // STRIP, second)
+    if q1_ref.shape[0] > rows:
+        q1_ref[rows:, :] = jnp.zeros_like(q1_ref[rows:, :])
+        nq_ref[rows:, :] = jnp.zeros_like(nq_ref[rows:, :])
     loads[2].wait()
-    cq_ref[...] = plain(nq_ref[...], w_q[...]).astype(NARROW)
+    cq_ref[...] = plain(nq_ref[0:rows, :], w_q[...]).astype(NARROW)
     loads[3].wait()
 
     def third(j):
         span = at(j, CHUNK)
-        vkv_ref[:, span] = plain(nq_ref[...], w_kv[:, span]).astype(NARROW)
+        vkv_ref[:, span] = plain(nq_ref[0:rows, :], w_kv[:, span]).astype(NARROW)
 
     loop(2 * features // CHUNK, third)
 
@@ -521,24 +524,33 @@
         loop(rows // GROUP, last)
 
 
+def place_parts(ref, pieces, parts):
+    part, features = parts[0].shape
+    width = features // 2
+    ref[at(piece_at(0, pieces), part), :] = parts[0][...]
+    for k in range(1, pieces):
+        for number in range(2):
+            ref[at(piece_at(k, pieces), part), number * width : (number + 1) * width] = parts[
+                number * (pieces - 1) + k
+            ][...]
+
+
 def query_feed_forward(
     pieces, share, hidden_share, q1_ref, cot_ref, gain_ref, bias_ref,
     w_out, up_ref, down_ref, *rest,
 ):
-    parts, rest = rest[:pieces], rest[pieces:]
+    parts, rest = rest[: 2 * pieces - 1], rest[2 * pieces - 1 :]
     (
         q3_ref, dq2_ref, up_grad_ref, down_grad_ref, norm_ref, co_ref,
         q2, normed, chosen, hidden, slope, out, grad,
     ) = rest
     rows, features = q1_ref.shape
-    part = parts[0].shape[0]
     width = up_ref.shape[2]
     step = pl.program_id(0)
 
     @pl.when(step == 0)
     def begin():
-        for k in range(pieces):
-            co_ref[at(piece_at(k, pieces), part), :] = parts[k][...]
+        place_parts(co_ref, pieces, parts)
 
         def first(i):
             span = at(i, STRIP)
@@ -584,7 +596,7 @@
 
 def reverse_backward(
     pieces, length_ref, dx2_ref, mv_ref, vq_ref, vkv_ref, nx_ref, log_ref, a_out,
-    *rest, launch=nothing,
+    *rest, launch=nothing, tick=nothing,
 ):
     dvq_ref, weight_ref, rest = rest[0], rest[1], rest[2:]
     k_refs, v_refs, rest = rest[:pieces], rest[pieces : 2 * pieces], rest[2 * pieces :]
@@ -605,6 +617,8 @@
     size = 256
 
     def pair(p):
+        pl.when(p == 2)(lambda: tick(1))
+        pl.when(p == 4)(lambda: tick(2))
         for strip in range(rows // size):
             span = slice(strip * size, (strip + 1) * size)
 
@@ -769,17 +783,20 @@
 
 
 def share_backward(
-    pieces, q1_ref, nq_ref, gain_ref, a_in, *rest, launch=nothing
+    pieces, q1, nq, gain_ref, a_in, *rest, launch=nothing
 ):
     parts = [rest[k * pieces : (k + 1) * pieces] for k in range(3)]
     rest = rest[3 * pieces :]
-    grad_ref, weight_ref, norm_ref, w_q, w_kv, summed, sem = rest
-    features = q1_ref.shape[1]
-    loads = copies(
+    grad_ref, weight_ref, norm_ref, w_q, w_kv, summed, q1_ref, nq_ref, sem = rest
+    part, features = q1_ref.shape
+    *loads, load_q, load_n = copies(
         sem,
         (a_in.at[2, :, pl.ds(0, features)], w_q),
         (a_in.at[3, :, pl.ds(features, 2 * features)], w_kv),
-    )
+        (q1.at[at(place_of(), part), :], q1_ref),
+        (nq.at[at(place_of(), part), :], nq_ref),
+    )
+    load_n.wait()
     for k in range(3):
         span = slice(k * features, (k + 1) * features)
         total = functools.reduce(jnp.add, [one[...].astype(SINGLE) for one in parts[k]])
@@ -789,8 +806,9 @@
     for load in loads:
         load.wait()
     upstream = right_t(summed[:, 0:features], w_q[...]) + right_t(summed[:, features:], w_kv[...])
-    part, gain, bias = norm_back(q1_ref[...], gain_ref[2:3, :], upstream)
-    grad_ref[...] = part.astype(NARROW)
+    load_q.wait()
+    piece, gain, bias = norm_back(q1_ref[...], gain_ref[2:3, :], upstream)
+    grad_ref[...] = piece.astype(NARROW)
     norm_ref[...] = jnp.zeros_like(norm_ref)
     norm_ref[0:1, :] = gain
     norm_ref[1:2, :] = bias
@@ -800,16 +818,14 @@
     pieces, share, q_ref, dq2_ref, n1_ref, pq_ref, mq_ref, log_ref, cross_ref, gain_ref,
     a_in, a_out, *rest
 ):
-    parts, rest = rest[:pieces], rest[pieces:]
+    parts, rest = rest[: 2 * pieces - 1], rest[2 * pieces - 1 :]
     (
         weight_ref, grad_ref, norm_ref,
         w_in, w_out, gathered, dq1, rounded, dmq, deltas, dkv, dpq, sem,
     ) = rest
     rows, features = q_ref.shape
-    part = parts[0].shape[0]
     loads = copies(sem, (a_out.at[1], w_out), (a_in.at[1], w_in))
-    for k in range(pieces):
-        gathered[at(piece_at(k, pieces), part), :] = parts[k][...]
+    place_parts(gathered, pieces, parts)
 
     def first(i):
         span = at(i, STRIP)
@@ -954,11 +970,18 @@
     return ref
 
 
+class Fold:
+    def __init__(self, own, take, arrived, shape, keep=whole, keep_shape=None):
+        self.own, self.take, self.arrived, self.shape = own, take, arrived, shape
+        self.keep, self.keep_shape = keep, keep_shape or shape
+
+
 class Move:
     late = None
 
-    def __init__(self, source, shape, axis, flip, take=whole):
+    def __init__(self, source, shape, axis, flip, take=whole, phase=0):
         self.source, self.shape, self.axis, self.flip, self.take = source, shape, axis, flip, take
+        self.phase = phase
 
 
 def in_order(held, rep):
@@ -968,67 +991,83 @@
     return held
 
 
+def lanes_of(ref, start, width):
+    return ref.at[(slice(None),) * (len(ref.shape) - 1) + (pl.ds(start, width),)]
+
+
 class Reduction:
     def __init__(self, tensor):
         if len(tensor.shape) == 2:
             blocks = lax.axis_size("blk")
             height = tensor.shape[0] // blocks
-            tensor = tensor.reshape(blocks, 2, height // 2, tensor.shape[1])
-        self.tensor = tensor
+            tensor = tensor.reshape(blocks // 2, 2, 2, height // 2, tensor.shape[1])
+        self.tensor, self.take, self.arrived, self.shape = tensor, whole, [], tensor.shape
+
+    def fold(self, keep=whole, keep_shape=None):
+        return Fold(self.tensor, self.take, self.arrived, self.shape, keep, keep_shape)
 
     def moves(self, stage):
-        tensor = self.tensor
-        shape = tensor.shape
+        shape = self.shape
         if stage == "core":
+            self.next = shape[:2] + shape[3:]
             return [
-                Move(tensor, shape[:1] + shape[2:], "rep", 1,
-                     lambda ref: ref.at[:, 1 - place_of("rep") % 2])
+                Move(self.tensor, self.next, "rep", 1,
+                     lambda ref: ref.at[:, :, 1 - place_of("rep") % 2])
             ]
         if stage == "x":
             width = shape[-1] // 2
-
-            def columns(ref):
-                span = pl.ds(pl.multiple_of((1 - place_of("rep") // 2) * width, width), width)
-                return ref.at[(slice(None),) * (len(shape) - 1) + (span,)]
-
-            return [Move(tensor, shape[:-1] + (width,), "rep", 2, columns)]
+            self.next = shape[:-1] + (width,)
+
+            def own(ref):
+                return lanes_of(ref, pl.multiple_of((place_of("rep") // 2) * width, width), width)
+
+            def other(ref):
+                start = (1 - place_of("rep") // 2) * width
+                return lanes_of(ref, pl.multiple_of(start, width), width)
+
+            return [Move(self.fold(own, self.next), self.next, "rep", 2, other)]
         if stage == "y":
-            tensor = self.tensor = tensor.reshape((shape[0] // 2, 2) + shape[1:])
-            return [
-                Move(tensor, tensor.shape[:1] + shape[1:], "blk", 1,
-                     lambda ref: ref.at[:, 1 - place_of() % 2])
-            ]
+            self.next = shape[:1] + shape[2:]
+            fold = self.fold(lambda ref: ref.at[:, place_of() % 2], self.next)
+            return [Move(fold, self.next, "blk", 1, lambda ref: ref.at[:, 1 - place_of() % 2])]
         if stage == "z":
             length = shape[0]
+            self.next = shape[1:]
+            fold = self.fold(lambda ref: ref.at[place_of() // 2], self.next)
             return [
-                Move(tensor, shape[1:], "blk", 2 * k,
+                Move(fold, self.next, "blk", 2 * k,
                      lambda ref, k=k: ref.at[flipped(place_of() // 2, k, length)])
                 for k in range(1, length)
             ]
-        return [Move(tensor, shape, "rep", k) for k in range(1, 4)]
-
-    def absorb(self, stage, arrived):
-        tensor = self.tensor
-        rep, blk = lax.axis_index("rep"), lax.axis_index("blk")
+        if stage == "back":
+            fold = self.fold()
+            return [Move(fold, shape, "rep", k) for k in range(1, 4)]
+        if stage == "back_x":
+            return [Move(self.fold(), shape, "rep", 2)]
+        return [Move(self.tensor, shape, "rep", 1), Move(self.other, shape, "rep", 1)]
+
+    def absorb(self, stage, arrived, kept):
         if stage == "core":
-            own = pick(tensor, rep % 2, 1)
-        elif stage == "x":
-            width = tensor.shape[-1] // 2
-            own = lax.dynamic_slice_in_dim(tensor, (rep // 2) * width, width, tensor.ndim - 1)
-        elif stage == "y":
-            own = pick(tensor, blk % 2, 1)
-        elif stage == "z":
-            own = pick(tensor, blk // 2, 0)
+            self.take = lambda ref: ref.at[:, :, place_of("rep") % 2]
         else:
-            held = in_order([tensor] + list(arrived), rep)
+            self.take = whole
+        if kept:
+            self.tensor = kept[0]
+        if stage in ("back", "back_x", "back_core"):
+            if stage == "back_x":
+                self.other = arrived[0]
+                return
+            rep = lax.axis_index("rep")
+            if stage == "back":
+                held = [self.tensor] + list(arrived)
+            else:
+                held = [self.tensor, arrived[0], self.other, arrived[1]]
+            held = in_order(held, rep)
             self.tensor = jnp.concatenate(
                 [jnp.concatenate((held[k], held[k + 2]), axis=1) for k in range(2)], axis=0
             )
             return
-        total = own.astype(SINGLE)
-        for one in arrived:
-            total = total + one.astype(SINGLE)
-        self.tensor = total.astype(NARROW)
+        self.shape, self.arrived = self.next, list(arrived)
 
 
 class RepSum:
@@ -1036,31 +1075,115 @@
         self.tensor, self.dim = tensor, dim
 
     def moves(self, stage):
-        shape = list(self.tensor.shape)
         if stage == "out":
-            size = shape[self.dim] = shape[self.dim] // 4
+            self.shape = list(self.tensor.shape)
+            size = self.shape[self.dim] = self.shape[self.dim] // 4
 
             def quarter(ref, k):
                 span = pl.ds(pl.multiple_of(flipped(place_of("rep"), k, 4) * size, size), size)
                 return ref.at[span, :] if self.dim == 0 else ref.at[:, span]
 
+            self.quarter = quarter
             return [
-                Move(self.tensor, tuple(shape), "rep", k, lambda ref, k=k: quarter(ref, k))
+                Move(self.tensor, tuple(self.shape), "rep", k, lambda ref, k=k: quarter(ref, k))
                 for k in range(1, 4)
             ]
-        return [Move(self.tensor, tuple(shape), "rep", k) for k in range(1, 4)]
-
-    def absorb(self, stage, arrived):
-        rep = lax.axis_index("rep")
+        fold = Fold(
+            self.tensor, lambda ref: self.quarter(ref, 0), self.arrived, tuple(self.shape)
+        )
+        return [Move(fold, tuple(self.shape), "rep", k) for k in range(1, 4)]
+
+    def absorb(self, stage, arrived, kept):
         if stage == "out":
-            size = self.tensor.shape[self.dim] // 4
-            total = lax.dynamic_slice_in_dim(self.tensor, rep * size, size, self.dim).astype(SINGLE)
-            for one in arrived:
-                total = total + one.astype(SINGLE)
-            self.tensor = total.astype(NARROW)
+            self.arrived = list(arrived)
             return
-        held = in_order([self.tensor] + list(arrived), rep)
+        held = in_order([kept[0]] + list(arrived), lax.axis_index("rep"))
         self.tensor = jnp.concatenate(held, axis=self.dim)
+
+
+class Exchange:
+    def __init__(self, pieces):
+        self.pieces = pieces
+
+    def moves(self, stage):
+        return [Move(one, one.shape, "blk", k) for k, one in enumerate(self.pieces) if k]
+
+    def absorb(self, stage, arrived, kept):
+        self.result = self.pieces[:1] + list(arrived)
+
+
+class Pieces:
+    def __init__(self, tensor, part, start, width):
+        self.tensor, self.part, self.start, self.width = tensor, part, start, width
+
+    def moves(self, stage):
+        part, span = self.part, slice(self.start, self.start + self.width)
+        count = lax.axis_size("blk")
+        return [
+            Move(self.tensor, (part, self.width), "blk", k,
+                 lambda ref, k=k: ref.at[at(flipped(place_of(), k, count), part), span])
+            for k in range(1, count)
+        ]
+
+    def absorb(self, stage, arrived, kept):
+        self.result = list(arrived)
+
+
+class Gather:
+    def __init__(self, tensor):
+        self.tensor = tensor
+
+    def moves(self, stage):
+        return [
+            Move(self.tensor, self.tensor.shape, "blk", k) for k in range(1, lax.axis_size("blk"))
+        ]
+
+    def absorb(self, stage, arrived, kept):
+        self.result = [self.tensor] + list(arrived)
+
+
+class Spread:
+    def __init__(self, tensor):
+        self.tensor = tensor
+
+    def moves(self, stage):
+        count = lax.axis_size("blk")
+        rows, width = self.tensor.shape[0], self.tensor.shape[1] // 2
+        moves, self.places = [], []
+        for number in range(2):
+            span = slice(number * width, (number + 1) * width)
+            own = lambda ref, span=span: ref.at[:, span]
+            along = []
+            for k in range(2, count, 2):
+                along.append(Move(self.tensor, (rows, width), "blk", k, own, number))
+                self.places.append((number, k))
+            moves += along
+            moves.append(Move(self.tensor, (rows, width), "blk", 1, own, number + 1))
+            self.places.append((number, 1))
+            for one in along:
+                moves.append(Move(one, (rows, width), "blk", 1, whole, number + 1))
+                self.places.append((number, one.flip + 1))
+        return moves
+
+    def absorb(self, stage, arrived, kept):
+        found = dict(zip(self.places, arrived))
+        count = lax.axis_size("blk")
+        self.result = [found[number, k] for number in range(2) for k in range(1, count)]
+
+
+class Norms:
+    def __init__(self, tensor):
+        self.tensor = tensor
+
+    def moves(self, stage):
+        axis = "rep" if stage == "out" else "blk"
+        return [
+            Move(self.tensor, self.tensor.shape, axis, k) for k in range(1, lax.axis_size(axis))
+        ]
+
+    def absorb(self, stage, arrived, kept):
+        for one in arrived:
+            self.tensor = self.tensor + one
 
 
 VMEM = pl.BlockSpec(memory_space=pltpu.VMEM)
@@ -1072,9 +1195,13 @@
     return jax.ShapeDtypeStruct(shape, kind)
 
 
+def index_of(items, item):
+    return next(k for k, one in enumerate(items) if one is item)
+
+
 def call(
     kernel, outs, operands, specs, scratch, flops, grid=None, out_specs=None, semaphores=0,
-    moves=(), ident=None,
+    moves=(), ident=None, ticking=False,
 ):
     scratch = [pltpu.VMEM(shape, kind) for shape, kind in scratch]
     if semaphores:
@@ -1082,18 +1209,33 @@
     out_specs = [VMEM] * len(outs) if out_specs is None else out_specs
     extra = {} if grid is None else {"grid": grid}
     params = {}
-    sources = []
+    sources, folds = [], []
+
+    def need(array):
+        if not any(array is one for one in sources):
+            sources.append(array)
+
     for move in moves:
-        if move.late is None and not any(move.source is one for one in sources):
-            sources.append(move.source)
-    number = [
-        next((k for k, one in enumerate(sources) if one is move.source), None) for move in moves
-    ]
+        if isinstance(move.source, Fold):
+            if not any(move.source is one for one in folds):
+                folds.append(move.source)
+                for array in [move.source.own] + move.source.arrived:
+                    need(array)
+        elif move.late is None and not isinstance(move.source, Move):
+            need(move.source)
     fixed_in, fixed_out = len(operands), len(outs)
     partners = sorted({(move.axis, move.flip) for move in moves})
     body_kernel = kernel
+    lasts = max([move.phase for move in moves], default=0)
     if moves:
         params = {"collective_id": ident, "has_side_effects": True}
+        terms = sum(1 + len(fold.arrived) for fold in folds)
+        for fold in folds:
+            scratch += [pltpu.VMEM(fold.shape, NARROW)] * (1 + len(fold.arrived))
+        scratch += [
+            pltpu.SemaphoreType.DMA((max(terms, 1),)),
+            pltpu.SemaphoreType.DMA((max(len(folds), 1),)),
+        ]
         scratch += [pltpu.SemaphoreType.DMA((len(moves),))] * 2
 
         def body_kernel(*refs):
@@ -1101,16 +1243,34 @@
             sent, refs = refs[: len(sources)], refs[len(sources) :]
             results, refs = refs[:fixed_out], refs[fixed_out:]
             landed, refs = refs[: len(moves)], refs[len(moves) :]
-            rest, (send_sem, recv_sem) = refs[:-2], refs[-2:]
+            kept, refs = refs[: len(folds)], refs[len(folds) :]
+            rest, refs = refs[: len(refs) - 4 - terms], refs[len(refs) - 4 - terms :]
+            buffers, (load_sem, keep_sem, send_sem, recv_sem) = refs[:terms], refs[terms:]
+            before = {}
+            for move in moves:
+                if isinstance(move.source, Move):
+                    number = index_of(moves, move.source)
+                    before[number] = min(move.phase, before.get(number, move.phase))
 
             def target(axis, flip):
                 return {axis: flipped(lax.axis_index(axis), flip, lax.axis_size(axis))}
 
+            def buffers_of(fold):
+                start = sum(1 + len(one.arrived) for one in folds[: index_of(folds, fold)])
+                return start, buffers[start : start + 1 + len(fold.arrived)]
+
             def made(k):
                 move = moves[k]
-                late = move.late is not None
+                if move.late is not None:
+                    source = results[move.late]
+                elif isinstance(move.source, Fold):
+                    source = buffers_of(move.source)[1][0]
+                elif isinstance(move.source, Move):
+                    source = landed[index_of(moves, move.source)]
+                else:
+                    source = sent[index_of(sources, move.source)]
                 return pltpu.make_async_remote_copy(
-                    src_ref=move.take(results[move.late] if late else sent[number[k]]),
+                    src_ref=move.take(source),
                     dst_ref=landed[k],
                     send_sem=send_sem.at[k],
                     recv_sem=recv_sem.at[k],
@@ -1118,7 +1278,43 @@
                     device_id_type=pl.DeviceIdType.MESH,
                 )
 
+            def loads(fold):
+                start, held = buffers_of(fold)
+                return [
+                    pltpu.make_async_copy(
+                        (fold.take if k == 0 else whole)(sent[index_of(sources, array)]),
+                        held[k],
+                        load_sem.at[start + k],
+                    )
+                    for k, array in enumerate([fold.own] + fold.arrived)
+                ]
+
+            def keeping(k):
+                fold = folds[k]
+                return pltpu.make_async_copy(
+                    fold.keep(buffers_of(fold)[1][0]), kept[k], keep_sem.at[k]
+                )
+
+            def add(fold):
+                held = buffers_of(fold)[1]
+
+                def one(index):
+                    if len(held) == 2:
+                        held[0][index] = held[0][index] + held[1][index]
+                    elif len(held) > 2:
+                        held[0][index] = functools.reduce(
+                            jnp.add, [part[index].astype(SINGLE) for part in held]
+                        ).astype(NARROW)
+
+                if len(fold.shape) == 2:
+                    one((slice(None), slice(None)))
+                else:
+                    loop(fold.shape[0], one)
+
             def begin():
+                for fold in folds:
+                    for load in loads(fold):
+                        load.start()
                 barrier = pltpu.get_barrier_semaphore()
                 for axis, flip in partners:
                     pl.semaphore_signal(
@@ -1126,36 +1322,68 @@
                         device_id_type=pl.DeviceIdType.MESH,
                     )
                 pl.semaphore_wait(barrier, len(partners))
-                launch(None)
+                for k, move in enumerate(moves):
+                    if move.phase == 0 and move.late is None and not isinstance(move.source, Fold):
+                        made(k).start()
+                for number, fold in enumerate(folds):
+                    for load in loads(fold):
+                        load.wait()
+                    add(fold)
+                    for k, move in enumerate(moves):
+                        if move.source is fold:
+                            made(k).start()
+                    keeping(number).start()
 
             def launch(which):
                 for k in range(len(moves)):
                     if moves[k].late == which:
                         made(k).start()
 
+            def tick(phase):
+                for k, needed in before.items():
+                    if needed == phase:
+                        made(k).wait_recv()
+                for k, move in enumerate(moves):
+                    if move.phase == phase:
+                        made(k).start()
+
             def finish():
+                if not ticking:
+                    for phase in range(1, lasts + 1):
+                        tick(phase)
                 for k in range(len(moves)):
-                    made(k).wait()
-
+                    made(k).wait_send()
+                    if k not in before:
+                        made(k).wait_recv()
+                for k in range(len(folds)):
+                    keeping(k).wait()
+
+            options = {}
+            if any(move.late is not None for move in moves):
+                options["launch"] = launch
+            if ticking:
+                options["tick"] = tick
             if grid is None:
                 begin()
-                if any(move.late is not None for move in moves):
-                    kernel(*ins, *results, *rest, launch=launch)
-                else:
-                    kernel(*ins, *results, *rest)
+                kernel(*ins, *results, *rest, **options)
                 finish()
             else:
                 pl.when(pl.program_id(0) == 0)(begin)
-                kernel(*ins, *results, *rest)
+                kernel(*ins, *results, *rest, **options)
                 pl.when(pl.program_id(0) == pl.num_programs(0) - 1)(finish)
 
     result = pl.pallas_call(
         body_kernel,
-        out_shape=list(outs) + [like(*m.shape, kind=m.source.dtype) for m in moves],
+        out_shape=list(outs)
+        + [
+            like(*m.shape, kind=m.source.dtype if hasattr(m.source, "dtype") else NARROW)
+            for m in moves
+        ]
+        + [like(*fold.keep_shape) for fold in folds],
         in_specs=list(specs) + [ANY] * len(sources),
-        out_specs=list(out_specs) + [ANY] * len(moves),
+        out_specs=list(out_specs) + [ANY] * (len(moves) + len(folds)),
         scratch_shapes=scratch,
-        compiler_params=pltpu.CompilerParams(vmem_limit_bytes=56 * 2**20, **params),
+        compiler_params=pltpu.CompilerParams(vmem_limit_bytes=60 * 2**20, **params),
         cost_estimate=pl.CostEstimate(
             flops=int(flops),
             bytes_accessed=sum(o.size * o.dtype.itemsize for o in operands),
@@ -1163,7 +1391,8 @@
         ),
         **extra,
     )(*operands, *sources)
-    return list(result[:fixed_out]), list(result[fixed_out:])
+    end = fixed_out + len(moves)
+    return list(result[:fixed_out]), list(result[fixed_out:end]), (folds, list(result[end:]))
 
 
 class Courier:
@@ -1184,72 +1413,28 @@
             ends.append(len(moves))
         if moves:
             self.ident += 1
-        results, arrived = call(
+        results, arrived, (folds, kept) = call(
             kernel, outs, operands, specs, scratch, flops, moves=tuple(moves), ident=self.ident, **extra
         )
         start = 0
         for (job, stage, *late), end in zip(jobs, ends):
             if late:
                 job.tensor = results[late[0]]
-            job.absorb(stage, arrived[start:end])
+            own = [
+                kept[k]
+                for k, fold in enumerate(folds)
+                if any(move.source is fold for move in moves[start:end])
+            ]
+            job.absorb(stage, arrived[start:end], own)
             start = end
         return results
 
 
-class Exchange:
-    def __init__(self, pieces):
-        self.pieces = pieces
-
-    def moves(self, stage):
-        return [Move(one, one.shape, "blk", k) for k, one in enumerate(self.pieces) if k]
-
-    def absorb(self, stage, arrived):
-        self.result = self.pieces[:1] + list(arrived)
-
-
-class Pieces:
-    def __init__(self, tensor, part, start, width):
-        self.tensor, self.part, self.start, self.width = tensor, part, start, width
-
-    def moves(self, stage):
-        part, span = self.part, slice(self.start, self.start + self.width)
-        count = lax.axis_size("blk")
-        return [
-            Move(self.tensor, (part, self.width), "blk", k,
-                 lambda ref, k=k: ref.at[at(flipped(place_of(), k, count), part), span])
-            for k in range(1, count)
-        ]
-
-    def absorb(self, stage, arrived):
-        self.result = list(arrived)
-
-
-class Gather:
-    def __init__(self, tensor):
-        self.tensor = tensor
-
-    def moves(self, stage):
-        return [
-            Move(self.tensor, self.tensor.shape, "blk", k) for k in range(1, lax.axis_size("blk"))
-        ]
-
-    def absorb(self, stage, arrived):
-        self.result = [self.tensor] + list(arrived)
-
-
-class Norms:
-    def __init__(self, tensor):
-        self.tensor = tensor
-
-    def moves(self, stage):
-        axis = "rep" if stage == "out" else "blk"
-        return [
-            Move(self.tensor, self.tensor.shape, axis, k) for k in range(1, lax.axis_size(axis))
-        ]
-
-    def absorb(self, stage, arrived):
-        for one in arrived:
-            self.tensor = self.tensor + one
+def in_halves(arrays):
+    width = arrays[0].shape[1] // 2
+    return (
+        arrays[:1] + [one[:, :width] for one in arrays[1:]] + [one[:, width:] for one in arrays[1:]]
+    )
 
 
 def body(
@@ -1289,10 +1474,6 @@
     def own_columns(tensor):
         return lax.dynamic_slice_in_dim(tensor, place * share, share, 1)
 
-    def own_rows(tensor):
-        tensor = jnp.pad(tensor, ((0, padded - count), (0, 0)))
-        return lax.dynamic_slice_in_dim(tensor, place * part, part, 0)
-
     square = 2.0 * features * features
     run = courier.run
 
@@ -1314,7 +1495,7 @@
         causal_forward,
         [
             like(count, features), like(count, wide), like(count, features),
-            like(count, features, kind=SINGLE), like(count, features), like(count, features),
+            like(padded, features, kind=SINGLE), like(padded, features), like(count, features),
             like(count, 2 * features), like(16, count, kind=SINGLE),
         ],
         [q, norm_gain, norm_bias, attn_in, attn_out],
@@ -1381,9 +1562,9 @@
             [],
             padded * square,
         )
-        co_parts, log_parts = Gather(merged[0]), Gather(merged[1])
+        co_parts, log_parts = Spread(merged[0]), Gather(merged[1])
         up_x, down_x = Reduction(up_x), Reduction(down_x)
-        reverse_weight = Reduction(like(blocks, 2, share // 2, 2 * features))
+        reverse_weight = Reduction(like(blocks // 2, 2, 2, share // 2, 2 * features))
         courier.load(
             (co_parts, ""), (log_parts, ""), (up_x, "core"), (down_x, "core"),
             (reverse_weight, "core", 1),
@@ -1394,9 +1575,10 @@
         weights = jnp.transpose(jnp.exp(whole_logs - merged_log)[:, :HEADS], (0, 2, 1))
         shares = lax.all_to_all(outs.reshape(blocks, part, features), "blk", 0, 0)
         merged_out = jnp.sum(jnp.repeat(weights, HEAD, axis=2) * shares.astype(SINGLE), axis=0)
-        co_parts, log_parts = Gather(None), Gather(None)
-        co_parts.result, log_parts.result = gather(merged_out.astype(NARROW)), gather(merged_log)
-    folded = (blocks, 2, share // 2) if carried else (features,)
+        co_parts, log_parts = Spread(None), Gather(None)
+        co_parts.tensor, *co_parts.result = in_halves(gather(merged_out.astype(NARROW)))
+        log_parts.result = gather(merged_log)
+    folded = (blocks // 2, 2, 2, share // 2) if carried else (features,)
     dvq, reverse_grad, *kv_pieces = run(
         functools.partial(reverse_backward, blocks),
         [like(rows, features), like(*folded, 2 * features)]
@@ -1407,10 +1589,11 @@
          ((16, rows), SINGLE), ((padded, 2 * features), SINGLE)],
         rows * square * 16,
         semaphores=1,
+        ticking=carried,
     )
     k_parts, v_parts = Exchange(kv_pieces[:blocks]), Exchange(kv_pieces[blocks:])
     if carried:
-        courier.load((up_x, "x"), (k_parts, ""))
+        courier.load((k_parts, ""), (up_x, "x"), (reverse_weight, "x"))
     else:
         k_parts.result, v_parts.result = exchange(k_parts.pieces), exchange(v_parts.pieces)
     q3, dq2, up_q, down_q, norm_four, co = run(
@@ -1419,13 +1602,15 @@
             like(count, features), like(count, features, kind=SINGLE), like(share_rows, hidden),
             like(hidden_rows, features), like(8, features, kind=SINGLE), like(padded, features),
         ],
-        [q1, cot_q, norm_gain, norm_bias, attn_out, mlp_in, mlp_out] + co_parts.result,
+        [q1, cot_q, norm_gain, norm_bias, attn_out, mlp_in, mlp_out, co_parts.tensor]
+        + co_parts.result,
         [
             fixed(count, features), fixed(count, features), fixed(6, features),
             fixed(6, features), pl.BlockSpec((1, features, features), lambda j: (2, 0, 0)),
             pl.BlockSpec((1, features, CHUNK), lambda j: (1, 0, j)),
             pl.BlockSpec((1, CHUNK, features), lambda j: (1, j, 0)),
-        ] + [fixed(part, features)] * blocks,
+            fixed(part, features),
+        ] + [fixed(part, features // 2)] * (2 * blocks - 2),
         [((count, features), SINGLE), ((count, features), NARROW), ((share_rows, count), NARROW),
          ((count, CHUNK), NARROW), ((count, CHUNK), NARROW),
          ((count, features), SINGLE), ((count, features), SINGLE)],
@@ -1439,7 +1624,7 @@
     )
     if carried:
         up_q, down_q = RepSum(up_q, 1), RepSum(down_q, 0)
-        courier.load((down_x, "x"), (v_parts, ""), (up_x, "y"))
+        courier.load((v_parts, ""), (down_x, "x"), (up_x, "y"))
     dckv, cross_out_weight, *q_pieces = run(
         functools.partial(cross_backward, blocks, share),
         [like(rows, 2 * features), like(share_rows, features)] + [like(part, features)] * blocks,
@@ -1453,10 +1638,10 @@
     )
     q_parts = Exchange(q_pieces)
     if carried:
-        kv_weight = Reduction(like(blocks, 2, share // 2, 2 * features))
-        window_weight = Reduction(like(blocks, 2, share // 2, 4 * features))
+        kv_weight = Reduction(like(blocks // 2, 2, 2, share // 2, 2 * features))
+        window_weight = Reduction(like(blocks // 2, 2, 2, share // 2, 4 * features))
         courier.load(
-            (q_parts, ""), (down_x, "y"), (reverse_weight, "x"), (up_q, "out"), (down_q, "out"),
+            (q_parts, ""), (down_x, "y"), (reverse_weight, "y"), (up_q, "out"), (down_q, "out"),
             (kv_weight, "core", 0), (window_weight, "core", 1),
         )
     else:
@@ -1477,33 +1662,33 @@
         semaphores=4,
     )
     if carried:
-        share_weight = Reduction(like(blocks, 2, share // 2, wide))
+        share_weight = Reduction(like(blocks // 2, 2, 2, share // 2, wide))
         courier.load((share_weight, "core", 1))
     dq1_share, share_grad, norm_two = run(
         functools.partial(share_backward, blocks),
         [like(part, features), like(*folded, wide), like(8, features, kind=SINGLE)],
-        [own_rows(q1), own_rows(nq), norm_gain, attn_in]
+        [q1, nq, norm_gain, attn_in]
         + q_parts.result + k_parts.result + v_parts.result,
-        [VMEM, VMEM, VMEM, ANY] + [VMEM] * (3 * blocks),
+        [ANY, ANY, VMEM, ANY] + [VMEM] * (3 * blocks),
         [((features, features), NARROW), ((features, 2 * features), NARROW),
-         ((part, wide), NARROW)],
+         ((part, wide), NARROW), ((part, features), SINGLE), ((part, features), NARROW)],
         part * square * 6,
-        semaphores=2,
-    )
-    dq1_parts = Gather(dq1_share)
+        semaphores=4,
+    )
+    dq1_parts = Spread(dq1_share)
 
     def arrive(*jobs):
         courier.load(*jobs)
         run(nothing, [], [], [], [], 0)
 
     if carried:
-        arrive((dq1_parts, ""), (window_weight, "x"), (reverse_weight, "y"))
+        arrive((dq1_parts, ""), (window_weight, "x"))
         courier.load(
             (up_x, "z"), (down_x, "z"), (reverse_weight, "z"), (window_weight, "y"),
             (share_weight, "y"), (kv_weight, "x"), (up_q, "back"), (down_q, "back"),
         )
     else:
-        dq1_parts.result = gather(dq1_share)
+        dq1_parts.tensor, *dq1_parts.result = in_halves(gather(dq1_share))
     causal_weight, grad_q, norm_one = run(
         functools.partial(causal_backward, blocks, share),
         [
@@ -1511,8 +1696,8 @@
             like(8, features, kind=SINGLE),
         ],
         [q, dq2, n1, pq, mq, log_q, cross_out_weight, norm_gain, attn_in, attn_out]
-        + dq1_parts.result,
-        [VMEM] * 8 + [ANY, ANY] + [VMEM] * blocks,
+        + [dq1_parts.tensor] + dq1_parts.result,
+        [VMEM] * 8 + [ANY, ANY] + [VMEM] * (2 * blocks - 1),
         [((features, wide), NARROW), ((features, features), NARROW), ((padded, features), NARROW),
          ((count, features), SINGLE), ((count, features), NARROW), ((count, features), NARROW),
          ((16, count), SINGLE), ((count, 2 * PAIR), SINGLE), ((count, wide), NARROW)],
@@ -1531,11 +1716,12 @@
         causal_weight = RepSum(causal_weight, 1)
         arrive(
             (share_weight, "x"), (causal_weight, "out"), (norms, "out"), (kv_weight, "y"),
-            (window_weight, "z"),
+            (window_weight, "z"), (up_x, "back_x"), (down_x, "back_x"), (reverse_weight, "back_x"),
         )
         arrive(
             (share_weight, "z"), (kv_weight, "z"), (causal_weight, "back"), (norms, "back"),
-            (up_x, "back"), (down_x, "back"), (reverse_weight, "back"), (window_weight, "back"),
+            (up_x, "back_core"), (down_x, "back_core"), (reverse_weight, "back_core"),
+            (window_weight, "back"),
         )
         arrive((share_weight, "back"), (kv_weight, "back"))
         up_x, down_x, reverse_weight, window_weight, kv_weight, share_weight, causal_weight = (

time: 524 us -> 479 us (0.914)
  other arithmetic: 68.1 us -> 13.7 us
  Pallas kernels: 429 us -> 441 us
    convert_element_type x26 -> x0, other arithmetic: 53.2 us -> none  [absorb(): self.tensor = total.astype(NARROW)]
    pallas_call x16, Pallas kernels: 429 us -> 441 us  [call(): pl.pallas_call(body_kernel, out_shape=list(outs) + [like(*m.shape, kind=m...]
where the time goes in v5:
time: 479 us; the launch traced here: 470 us
  Pallas kernels  441 us (92%)
  other arithmetic  13.7 us (3%)
  local copies, waits for them, and re-layouts  13 us (3%)
    pallas_call x16, Pallas kernels, call(): pl.pallas_call(body_kernel, out_shape=list(outs) + [like(*m.shape, kind=m...  441 us

profile of v5, /device:TPU:0, one launch (start us, length us, event | category | flops | bytes accessed | tf_op | source)
XLA Modules:
  0.0 470.1 jit_solution(13981274337266104861)
XLA Ops:
  0.6 30.2 %shard_map.196 = (bf16[800,768]{1,0:T(8,128)(2,1)}, bf16[800,2304]{1,0:T(8,128)(2,1)}, bf16[800,768]{1,0:T(8,128)(2,1)}, f32[896,768]{1,0:T(8,128)}, bf16[896,76...) custom-call(bf16[800,768]{1,0:T(8,128)(2,1)} %bitcast.55, ...), custom_call_target="tpu_custom_call" | custom-call | flops 14155776000 | bytes 20140032 | tf_op jit(solution)/shard_map/pallas_call | solution.py:1375
  30.8 0.0 copy-start.31
  30.8 15.2 %shard_map.195 = (bf16[512,768]{1,0:T(8,128)(2,1)}, bf16[512,2304]{1,0:T(8,128)(2,1)}, bf16[512,768]{1,0:T(8,128)(2,1)}, f32[512,768]{1,0:T(8,128)}, bf16[512,76...) custom-call(bf16[512,768]{1,0:T(8,128)(2,1)} %bitcast.58, f32[6,768]{1,0:T(8,128)} %refs_7_.3, ...), custom_call_target="tpu_custom_call" | custom-call | flops 5435817984 | bytes 19697664 | tf_op jit(solution)/shard_map/pallas_call | solution.py:1375
  46.0 0.1 broadcast_in_dim.27
  46.1 0.7 select_n.425.valid_ref
  46.8 12.6 %shard_map.197 = (bf16[896,768]{1,0:T(8,128)(2,1)}, f32[16,112]{1,0:T(8,128)}, f32[16,112]{1,0:T(8,128)}, f32[16,112]{1,0:T(8,128)}, f32[16,112]{1,0:T(8,128)}, ...) custom-call(bf16[800,768]{1,0:T(8,128)(2,1)} %get-tuple-element.277.cq_ref.refs_2_, ...), custom_call_target="tpu_custom_call" | custom-call | flops 5662310400 | bytes 2803712 | tf_op jit(solution)/shard_map/pallas_call | solution.py:1375
  60.0 24.7 %shard_map.198 = (bf16[512,768]{1,0:T(8,128)(2,1)}, f32[512,768]{1,0:T(8,128)}, f32[16,512]{1,0:T(8,128)}, f32[16,112]{1,0:T(8,128)}, f32[16,112]{1,0:T(8,128)},...) custom-call(s32[1]{0:T(128)S(6)} %copy.27.refs_0_, ...), custom_call_target="tpu_custom_call" | custom-call | flops 4831838208 | bytes 9535492 | tf_op jit(solution)/shard_map/pallas_call | solution.py:1375
  84.7 31.1 %shard_map.199 = (bf16[512,768]{1,0:T(8,128)(2,1)}, f32[512,768]{1,0:T(8,128)}, bf16[768,3072]{1,0:T(8,128)(2,1)}, bf16[3072,768]{1,0:T(8,128)(2,1)}, f32[8,768]...) custom-call(f32[512,768]{1,0:T(8,128)} %get-tuple-element.287.refs_0, ...), custom_call_target="tpu_custom_call" | custom-call | flops 14495514624 | bytes 21270528 | tf_op jit(solution)/shard_map/pallas_call | solution.py:1375
  115.8 4.8 %shard_map.200 = (bf16[112,768]{1,0:T(8,128)(2,1)}, f32[16,112]{1,0:T(8,128)}) custom-call(bf16[896,768]{1,0:T(8,128)(2,1)} %get-tuple-element.286.refs_12_.refs_6_.own_ref, f32[16,112]{1,0:T(8,128)} %get-tuple-element.290.refs_0_, f32[16,112]{1,0:T(8,128)} %get-tuple-element.291.refs_1_, f32[16,112]{1,0:T(8,128)} %get-tuple-element.292.refs_2_, ...), custom_call_target="tpu_custom_call" | custom-call | flops 1056964608 | bytes 2637824 | tf_op jit(solution)/shard_map/pallas_call | solution.py:1375
  120.6 32.8 %shard_map.201 = (bf16[512,768]{1,0:T(8,128)(2,1)}, bf16[4,2,2,48,1536]{4,3,2,1,0:T(8,128)(2,1)}, bf16[112,768]{1,0:T(8,128)(2,1)}, bf16[112,768]{1,0:T(8,128)(2...) custom-call(s32[1]{0:T(128)S(6)} %copy.27.refs_0_, ...), custom_call_target="tpu_custom_call" | custom-call | flops 9663676416 | bytes 11141124 | tf_op jit(solution)/shard_map/pallas_call | solution.py:1375
  153.4 49.6 %shard_map.202 = (bf16[800,768]{1,0:T(8,128)(2,1)}, f32[800,768]{1,0:T(8,128)}, bf16[96,3072]{1,0:T(8,128)(2,1)}, bf16[384,768]{1,0:T(8,128)(2,1)}, f32[8,768]{1...) custom-call(f32[896,768]{1,0:T(8,128)} %get-tuple-element.289.refs_0, ...), custom_call_target="tpu_custom_call" | custom-call | flops 16986931200 | bytes 28987392 | tf_op jit(solution)/shard_map/pallas_call | solution.py:1375
  203.0 0.9 select_n.515.refs_4_
  203.9 36.6 %shard_map.203 = (bf16[512,1536]{1,0:T(8,128)(2,1)}, bf16[96,768]{1,0:T(8,128)(2,1)}, bf16[112,768]{1,0:T(8,128)(2,1)}, bf16[112,768]{1,0:T(8,128)(2,1)}, bf16[1...) custom-call(f32[800,768]{1,0:T(8,128)} %get-tuple-element.349.refs_0, ...), custom_call_target="tpu_custom_call" | custom-call | flops 11324620800 | bytes 11413504 | tf_op jit(solution)/shard_map/pallas_call | solution.py:1375
  240.5 46.7 %shard_map.204 = (bf16[4,2,2,48,1536]{4,3,2,1,0:T(8,128)(2,1)}, bf16[4,2,2,48,3072]{4,3,2,1,0:T(8,128)(2,1)}, f32[512,768]{1,0:T(8,128)}, f32[8,768]{1,0:T(8,128...) custom-call(bf16[512,768]{1,0:T(8,128)(2,1)} %bitcast.59, ...), custom_call_target="tpu_custom_call" | custom-call | flops 14495514624 | bytes 29902848 | tf_op jit(solution)/shard_map/pallas_call | solution.py:1375
  287.3 11.6 %shard_map.205 = (bf16[112,768]{1,0:T(8,128)(2,1)}, bf16[4,2,2,48,2304]{4,3,2,1,0:T(8,128)(2,1)}, f32[8,768]{1,0:T(8,128)}, bf16[4,2,48,2304]{3,2,1,0:T(8,128)(2,1)}) custom-call(f32[896,768]{1,0:T(8,128)} %get-tuple-element.289.refs_0_, bf16[896,768]{1,0:T(8,128)(2,1)} %get-tuple-element.388.refs_1_, f32[6,768]{1,0:T(8,128)} %refs_7_.3, ...), custom_call_target="tpu_custom_call" | custom-call | flops 792723456 | bytes 22431744 | tf_op jit(solution)/shard_map/pallas_call | solution.py:1375
  298.9 29.9 %shard_map.206 = (bf16[112,384]{1,0:T(8,128)(2,1)}, bf16[112,384]{1,0:T(8,128)(2,1)}, bf16[112,384]{1,0:T(8,128)(2,1)}, bf16[112,384]{1,0:T(8,128)(2,1)}, bf16[1...) custom-call(bf16[112,768]{1,0:T(8,128)(2,1)} %get-tuple-element.413., ...), custom_call_target="tpu_custom_call" | custom-call | tf_op jit(solution)/shard_map/pallas_call | solution.py:1375
  328.8 44.3 %shard_map.207 = (bf16[96,4096]{1,0:T(8,128)(2,1)}, f32[800,768]{1,0:T(8,128)}, f32[8,768]{1,0:T(8,128)}, bf16[48,1536]{1,0:T(8,128)(2,1)}, bf16[48,1536]{1,0:T(...) custom-call(bf16[800,768]{1,0:T(8,128)(2,1)} %bitcast.56, ...), custom_call_target="tpu_custom_call" | custom-call | flops 15099494400 | bytes 30298112 | tf_op jit(solution)/shard_map/pallas_call | solution.py:1375
  373.1 0.8 slice_multiply_fusion
  374.0 0.0 copy-done.30
  374.0 0.8 fusion.17
  374.8 0.8 fusion.19
  375.6 0.1 stack.55
  375.7 0.6 pad.4.refs_3_
  376.3 31.8 %shard_map.208 = (bf16[4,48,1152]{2,1,0:T(8,128)(2,1)}, bf16[96,1024]{1,0:T(8,128)(2,1)}, bf16[96,1024]{1,0:T(8,128)(2,1)}, bf16[96,1024]{1,0:T(8,128)(2,1)}, f3...) custom-call(bf16[4,48,2304]{2,1,0:T(8,128)(2,1)} %get-tuple-element., ...), custom_call_target="tpu_custom_call" | custom-call | tf_op jit(solution)/shard_map/pallas_call | solution.py:1375
  408.2 1.5 add_add_fusion.refs_8_
  409.7 28.5 %shard_map.209 = (bf16[48,1152]{1,0:T(8,128)(2,1)}, bf16[48,1152]{1,0:T(8,128)(2,1)}, bf16[48,1152]{1,0:T(8,128)(2,1)}, bf16[48,768]{1,0:T(8,128)(2,1)}, bf16[48...) custom-call(bf16[4,48,1152]{2,1,0:T(8,128)(2,1)} %get-tuple-element., ...), custom_call_target="tpu_custom_call" | custom-call | tf_op jit(solution)/shard_map/pallas_call | solution.py:1375
  438.3 1.2 broadcast_select_fusion.22
  439.5 0.1 maximum_bitcast_fusion.2
  439.6 0.0 copy-done.13
  439.6 0.0 copy-done.14
  439.6 0.0 copy-done.15
  439.6 0.0 copy-done.16
  439.6 0.0 copy-done.17
  439.7 0.0 copy-done.18
  439.7 0.0 copy-done.19
  439.7 0.1 broadcast_select_fusion.10
  439.9 1.6 maximum_convert_fusion.2
  441.5 0.1 broadcast_select_fusion.42
  441.7 1.6 maximum_convert_fusion.1
  443.3 0.1 broadcast_select_fusion.46
  443.4 0.8 copy-done.9
  444.2 0.1 copy-done.10
  444.3 0.1 copy-done.11
  444.3 0.1 copy-done.12
  444.5 0.1 broadcast_select_fusion.5
  444.6 0.7 copy-done.7
  445.3 0.0 copy-done.8
  445.4 0.0 copy-done.27
  445.4 0.0 copy-done.28
  445.5 1.1 maximum_convert_fusion.3
  446.8 10.5 %shard_map.210 = (bf16[48,1152]{1,0:T(8,128)(2,1)}, bf16[48,1152]{1,0:T(8,128)(2,1)}, bf16[48,1152]{1,0:T(8,128)(2,1)}, bf16[48,768]{1,0:T(8,128)(2,1)}, bf16[48...) custom-call(bf16[48,1152]{1,0:T(8,128)(2,1)} %get-tuple-element.508.refs_0_, ...), custom_call_target="tpu_custom_call" | custom-call | tf_op jit(solution)/shard_map/pallas_call | solution.py:1375
  457.3 1.0 broadcast_select_fusion.70
  458.4 1.1 broadcast_select_fusion.52
  459.5 0.1 fusion.12
  459.6 0.0 copy-start.6
  459.6 2.1 maximum_convert_fusion
  461.7 1.0 dynamic-slice_add_fusion
  462.7 0.6 fusion.20
  463.3 1.3 constant_dynamic-slice_fusion
  464.6 0.9 copy.24
  465.5 1.2 constant_dynamic-slice_fusion.1
  466.8 0.8 copy.22
  467.6 0.9 copy.28
  468.5 1.1 copy.29
  (60 shorter events, 0.5 us)
Async XLA Ops:
  30.8 15.2 %copy-start.31 = (s32[1,8]{1,0:T(1,128)S(1)}, s32[1,8]{1,0:T(1,128)}, u32[]{:S(2)}) copy-start(s32[1,8]{1,0:T(1,128)} %param.14) | copy-start | bytes 100
  328.8 45.2 %copy-start.30 = (f32[8,768]{1,0:T(8,128)S(1)}, f32[8,768]{1,0:T(8,128)}, u32[]{:S(2)}) copy-start(f32[8,768]{1,0:T(8,128)} %get-tuple-element.449) | copy-start | bytes 73732
  409.7 28.6 %copy-start.4 = (bf16[192,384]{1,0:T(8,128)(2,1)S(1)}, bf16[192,384]{1,0:T(8,128)(2,1)}, u32[]{:S(2)}) copy-start(bf16[192,384]{1,0:T(8,128)(2,1)} %get-tuple-element.486.refs_12_) | copy-start | bytes 442372
  409.7 28.6 %copy-start.5 = (bf16[192,384]{1,0:T(8,128)(2,1)S(1)}, bf16[192,384]{1,0:T(8,128)(2,1)}, u32[]{:S(2)}) copy-start(bf16[192,384]{1,0:T(8,128)(2,1)} %get-tuple-element.485.refs_11_) | copy-start | bytes 442372
  438.2 1.4 copy-start.13
  438.2 1.4 copy-start.14
  438.2 1.4 copy-start.15
  438.2 1.4 copy-start.16
  438.2 1.4 copy-start.17
  438.2 1.4 copy-start.18
  438.2 1.4 copy-start.19
  438.2 1.4 copy-start.20
  439.8 1.6 copy-start.2
  439.9 1.6 copy-start.3
  439.9 1.6 copy-start.25
  439.9 1.6 copy-start.26
  441.6 1.6 copy-start.21
  441.6 1.6 copy-start.22
  441.7 1.6 copy-start.23
  441.7 1.6 copy-start.24
  443.2 0.9 copy-start.9
  443.2 1.0 copy-start.10
  443.2 1.1 copy-start.11
  443.2 1.2 copy-start.12
  444.5 0.9 copy-start.7
  444.5 0.9 copy-start.8
  444.5 1.0 copy-start.27
  444.5 1.0 copy-start.28
  459.6 2.1 copy-start.6
  459.6 2.1 copy-start.29
  461.7 5.9 %copy-start.1 = (bf16[512,768]{1,0:T(8,128)(2,1)S(1)}, bf16[512,768]{1,0:T(8,128)(2,1)}, u32[]{:S(2)}) copy-start(bf16[512,768]{1,0:T(8,128)(2,1)} %get-tuple-element.288) | copy-start | bytes 2359300
  465.5 2.9 copy-start
